TPU v7x, 32 devices: a whole 2x2x4 slice. The times are simulated.
32 devices in a mesh: modes: 16 (over z, x, core), rad: 2 (over y).
Axes of the slice: x: 2, y: 2, z: 4, core: 2. Of those that a mesh axis runs over, the one named last changes fastest.
Arguments:
- forcing: bfloat16 [3, 1024, 256, 256], P(None, 'modes', 'rad'), may hold values from -6 to 6
- diffusion: float32 [3], replicated, may hold values from 0.05 to 1
- axial_forward: float32 [256, 256], replicated, may hold values from -0.375 to 0.375
- axial_inverse_map: float32 [256, 256], replicated, may hold values from -0.375 to 0.375
- axial_eigenvalues: float32 [256], replicated, may hold values from 0.05 to 10
- radial_forward: float32 [128, 256, 256], P(('modes', 'rad')), may hold values from -0.375 to 0.375
- radial_backward: float32 [128, 256, 256], P(('modes', 'rad')), may hold values from -0.375 to 0.375
- radial_eigenvalues: float32 [128, 256], P(('modes', 'rad')), may hold values from 0.05 to 10
Outputs:
- solution: float32 [3, 128, 2, 256, 256], P(None, 'modes', None, 'rad')
All inputs are finite; a program needn't handle non-finite values.
Results may differ from a plain program's by a relative error of at most 0.0003.
Values may be sent and summed in bfloat16 or wider, within the bound.
No kernel may reach another device: no remote copies, remote signals or barrier semaphores. Data moves between devices by JAX's collectives and lax.ppermute only.
A program may use at most 128 MiB of HBM per device.

v0:
```python
import math

import jax
import jax.numpy as jnp
from jax import lax
from jax.sharding import PartitionSpec as P


def azimuthal_tables(retained, points):
    row_index = jnp.arange(2 * retained, dtype=jnp.int32)
    wavenumber = row_index // 2
    quarter = (row_index % 2).astype(jnp.float32) * (0.5 * math.pi)
    theta_index = jnp.arange(points, dtype=jnp.int32)
    phase_index = wavenumber[:, None] * theta_index[None, :] % points
    radians = phase_index.astype(jnp.float32) * (2.0 * math.pi / points) + quarter[:, None]
    table = jnp.cos(radians) * (1.0 / math.sqrt(points))
    upper = table.astype(jnp.bfloat16)
    widened = lax.optimization_barrier(upper).astype(jnp.float32)
    lower = (table - widened).astype(jnp.bfloat16)
    return (upper, lower)


def modal_solve(spectral_coefficients, forward_map, backward, eigenvalues, axial_part, diffusion):
    highest_mode = lax.Precision.HIGHEST
    radial_coefficients = jnp.einsum(
        "hzv,bhtvp->bhtzp", forward_map, spectral_coefficients, precision=highest_mode
    )
    denominator = 1.0 + diffusion[:, None, None, None, None] * (
        eigenvalues[None, :, None, :, None] + axial_part[None, None, None, None, :]
    )
    return jnp.einsum(
        "mri,fmciq->fmcrq", backward, radial_coefficients / denominator, precision=highest_mode
    )


def per_device(
    forcing,
    diffusion,
    axial_forward,
    axial_inverse_map,
    axial_eigenvalues,
    radial_forward,
    radial_backward,
    radial_eigenvalues,
):
    highest_mode = lax.Precision.HIGHEST
    fields, slab_points, radial_block, axial_points = forcing.shape
    mode_processors = lax.axis_size("modes")
    radial_devices = lax.axis_size("rad")
    total_theta = slab_points * mode_processors
    retained = radial_forward.shape[0] * mode_processors * radial_devices
    table_upper, table_lower = azimuthal_tables(retained, total_theta)
    flat_values = forcing.reshape(fields, slab_points, radial_block * axial_points)
    columns = lax.all_to_all(flat_values, "modes", split_axis=2, concat_axis=1, tiled=True)
    first = jnp.einsum("kt,ftc->fkc", table_upper, columns, preferred_element_type=jnp.float32)
    second = jnp.einsum("kt,ftc->fkc", table_lower, columns, preferred_element_type=jnp.float32)
    spectral = lax.all_to_all(first + second, "modes", split_axis=1, concat_axis=2, tiled=True)
    local_modes = spectral.shape[1] // 2
    spectral = spectral.reshape(fields, local_modes, 2, radial_block, axial_points)
    axial_coef = jnp.einsum("fmcrz,qz->fmcrq", spectral, axial_forward, precision=highest_mode)
    exchanged = lax.all_to_all(axial_coef, "rad", split_axis=4, concat_axis=3, tiled=True)
    forward_rows, backward_rows, eigen_rows = (
        lax.all_gather(radial_forward, "rad", axis=0, tiled=True),
        lax.all_gather(radial_backward, "rad", axis=0, tiled=True),
        lax.all_gather(radial_eigenvalues, "rad", axis=0, tiled=True),
    )
    axial_block = axial_points // radial_devices
    axial_part = lax.dynamic_slice_in_dim(
        axial_eigenvalues, lax.axis_index("rad") * axial_block, axial_block
    )
    solved = modal_solve(exchanged, forward_rows, backward_rows, eigen_rows, axial_part, diffusion)
    returned = lax.all_to_all(solved, "rad", split_axis=3, concat_axis=4, tiled=True)
    return jnp.einsum("fmcrq,zq->fmcrz", returned, axial_inverse_map, precision=highest_mode)


def solution(mesh):
    in_specs = (
        P(None, "modes", "rad", None),
        P(),
        P(),
        P(),
        P(),
        P(("modes", "rad"), None, None),
        P(("modes", "rad"), None, None),
        P(("modes", "rad"), None),
    )
    out_specs = P(None, "modes", None, "rad", None)
    return jax.shard_map(
        per_device, mesh=mesh, in_specs=in_specs, out_specs=out_specs, check_vma=False
    )
```

profile of v0, /device:TPU:17, one launch (start us, length us, event | category | flops | bytes accessed | tf_op | source)
XLA Modules:
  0.0 925.3 jit_solution(11767855053437400910)
XLA Ops:
  6.5 0.0 copy-start
  6.5 35.3 %copy.24 = bf16[3,64,128,256]{1,0,3,2:T(4,128)(2,1)} copy(bf16[3,64,128,256]{3,2,1,0:T(8,128)(2,1)} %param.8) | data formatting | bytes 25165824 | tf_op args[0]
  41.9 28.7 %reshape.58 = bf16[16,2,196608]{2,1,0:T(2,128)(2,1)} reshape(bf16[32768,3,64]{2,1,0:T(4,128)(2,1)} %bitcast.65) | data formatting | bytes 25165824
  70.5 6.5 all-to-all-start
  77.0 4.3 fusion.20
  81.4 267.6 %all-to-all-done = bf16[16,2,196608]{2,1,0:T(2,128)(2,1)} async-done(((bf16[16,2,196608]{2,1,0:T(2,128)(2,1)}), bf16[16,2,196608]{2,1,0:T(2,128)(2,1)}, u32[]{:S(2)}, u32[]{:S(2)}) %all-to-all-start) | async-done | bytes 12582944 | tf_op jit(solution)/shard_map/all_to_all | solution.py:54
  349.0 26.4 %reshape.59 = bf16[32768,3,64]{2,1,0:T(4,128)(2,1)} reshape(bf16[16,2,196608]{2,1,0:T(2,128)(2,1)} %all-to-all-done) | data formatting | bytes 25165824
  375.3 45.6 %copy.41 = bf16[3,64,16,2048]{3,1,2,0:T(8,128)(2,1)} copy(bf16[3,64,16,2048]{1,0,3,2:T(4,128)(2,1)} %bitcast.64) | data formatting | bytes 25165824 | tf_op jit(solution)/shard_map/all_to_all | solution.py:54
  420.9 0.0 copy-start.1
  420.9 12.0 %fusion.17 = f32[256,3,2048]{2,0,1:T(8,128)S(1)} fusion(bf16[3,1024,2048]{2,1,0:T(8,128)(2,1)} %bitcast.66, f32[256]{0:T(256)S(1)} %fusion.29, s32[256]{0:T(256)S(1)} %and_select_fusion.1), kind=kOutput, calls=%fused_computation.25 | convolution fusion | flops 3225681920 | bytes 18876416 | tf_op jit(solution)/shard_map/kt,ftc->fkc/dot_general | solution.py:55
  432.9 0.0 copy-done.1
  432.9 7.8 add_bitcast_fusion
  440.8 7.6 copy.27
  448.4 5.2 all-to-all-start.1
  453.6 0.0 all-gather.4.cloned.1.call-start
  453.6 0.7 all-gather.4.cloned.1.call-update
  454.3 181.3 %all-to-all-done.1 = f32[3,256,2048]{2,0,1:T(4,128)} async-done(((f32[3,256,2048]{2,0,1:T(4,128)}), f32[3,256,2048]{2,0,1:T(4,128)}, u32[]{:S(2)}, u32[]{:S(2)}) %all-to-all-start.1) | async-done | bytes 6291488 | tf_op jit(solution)/shard_map/all_to_all | solution.py:57
  635.7 9.7 %copy.47 = f32[3,16,16,2048]{3,1,2,0:T(8,128)} copy(f32[3,16,16,2048]{3,0,2,1:T(4,128)} %bitcast.9) | data formatting | bytes 12582912 | tf_op jit(solution)/shard_map/all_to_all | solution.py:57
  645.4 7.1 reshape.49
  652.5 0.0 copy-done
  652.5 8.9 fusion.23
  661.4 10.3 %copy.29 = f32[3,8,2,128,256]{3,2,1,0,4:T(2,128)} copy(f32[3,8,2,128,256]{4,3,2,1,0:T(8,128)} %fusion.23) | data formatting | bytes 12582912 | tf_op jit(solution)/shard_map/fmcrz,qz->fmcrq/dot_general | solution.py:60
  671.7 0.0 copy-start.3
  671.7 0.0 copy-start.5
  671.7 0.0 copy-start.4
  671.7 6.5 all-to-all-start.2
  678.2 0.0 all-gather.6.cloned.1.call-start
  678.2 0.7 all-gather.6.cloned.1.call-update
  679.0 0.0 copy-done.3
  679.0 90.8 %all-gather = f32[2,4,256]{2,1,0:T(4,128)S(1)} all-gather(f32[1,4,256]{2,1,0:T(4,128)S(1)} %bitcast.73), channel_id=1, replica_groups=mesh['modes'=16,'rad'=2] {'rad'}, dimensions={0}, use_global_device_ids=true | all-gather | bytes 12288 | tf_op jit(solution)/shard_map/all_gather | solution.py:65
  769.8 0.0 copy-done.5
  769.8 0.1 dynamic_slice.3
  769.8 0.1 broadcast_add_fusion
  770.0 0.0 copy-done.4
  770.0 0.4 multiply_add_fusion
  770.4 0.0 all-to-all-done.2
  770.4 7.4 copy.30
  777.8 6.8 copy.43
  784.6 0.0 all-gather.4.cloned.1.call-done
  784.6 14.5 %fusion.4 = f32[8,3,2,128,256]{4,3,2,1,0:T(8,128)} fusion(f32[3,8,2,256,128]{4,3,2,0,1:T(8,128)} %bitcast.68, f32[8,256,256]{2,1,0:T(8,128)} %all-gather.4.cloned.1.call-done), kind=kOutput, calls=%fused_computation.9 | convolution fusion | flops 4831838208 | bytes 14680064 | tf_op jit(solution)/shard_map/hzv,bhtvp->bhtzp/dot_general | solution.py:25
  799.1 0.0 all-gather.6.cloned.1.call-done
  799.1 10.8 %fusion.2 = f32[3,8,2,256,128]{3,4,2,0,1:T(8,128)} fusion(f32[8,3,2,128,256]{4,3,2,1,0:T(8,128)} %fusion.4, f32[3,8,256,128]{2,3,0,1:T(8,128)S(1)} %multiply_add_fusion, f32[8,256,256]{2,1,0:T(8,128)} %all-gather.6.cloned.1.call-done), kind=kOutput, calls=%fused_computation.7 | convolution fusion | flops 4833411072 | bytes 17825792 | tf_op jit(solution)/shard_map/mri,fmciq->fmcrq/dot_general | solution.py:31
  809.9 10.3 %copy.33 = f32[3,8,2,256,128]{4,2,0,1,3:T(2,128)} copy(f32[3,8,2,256,128]{3,4,2,0,1:T(8,128)} %fusion.2) | data formatting | bytes 12582912 | tf_op jit(solution)/shard_map/mri,fmciq->fmcrq/transpose | solution.py:31
  820.2 72.6 %all_to_all.69 = f32[3,8,2,256,128]{4,2,0,1,3:T(2,128)S(1)} all-to-all(f32[3,8,2,256,128]{4,2,0,1,3:T(2,128)} %copy.33), channel_id=1, replica_groups=mesh['modes'=16,'rad'=2] {'rad'}, dimensions={3} | all-to-all | bytes 12582912 | tf_op jit(solution)/shard_map/all_to_all | solution.py:72
  892.8 7.6 copy.46
  900.4 9.0 all_to_all.64
  909.4 0.0 copy-done.2
  909.4 8.9 fusion.21
  (4 shorter events, 0.0 us)
Async XLA Ops:
  6.5 646.0 %copy-start = (f32[256,256]{1,0:T(8,128)S(1)}, f32[256,256]{1,0:T(8,128)}, u32[]{:S(2)}) copy-start(f32[256,256]{1,0:T(8,128)} %param.10) | copy-start | bytes 786436
  70.5 278.4 %all-to-all-start = ((bf16[16,2,196608]{2,1,0:T(2,128)(2,1)}), bf16[16,2,196608]{2,1,0:T(2,128)(2,1)}, u32[]{:S(2)}, u32[]{:S(2)}) async-start(bf16[16,2,196608]{2,1,0:T(2,128)(2,1)} %reshape.58), calls=%async_computation | async-start | bytes 25165824 | tf_op jit(solution)/shard_map/all_to_all | solution.py:54
  420.9 12.0 %copy-start.1 = (bf16[3,64,16,2048]{3,1,2,0:T(8,128)(2,1)S(1)}, bf16[3,64,16,2048]{3,1,2,0:T(8,128)(2,1)}, u32[]{:S(2)}) copy-start(bf16[3,64,16,2048]{3,1,2,0:T(8,128)(2,1)} %copy.41) | copy-start | bytes 37748740
  448.4 187.3 %all-to-all-start.1 = ((f32[3,256,2048]{2,0,1:T(4,128)}), f32[3,256,2048]{2,0,1:T(4,128)}, u32[]{:S(2)}, u32[]{:S(2)}) async-start(f32[3,256,2048]{2,0,1:T(4,128)} %copy.27), calls=%async_computation.1 | async-start | bytes 16777216 | tf_op jit(solution)/shard_map/all_to_all | solution.py:57
  453.6 331.0 %all-gather.4.cloned.1.call-start = ((), (), s32[]{:S(2)}) async-start(), calls=%async_computation.4 | async-start | bytes 3145728 | tf_op jit(solution)/shard_map/all_gather | solution.py:63
  671.7 7.2 copy-start.3
  671.7 98.1 %copy-start.5 = (f32[256]{0:T(256)S(1)}, f32[256]{0:T(256)}, u32[]{:S(2)}) copy-start(f32[256]{0:T(256)} %param.12) | copy-start | bytes 3076
  671.7 98.3 %copy-start.4 = (f32[3]{0:T(128)S(1)}, f32[3]{0:T(128)}, u32[]{:S(2)}) copy-start(f32[3]{0:T(128)} %param.9) | copy-start | bytes 40
  671.7 98.7 %all-to-all-start.2 = ((f32[3,8,2,128,256]{3,2,1,0,4:T(2,128)}), f32[3,8,2,128,256]{3,2,1,0,4:T(2,128)}, u32[]{:S(2)}, u32[]{:S(2)}) async-start(f32[3,8,2,128,256]{3,2,1,0,4:T(2,128)} %copy.29), calls=%async_computation.2 | async-start | bytes 12582912 | tf_op jit(solution)/shard_map/all_to_all | solution.py:61
  678.2 120.9 %all-gather.6.cloned.1.call-start = ((), (), s32[]{:S(2)}) async-start(), calls=%async_computation.5 | async-start | bytes 3145728 | tf_op jit(solution)/shard_map/all_gather | solution.py:64
  900.4 9.0 copy-start.2
Sparse Core Ops, SparseCore 0:
  456.0 33.7 all-gather.3
  680.6 56.1 all-gather.5
where the time goes:
time: 937 us; the launch traced here: 925 us
  waiting for transfers between devices  450 us (48%)
  local copies, waits for them, and re-layouts  212 us (23%)
  blocking collectives  163 us (17%)
  matrix products  62.8 us (7%)
  starting transfers between devices  18.2 us (2%)
  between operations  13.8 us (1%)
    all_to_all x1, waiting for transfers between devices, per_device(): lax.all_to_all(flat_values, 'modes', split_axis=2, concat_axis=1, tiled=T...  268 us
    all_to_all x1, waiting for transfers between devices, per_device(): lax.all_to_all(first + second, 'modes', split_axis=1, concat_axis=2, tile...  181 us
    all_gather x1, blocking collectives, per_device(): lax.all_gather(radial_eigenvalues, 'rad', axis=0, tiled=True)  90.8 us
    unnamed x16, local copies, waits for them, and re-layouts  90.4 us
    all_to_all x1, blocking collectives, per_device(): lax.all_to_all(solved, 'rad', split_axis=3, concat_axis=4, tiled=True)  72.6 us
    all_to_all x1, local copies, waits for them, and re-layouts, per_device(): lax.all_to_all(flat_values, 'modes', split_axis=2, concat_axis=1, tiled=T...  45.6 us
  transfers between devices with their start and end apart: 5, of which 2 were waited for; matrix products, arithmetic and copies ran while one was open for 8% of the time, Pallas kernels for 0%

commit v1 on v0

--- a/solution.py
+++ b/solution.py
@@ -1,9 +1,362 @@
+import functools
 import math
 
 import jax
 import jax.numpy as jnp
+import numpy as np
 from jax import lax
+from jax.experimental import pallas as pl
+from jax.experimental.pallas import tpu as pltpu
 from jax.sharding import PartitionSpec as P
+
+BF16 = jnp.bfloat16
+F32 = jnp.float32
+VMEM_BYTES = 48 * 1024 * 1024
+
+CODE_SPAN = 126.0
+CODE_MID = 0.5
+LN2 = math.log(2.0)
+DECODE_SLOPE = 1.0 / (LN2 * CODE_SPAN)
+DECODE_SHIFT = CODE_MID / CODE_SPAN
+TINY = 1e-35
+LOG_BASE = 125.0
+LOG_RANGE = 250.0
+UNIT_PART = 2.0**-6
+
+
+def code_scale(largest):
+    return (largest * 1.008).astype(BF16).astype(F32)
+
+
+def linear_encode(values, scale):
+    inverse = jnp.where(scale > TINY, CODE_SPAN / jnp.maximum(scale, TINY), 0.0)
+    return jnp.exp2(values * inverse + CODE_MID)
+
+
+def linear_decode(coded, scale):
+    return scale * (jnp.log(coded) * DECODE_SLOPE - DECODE_SHIFT)
+
+
+def log_gain(bound):
+    return LOG_RANGE / math.log2(1.0 + bound / UNIT_PART)
+
+
+def log_encode(values, unit, gain):
+    inverse = jnp.where(unit > TINY, 1.0 / jnp.maximum(unit, TINY), 0.0)
+    magnitude = jnp.exp2(jnp.log(1.0 + jnp.abs(values) * inverse) * (gain / LN2) - LOG_BASE)
+    return jnp.where(values < 0.0, -magnitude, magnitude)
+
+
+def log_decode(coded, unit, gain):
+    magnitude = jnp.exp2(jnp.log(jnp.abs(coded)) * (1.0 / (LN2 * gain)) + LOG_BASE / gain)
+    magnitude = unit * (magnitude - 1.0)
+    return jnp.where(coded < 0.0, -magnitude, magnitude)
+
+
+def window_basis(window, total, retained, rank):
+    points = np.arange(window)
+    inner = np.arange(1, window)
+    diagonal = np.cos(np.pi * (2 * points - window + 1) / total) * np.cos(
+        np.pi * (2 * retained - 1) / total
+    )
+    beside = -np.sin(np.pi * inner / total) * np.sin(np.pi * (window - inner) / total)
+    _, vectors = np.linalg.eigh(np.diag(diagonal) + np.diag(beside, 1) + np.diag(beside, -1))
+    basis = vectors[:, :rank]
+    signs = np.where(np.sum(basis * (points + 0.37)[:, None] ** 2, axis=0) < 0, -1.0, 1.0)
+    return basis * signs
+
+
+def mode_rows(total, retained):
+    phase = np.arange(retained)[:, None] * np.arange(total)[None, :] % total
+    radians = phase * (2.0 * np.pi / total)
+    rows = np.stack([np.cos(radians), -np.sin(radians)], axis=1) / np.sqrt(total)
+    return rows.reshape(2 * retained, total)
+
+
+def halves(table):
+    upper = table.astype(np.float32).astype(jnp.bfloat16)
+    lower = (table - upper.astype(np.float64)).astype(np.float32).astype(jnp.bfloat16)
+    return upper, lower
+
+
+def split(values):
+    upper = values.astype(BF16)
+    return upper, (values - upper.astype(F32)).astype(BF16)
+
+
+def dot3(left, right, contract=((1,), (0,))):
+    dims = (contract, ((), ()))
+    dot = functools.partial(lax.dot_general, dimension_numbers=dims, preferred_element_type=F32)
+    return dot(left[0], right[0]) + (dot(left[0], right[1]) + dot(left[1], right[0]))
+
+
+ROWS_BY_ROWS = ((1,), (1,))
+
+
+def encode_body(upper_ref, lower_ref, forcing_ref, out_ref, *, group, kept):
+    points, rows, width = forcing_ref.shape[1:]
+    block = forcing_ref[0].astype(F32)
+    for part in range(rows // group):
+        piece = block[:, part * group : (part + 1) * group, :].reshape(points * group, width)
+        piece = piece.astype(BF16)
+        coefficients = jnp.dot(upper_ref[...], piece, preferred_element_type=F32)
+        coefficients += jnp.dot(lower_ref[...], piece, preferred_element_type=F32)
+        coefficients = coefficients.reshape(group, kept, width)
+        scale = code_scale(jnp.max(jnp.abs(coefficients), axis=1, keepdims=True))
+        coded = linear_encode(coefficients, scale)
+        place = lax.broadcasted_iota(jnp.int32, coded.shape, 1)
+        coded = jnp.where(place == kept - 1, scale, coded)
+        out_ref[part] = coded.reshape(group * kept, width).astype(BF16)
+
+
+def middle_body(
+    unit_ref, table_upper_ref, table_lower_ref, axial_ref, in_ref, out_ref, *, kept, rows, gain, field
+):
+    sources, _, width = in_ref.shape
+    axial = split(axial_ref[...])
+    table = (table_upper_ref[...], table_lower_ref[...])
+    owners = out_ref.shape[0]
+    parts = []
+    for row in range(rows):
+        coded = in_ref[:, row * kept : (row + 1) * kept, :].astype(F32)
+        values = linear_decode(coded, coded[:, kept - 1 : kept, :])
+        place = lax.broadcasted_iota(jnp.int32, values.shape, 1)
+        values = jnp.where(place == kept - 1, 0.0, values).reshape(sources * kept, width)
+        spectrum = dot3(table, split(values))
+        axial_coef = dot3(split(spectrum), axial, ROWS_BY_ROWS)
+        coded = log_encode(axial_coef, unit_ref[field], gain)
+        parts.append(coded.reshape(owners, -1, width))
+    out_ref[...] = jnp.concatenate(parts, axis=1).astype(BF16)
+
+
+def solve_body(
+    place_ref,
+    unit_ref,
+    diffusion_ref,
+    axial_eigen_ref,
+    radial_eigen_ref,
+    axial_ref,
+    forward_ref,
+    backward_ref,
+    in_ref,
+    *rest,
+    gain,
+    field,
+    radial_devices,
+):
+    out_ref, send_ref, held_ref = rest[-3:]
+    mode = pl.program_id(0)
+    devices, rows, width = in_ref.shape
+    per_group = devices // radial_devices
+    stride = 2 * pl.num_programs(0)
+
+    @pl.when(mode == 0)
+    def _():
+        for source in range(devices):
+            target = (source % radial_devices) * per_group + source // radial_devices
+            values = log_decode(in_ref[source].astype(F32), unit_ref[field], gain)
+            for lane in range(width // 128):
+                held_ref[lane, target * rows : (target + 1) * rows, :] = values[
+                    :, lane * 128 : (lane + 1) * 128
+                ]
+
+    radial = devices * rows // stride
+    pieces = []
+    for part in range(2):
+        for lane in range(width // 128):
+            pieces.append(held_ref[lane, pl.ds(mode * 2 + part, radial, stride=stride), :])
+    values = jnp.concatenate(pieces, axis=1)
+    values = dot3(split(forward_ref[0]), split(values))
+    eigen = jnp.broadcast_to(radial_eigen_ref[0], (128, radial)).T[:, :1]
+    denominator = 1.0 + diffusion_ref[field] * (eigen + axial_eigen_ref[...])
+    inverse = 1.0 / denominator
+    values = jnp.concatenate([values[:, :width] * inverse, values[:, width:] * inverse], axis=1)
+    values = dot3(split(backward_ref[0]), split(values))
+    values = jnp.concatenate([values[:, :width], values[:, width:]], axis=0)
+    values = dot3(split(values), split(axial_ref[...]), ROWS_BY_ROWS)
+    values = values.reshape(2, radial_devices, radial // radial_devices, width)
+    first = place_ref[0] == 0
+    out_ref[0, 0] = jnp.where(first, values[:, 0], values[:, 1])
+    other = jnp.where(first, values[:, 1], values[:, 0]).reshape(radial, width)
+    scale = code_scale(jnp.max(jnp.abs(other), axis=0, keepdims=True))
+    send_ref[0, :radial, :] = linear_encode(other, scale).astype(BF16)
+    send_ref[0, radial:, :] = jnp.broadcast_to(scale, (16, width)).astype(BF16)
+
+
+def finish_body(place_ref, in_ref, _, out_ref):
+    radial, width = out_ref.shape[2] * out_ref.shape[3], out_ref.shape[4]
+    coded = in_ref[0].astype(F32)
+    values = linear_decode(coded[:radial], coded[radial : radial + 1])
+    out_ref[0, 0] = values.reshape(out_ref.shape[2:])
+
+
+def params():
+    return pltpu.CompilerParams(
+        vmem_limit_bytes=VMEM_BYTES, dimension_semantics=("arbitrary",)
+    )
+
+
+def whole(shape):
+    return pl.BlockSpec(shape, lambda *_: (0,) * len(shape))
+
+
+SMEM = pl.BlockSpec(memory_space=pltpu.SMEM)
+
+
+def paired_plan(
+    forcing,
+    diffusion,
+    axial_forward,
+    axial_inverse_map,
+    axial_eigenvalues,
+    radial_forward,
+    radial_backward,
+    radial_eigenvalues,
+):
+    fields, slab, radial_block, width = forcing.shape
+    processors, radial_devices = lax.axis_size("modes"), lax.axis_size("rad")
+    devices = processors * radial_devices
+    total, radial = slab * processors, radial_block * radial_devices
+    own_modes = radial_forward.shape[0]
+    retained = own_modes * devices
+    group = radial_block // processors
+    kept = slab // 2
+    rank = kept - 1
+    axes = ("modes", "rad")
+
+    basis = window_basis(slab, total, retained, rank)
+    spread = np.zeros((group, kept, slab, group))
+    for row in range(group):
+        spread[row, :rank, :, row] = basis.T
+    spread_upper, spread_lower = halves(spread.reshape(group * kept, slab * group))
+    combine = np.zeros((2 * retained, processors, kept))
+    modes = mode_rows(total, retained).reshape(2 * retained, processors, slab)
+    combine[:, :, :rank] = modes @ basis
+    table_upper, table_lower = halves(combine.reshape(2 * retained, processors * kept))
+
+    bound = math.sqrt(total) * 0.375 * width
+    gain = log_gain(bound)
+    largest = jnp.max(jnp.abs(forcing), axis=(1, 2, 3)).astype(F32)
+    unit = lax.pmax(largest, axes) * UNIT_PART
+    place = lax.axis_index("rad").astype(jnp.int32).reshape(1)
+    axial_eigen = axial_eigenvalues.reshape(1, width)
+    radial_eigen = radial_eigenvalues.reshape(own_modes, 1, radial)
+
+    def encode(field):
+        steps = processors // 2
+        return pl.pallas_call(
+            functools.partial(encode_body, group=group, kept=kept),
+            grid=(steps,),
+            in_specs=[
+                whole(spread_upper.shape),
+                whole(spread_lower.shape),
+                pl.BlockSpec((1, slab, 2 * group, width), lambda i: (field, 0, i, 0)),
+            ],
+            out_specs=pl.BlockSpec((2, group * kept, width), lambda i: (i, 0, 0)),
+            out_shape=jax.ShapeDtypeStruct((processors, group * kept, width), BF16),
+            compiler_params=params(),
+            name="window_coefficients",
+        )(jnp.asarray(spread_upper), jnp.asarray(spread_lower), forcing)
+
+    def middle(field, received):
+        rows = 2
+        per_owner = 2 * own_modes
+        return pl.pallas_call(
+            functools.partial(middle_body, kept=kept, rows=rows, gain=gain, field=field),
+            grid=(group // rows,),
+            in_specs=[
+                SMEM,
+                whole(table_upper.shape),
+                whole(table_lower.shape),
+                whole(axial_forward.shape),
+                pl.BlockSpec((processors, rows * kept, width), lambda i: (0, i, 0)),
+            ],
+            out_specs=pl.BlockSpec((devices, rows * per_owner, width), lambda i: (0, i, 0)),
+            out_shape=jax.ShapeDtypeStruct((devices, group * per_owner, width), BF16),
+            compiler_params=params(),
+            name="modal_axial_coefficients",
+        )(unit, jnp.asarray(table_upper), jnp.asarray(table_lower), axial_forward, received)
+
+    out_shape = jax.ShapeDtypeStruct((fields, own_modes * radial_devices, 2, radial_block, width), F32)
+    out_block = (1, 1, 2, radial_block, width)
+    send_rows = radial + 16
+
+    def solve(field, received, out):
+        carried = [] if out is None else [out]
+        first = 9
+        return pl.pallas_call(
+            functools.partial(solve_body, gain=gain, field=field, radial_devices=radial_devices),
+            grid_spec=pltpu.PrefetchScalarGridSpec(
+                num_scalar_prefetch=1,
+                grid=(own_modes,),
+                in_specs=[
+                    SMEM,
+                    SMEM,
+                    whole(axial_eigen.shape),
+                    pl.BlockSpec((1, 1, radial), lambda i, _: (i, 0, 0)),
+                    whole(axial_inverse_map.shape),
+                    pl.BlockSpec((1, radial, radial), lambda i, _: (i, 0, 0)),
+                    pl.BlockSpec((1, radial, radial), lambda i, _: (i, 0, 0)),
+                    whole(received.shape),
+                ]
+                + [pl.BlockSpec(memory_space=pl.ANY) for _ in carried],
+                out_specs=[
+                    pl.BlockSpec(out_block, lambda i, y: (field, y[0] * own_modes + i, 0, 0, 0)),
+                    pl.BlockSpec((1, send_rows, width), lambda i, _: (i, 0, 0)),
+                ],
+                scratch_shapes=[
+                    pltpu.VMEM((width // 128, received.shape[0] * received.shape[1], 128), F32)
+                ],
+            ),
+            out_shape=[out_shape, jax.ShapeDtypeStruct((own_modes, send_rows, width), BF16)],
+            input_output_aliases={first: 0} if carried else {},
+            compiler_params=params(),
+            name="radial_solve",
+        )(
+            place,
+            unit,
+            diffusion,
+            axial_eigen,
+            radial_eigen,
+            axial_inverse_map,
+            radial_forward,
+            radial_backward,
+            received,
+            *carried,
+        )
+
+    def finish(field, received, out):
+        return pl.pallas_call(
+            finish_body,
+            grid_spec=pltpu.PrefetchScalarGridSpec(
+                num_scalar_prefetch=1,
+                grid=(own_modes,),
+                in_specs=[
+                    pl.BlockSpec((1, send_rows, width), lambda i, _: (i, 0, 0)),
+                    pl.BlockSpec(memory_space=pl.ANY),
+                ],
+                out_specs=pl.BlockSpec(
+                    out_block, lambda i, y: (field, (1 - y[0]) * own_modes + i, 0, 0, 0)
+                ),
+            ),
+            out_shape=out_shape,
+            input_output_aliases={2: 0},
+            compiler_params=params(),
+            name="partner_rows",
+        )(place, received, out)
+
+    def exchange(values, names):
+        return lax.all_to_all(values, names, split_axis=0, concat_axis=0, tiled=True)
+
+    windows = [exchange(encode(field), "modes") for field in range(fields)]
+    spectra = [exchange(middle(field, windows[field]), axes) for field in range(fields)]
+    out, sent = None, []
+    for field in range(fields):
+        out, send = solve(field, spectra[field], out)
+        sent.append(lax.ppermute(send, "rad", [(0, 1), (1, 0)]))
+        if field:
+            out = finish(field - 1, sent[field - 1], out)
+    return finish(fields - 1, sent[fields - 1], out)
 
 
 def azimuthal_tables(retained, points):
@@ -33,7 +386,7 @@
     )
 
 
-def per_device(
+def general_plan(
     forcing,
     diffusion,
     axial_forward,
@@ -73,6 +426,22 @@
     return jnp.einsum("fmcrq,zq->fmcrz", returned, axial_inverse_map, precision=highest_mode)
 
 
+def per_device(forcing, diffusion, axial_forward, *maps):
+    processors, radial_devices = lax.axis_size("modes"), lax.axis_size("rad")
+    _, slab, radial_block, width = forcing.shape
+    own_modes = maps[2].shape[0]
+    paired = (
+        radial_devices == 2
+        and radial_block == 8 * processors
+        and width % 128 == 0
+        and own_modes == 4
+        and slab % 32 == 0
+        and slab * processors == 8 * own_modes * processors * radial_devices
+    )
+    plan = paired_plan if paired else general_plan
+    return plan(forcing, diffusion, axial_forward, *maps)
+
+
 def solution(mesh):
     in_specs = (
         P(None, "modes", "rad", None),

time: 937 us -> 327 us (0.35)
  waiting for transfers between devices: 450 us -> 126 us
  local copies, waits for them, and re-layouts: 212 us -> 26.8 us
  blocking collectives: 163 us -> 59.2 us
  Pallas kernels: 0 us -> 69.9 us
  matrix products: 62.8 us -> 0 us
  starting transfers between devices: 18.2 us -> 35.2 us
  between operations: 13.8 us -> 0.29 us
    all_to_all x3 -> x6, waiting for transfers between devices: 449 us -> 104 us  [exchange(): lax.all_to_all(values, names, split_axis=0, concat_axis=0, tiled=True)]
    all_gather x1 -> x0, blocking collectives: 90.8 us -> none  [per_device(): lax.all_gather(radial_eigenvalues, 'rad', axis=0, tiled=True)]
    all_to_all x6 -> x0, local copies, waits for them, and re-layouts: 86.1 us -> none  [the longest x1 45.6 us: per_device(): lax.all_to_all(flat_values, 'modes', split_axis=2, concat_axis=1, tiled=T...]
    all_to_all x1 -> x0, blocking collectives: 72.6 us -> none  [per_device(): lax.all_to_all(solved, 'rad', split_axis=3, concat_axis=4, tiled=True)]
    pallas_call x0 -> x12, Pallas kernels: none -> 69.9 us  [the longest x3 21.6 us: middle(): pl.pallas_call(functools.partial(middle_body, kept=kept, rows=rows, gain=...]
    unnamed x16 -> x68, local copies, waits for them, and re-layouts: 90.4 us -> 26.8 us
    dot_general x6 -> x0, matrix products: 62.8 us -> none  [the longest x1 14.5 us: modal_solve(): jnp.einsum('hzv,bhtvp->bhtzp', forward_map, spectral_coefficients, precis...]
    pmax x0 -> x1, blocking collectives: none -> 59.2 us  [paired_plan(): unit = lax.pmax(largest, axes) * UNIT_PART]
  transfers between devices with their start and end apart: 5 -> 9, of which waited for: 2 -> 7; matrix products, arithmetic and copies ran while one was open for 8% -> 2% of each run, Pallas kernels for 0% -> 19%
where the time goes in v1:
time: 327 us; the launch traced here: 324 us
  waiting for transfers between devices  126 us (39%)
  Pallas kernels  69.9 us (21%)
  blocking collectives  59.2 us (18%)
  starting transfers between devices  35.2 us (11%)
  local copies, waits for them, and re-layouts  26.8 us (8%)
  other arithmetic  6.95 us (2%)
    all_to_all x6, waiting for transfers between devices, exchange(): lax.all_to_all(values, names, split_axis=0, concat_axis=0, tiled=True)  104 us
    pmax x1, blocking collectives, paired_plan(): unit = lax.pmax(largest, axes) * UNIT_PART  59.2 us
    all_to_all x6, starting transfers between devices, exchange(): lax.all_to_all(values, names, split_axis=0, concat_axis=0, tiled=True)  33.7 us
    unnamed x68, local copies, waits for them, and re-layouts  26.8 us
    ppermute x3, waiting for transfers between devices, paired_plan(): sent.append(lax.ppermute(send, 'rad', [(0, 1), (1, 0)]))  21.9 us
    pallas_call x3, Pallas kernels, middle(): pl.pallas_call(functools.partial(middle_body, kept=kept, rows=rows, gain=...  21.6 us
    pallas_call x3, Pallas kernels, encode(): pl.pallas_call(functools.partial(encode_body, group=group, kept=kept), gr...  21.4 us
    pallas_call x3, Pallas kernels, solve(): pl.pallas_call(functools.partial(solve_body, gain=gain, field=field, radi...  20.3 us
  transfers between devices with their start and end apart: 9, of which 7 were waited for; matrix products, arithmetic and copies ran while one was open for 2% of the time, Pallas kernels for 19%

profile of v1, /device:TPU:17, one launch (start us, length us, event | category | flops | bytes accessed | tf_op | source)
XLA Modules:
  0.0 324.4 jit_solution(3634065821505432987)
XLA Ops:
  1.0 0.9 copy-done.29
  1.9 7.2 %window_coefficients.4 = bf16[16,256,256]{2,1,0:T(8,128)(2,1)S(1)} custom-call(bf16[256,512]{1,0:T(8,128)(2,1)S(1)} %copy-done.27, bf16[256,512]{1,0:T(8,128)(2,1)S(1)} %copy-done.29, bf16[3,64,128,256]{3,2,1,0:T(8,128)(2,1)} %forcing_ref.5), custom_call_target="tpu_custom_call" | custom-call | tf_op jit(solution)/shard_map/window_coefficients/pallas_call | solution.py:247
  9.1 1.3 copy-done.10
  10.4 6.5 %all-to-all-start.2 = ((bf16[16,256,256]{2,1,0:T(8,128)(2,1)}), bf16[16,256,256]{2,1,0:T(8,128)(2,1)S(1)}, u32[]{:S(2)}, u32[]{:S(2)}) async-start(bf16[16,256,256]{2,1,0:T(8,128)(2,1)} %copy-done.10), calls=%async_computation.2 | async-start | bytes 4194304 | tf_op jit(solution)/shard_map/all_to_all | solution.py:349
  16.9 7.1 %window_coefficients.5 = bf16[16,256,256]{2,1,0:T(8,128)(2,1)S(1)} custom-call(bf16[256,512]{1,0:T(8,128)(2,1)S(1)} %copy-done.28, bf16[256,512]{1,0:T(8,128)(2,1)S(1)} %copy-done.30, bf16[3,64,128,256]{3,2,1,0:T(8,128)(2,1)} %forcing_ref.5), custom_call_target="tpu_custom_call" | custom-call | tf_op jit(solution)/shard_map/window_coefficients/pallas_call | solution.py:247
  24.0 1.3 copy-done.9
  25.3 38.7 %all-to-all-done.2.in_ref = bf16[16,256,256]{2,1,0:T(8,128)(2,1)S(1)} async-done(((bf16[16,256,256]{2,1,0:T(8,128)(2,1)}), bf16[16,256,256]{2,1,0:T(8,128)(2,1)S(1)}, u32[]{:S(2)}, u32[]{:S(2)}) %all-to-all-start.2) | async-done | bytes 2097184 | tf_op jit(solution)/shard_map/all_to_all | solution.py:349
  64.0 1.3 copy-done.6
  65.3 5.2 %all-to-all-start.4 = ((bf16[16,256,256]{2,1,0:T(8,128)(2,1)}), bf16[16,256,256]{2,1,0:T(8,128)(2,1)S(1)}, u32[]{:S(2)}, u32[]{:S(2)}) async-start(bf16[16,256,256]{2,1,0:T(8,128)(2,1)} %copy-done.9), calls=%async_computation.4 | async-start | bytes 4194304 | tf_op jit(solution)/shard_map/all_to_all | solution.py:349
  70.5 7.1 %window_coefficients.3 = bf16[16,256,256]{2,1,0:T(8,128)(2,1)S(1)} custom-call(bf16[256,512]{1,0:T(8,128)(2,1)S(1)} %copy-done.28, bf16[256,512]{1,0:T(8,128)(2,1)S(1)} %copy-done.30, bf16[3,64,128,256]{3,2,1,0:T(8,128)(2,1)} %forcing_ref.5), custom_call_target="tpu_custom_call" | custom-call | tf_op jit(solution)/shard_map/window_coefficients/pallas_call | solution.py:247
  77.7 1.3 copy-done.8
  79.0 38.7 %all-to-all-done.4.in_ref = bf16[16,256,256]{2,1,0:T(8,128)(2,1)S(1)} async-done(((bf16[16,256,256]{2,1,0:T(8,128)(2,1)}), bf16[16,256,256]{2,1,0:T(8,128)(2,1)S(1)}, u32[]{:S(2)}, u32[]{:S(2)}) %all-to-all-start.4) | async-done | bytes 2097184 | tf_op jit(solution)/shard_map/all_to_all | solution.py:349
  117.7 1.3 copy-done.4
  119.0 5.2 %all-to-all-start = ((bf16[16,256,256]{2,1,0:T(8,128)(2,1)}), bf16[16,256,256]{2,1,0:T(8,128)(2,1)S(1)}, u32[]{:S(2)}, u32[]{:S(2)}) async-start(bf16[16,256,256]{2,1,0:T(8,128)(2,1)} %copy-done.8), calls=%async_computation | async-start | bytes 4194304 | tf_op jit(solution)/shard_map/all_to_all | solution.py:349
  124.2 6.9 %abs_reduce_fusion = bf16[3]{0:T(256)(128)(2,1)S(1)} fusion(bf16[3,64,128,256]{3,2,1,0:T(8,128)(2,1)} %forcing_ref.5), kind=kLoop, calls=%fused_computation | loop fusion | flops 12582909 | bytes 12582918 | tf_op jit(solution)/shard_map/reduce_max | solution.py:239
  131.2 59.2 %pmax.7 = f32[3]{0:T(128)S(1)} all-reduce(bf16[3]{0:T(256)(128)(2,1)S(1)} %abs_reduce_fusion), channel_id=1, replica_groups=mesh['modes'=16,'rad'=2] {'modes','rad'}, use_global_device_ids=true, to_apply=%region_1.0 | all-reduce | flops 3 | bytes 18 | tf_op jit(solution)/shard_map/pmax | solution.py:240
  190.4 1.6 copy-done.7
  192.0 7.2 %modal_axial_coefficients.4 = bf16[32,64,256]{2,1,0:T(8,128)(2,1)S(1)} custom-call(f32[3]{0:T(128)S(1)} %broadcast_multiply_fusion.unit_ref, bf16[256,512]{1,0:T(8,128)(2,1)S(1)} %copy-done.21, bf16[256,512]{1,0:T(8,128)(2,1)S(1)} %copy-done.24, f32[256,256]{1,0:T(8,128)S(1)} %copy-done.18, bf16[16,256,256]{2,1,0:T(8,128)(2,1)S(1)} %copy-done.7), custom_call_target="tpu_custom_call" | custom-call | tf_op jit(solution)/shard_map/modal_axial_coefficients/pallas_call | solution.py:264
  199.2 1.0 copy-done.17
  200.2 1.3 copy-done.2
  201.6 7.4 %all-to-all-start.3 = ((bf16[32,64,256]{2,1,0:T(8,128)(2,1)}), bf16[32,64,256]{2,1,0:T(8,128)(2,1)S(1)}, u32[]{:S(2)}, u32[]{:S(2)}) async-start(bf16[32,64,256]{2,1,0:T(8,128)(2,1)} %copy-done.17), calls=%async_computation.3 | async-start | bytes 2097152 | tf_op jit(solution)/shard_map/all_to_all | solution.py:349
  209.0 1.6 copy-done.5
  210.6 0.9 copy-done.22
  211.5 0.9 copy-done.25
  212.5 7.2 %modal_axial_coefficients.5 = bf16[32,64,256]{2,1,0:T(8,128)(2,1)S(1)} custom-call(f32[3]{0:T(128)S(1)} %broadcast_multiply_fusion.unit_ref, bf16[256,512]{1,0:T(8,128)(2,1)S(1)} %copy-done.22, bf16[256,512]{1,0:T(8,128)(2,1)S(1)} %copy-done.25, f32[256,256]{1,0:T(8,128)S(1)} %copy-done.18, bf16[16,256,256]{2,1,0:T(8,128)(2,1)S(1)} %copy-done.5), custom_call_target="tpu_custom_call" | custom-call | tf_op jit(solution)/shard_map/modal_axial_coefficients/pallas_call | solution.py:264
  219.7 1.0 copy-done.16
  220.7 13.4 %all-to-all-done.3.in_ref = bf16[32,64,256]{2,1,0:T(8,128)(2,1)S(1)} async-done(((bf16[32,64,256]{2,1,0:T(8,128)(2,1)}), bf16[32,64,256]{2,1,0:T(8,128)(2,1)S(1)}, u32[]{:S(2)}, u32[]{:S(2)}) %all-to-all-start.3) | async-done | bytes 1048608 | tf_op jit(solution)/shard_map/all_to_all | solution.py:349
  234.1 1.0 copy-done.13
  235.1 4.7 %all-to-all-start.5 = ((bf16[32,64,256]{2,1,0:T(8,128)(2,1)}), bf16[32,64,256]{2,1,0:T(8,128)(2,1)S(1)}, u32[]{:S(2)}, u32[]{:S(2)}) async-start(bf16[32,64,256]{2,1,0:T(8,128)(2,1)} %copy-done.16), calls=%async_computation.5 | async-start | bytes 2097152 | tf_op jit(solution)/shard_map/all_to_all | solution.py:349
  239.8 1.6 copy-done.3
  242.4 0.9 copy-done.26
  243.3 7.2 %modal_axial_coefficients.3 = bf16[32,64,256]{2,1,0:T(8,128)(2,1)S(1)} custom-call(f32[3]{0:T(128)S(1)} %broadcast_multiply_fusion.unit_ref, bf16[256,512]{1,0:T(8,128)(2,1)S(1)} %copy-done.23, bf16[256,512]{1,0:T(8,128)(2,1)S(1)} %copy-done.26, f32[256,256]{1,0:T(8,128)S(1)} %copy-done.18, bf16[16,256,256]{2,1,0:T(8,128)(2,1)S(1)} %copy-done.3), custom_call_target="tpu_custom_call" | custom-call | tf_op jit(solution)/shard_map/modal_axial_coefficients/pallas_call | solution.py:264
  250.5 1.0 copy-done.15
  251.5 13.4 %all-to-all-done.5.in_ref = bf16[32,64,256]{2,1,0:T(8,128)(2,1)S(1)} async-done(((bf16[32,64,256]{2,1,0:T(8,128)(2,1)}), bf16[32,64,256]{2,1,0:T(8,128)(2,1)S(1)}, u32[]{:S(2)}, u32[]{:S(2)}) %all-to-all-start.5) | async-done | bytes 1048608 | tf_op jit(solution)/shard_map/all_to_all | solution.py:349
  265.0 1.0 copy-done.11
  265.9 4.7 %all-to-all-start.1 = ((bf16[32,64,256]{2,1,0:T(8,128)(2,1)}), bf16[32,64,256]{2,1,0:T(8,128)(2,1)S(1)}, u32[]{:S(2)}, u32[]{:S(2)}) async-start(bf16[32,64,256]{2,1,0:T(8,128)(2,1)} %copy-done.15), calls=%async_computation.1 | async-start | bytes 2097152 | tf_op jit(solution)/shard_map/all_to_all | solution.py:349
  270.8 1.2 copy-done.14
  272.9 6.7 %radial_solve.3 = (f32[3,8,2,128,256]{4,3,2,1,0:T(8,128)}, bf16[4,272,256]{2,1,0:T(8,128)(2,1)S(1)}) custom-call(s32[1]{0:T(128)} %bitcast.place_ref, f32[3]{0:T(128)S(1)} %broadcast_multiply_fusion.unit_ref, f32[3]{0:T(128)S(1)} %copy-done.32, f32[1,256]{1,0:T(1,128)S(1)} %bitcast.2, f32[4,1,256]{2,1,0:T(1,128)S(1)} %reshape.11.radial_eigen_ref, ...), custom_call_target="tpu_custom_call" | custom-call | tf_op jit(solution)/shard_map/radial_solve/pallas_call | solution.py:287
  279.7 1.2 collective-permute-start
  280.9 1.2 copy-done.12
  282.1 6.8 %radial_solve.4 = (f32[3,8,2,128,256]{4,3,2,1,0:T(8,128)}, bf16[4,272,256]{2,1,0:T(8,128)(2,1)}) custom-call(s32[1]{0:T(128)} %bitcast.place_ref, f32[3]{0:T(128)S(1)} %broadcast_multiply_fusion.unit_ref, f32[3]{0:T(128)S(1)} %copy-done.32, f32[1,256]{1,0:T(1,128)S(1)} %bitcast.3, ...), custom_call_target="tpu_custom_call", output_to_operand_aliasing={{0}: (9, {})} | custom-call | tf_op jit(solution)/shard_map/radial_solve/pallas_call | solution.py:287
  289.2 9.8 %collective-permute-done.in_ref = bf16[4,272,256]{2,1,0:T(8,128)(2,1)S(1)} collective-permute-done((bf16[4,272,256]{2,1,0:T(8,128)(2,1)S(1)}, bf16[4,272,256]{2,1,0:T(8,128)(2,1)S(1)}, u32[]{:S(2)}, u32[]{:S(2)}) %collective-permute-start) | collective-permute-done | bytes 557088 | tf_op jit(solution)/shard_map/ppermute | solution.py:356
  299.0 1.6 partner_rows.3.rest_0_
  300.6 6.8 %radial_solve.5 = (f32[3,8,2,128,256]{4,3,2,1,0:T(8,128)}, bf16[4,272,256]{2,1,0:T(8,128)(2,1)S(1)}) custom-call(s32[1]{0:T(128)} %bitcast.place_ref, f32[3]{0:T(128)S(1)} %broadcast_multiply_fusion.unit_ref, f32[3]{0:T(128)S(1)} %copy-done.32, f32[1,256]{1,0:T(1,128)S(1)} %bitcast.4, ...), custom_call_target="tpu_custom_call", output_to_operand_aliasing={{0}: (9, {})} | custom-call | tf_op jit(solution)/shard_map/radial_solve/pallas_call | solution.py:287
  307.4 3.7 %collective-permute-done.2.in_ref = bf16[4,272,256]{2,1,0:T(8,128)(2,1)} collective-permute-done((bf16[4,272,256]{2,1,0:T(8,128)(2,1)}, bf16[4,272,256]{2,1,0:T(8,128)(2,1)}, u32[]{:S(2)}, u32[]{:S(2)}) %collective-permute-start.2) | collective-permute-done | bytes 557088 | tf_op jit(solution)/shard_map/ppermute | solution.py:356
  311.0 3.3 %partner_rows.4._ = f32[3,8,2,128,256]{4,3,2,1,0:T(8,128)} custom-call(s32[1]{0:T(128)} %bitcast.place_ref, bf16[4,272,256]{2,1,0:T(8,128)(2,1)} %collective-permute-done.2.in_ref, f32[3,8,2,128,256]{4,3,2,1,0:T(8,128)} %get-tuple-element.16._), custom_call_target="tpu_custom_call", output_to_operand_aliasing={{}: (2, {})} | custom-call | tf_op jit(solution)/shard_map/partner_rows/pallas_call | solution.py:329
  314.4 8.4 %collective-permute-done.1.in_ref = bf16[4,272,256]{2,1,0:T(8,128)(2,1)S(1)} collective-permute-done((bf16[4,272,256]{2,1,0:T(8,128)(2,1)S(1)}, bf16[4,272,256]{2,1,0:T(8,128)(2,1)S(1)}, u32[]{:S(2)}, u32[]{:S(2)}) %collective-permute-start.1) | collective-permute-done | bytes 557088 | tf_op jit(solution)/shard_map/ppermute | solution.py:356
  322.8 1.6 partner_rows.5
  (54 shorter events, 3.2 us)
Async XLA Ops:
  0.0 0.9 copy-start.27
  1.0 0.9 copy-start.29
  1.9 15.0 %copy-start.28 = (bf16[256,512]{1,0:T(8,128)(2,1)S(1)}, bf16[256,512]{1,0:T(8,128)(2,1)}, u32[]{:S(2)}) copy-start(bf16[256,512]{1,0:T(8,128)(2,1)} %constant.16.clone.upper_ref) | copy-start | bytes 786436
  1.9 15.0 %copy-start.30 = (bf16[256,512]{1,0:T(8,128)(2,1)S(1)}, bf16[256,512]{1,0:T(8,128)(2,1)}, u32[]{:S(2)}) copy-start(bf16[256,512]{1,0:T(8,128)(2,1)} %constant.17.clone.lower_ref) | copy-start | bytes 786436
  9.1 1.3 copy-start.10
  10.4 53.6 %all-to-all-start.2 = ((bf16[16,256,256]{2,1,0:T(8,128)(2,1)}), bf16[16,256,256]{2,1,0:T(8,128)(2,1)S(1)}, u32[]{:S(2)}, u32[]{:S(2)}) async-start(bf16[16,256,256]{2,1,0:T(8,128)(2,1)} %copy-done.10), calls=%async_computation.2 | async-start | bytes 4194304 | tf_op jit(solution)/shard_map/all_to_all | solution.py:349
  24.0 1.3 copy-start.9
  64.0 1.3 copy-start.6
  65.3 52.3 %all-to-all-start.4 = ((bf16[16,256,256]{2,1,0:T(8,128)(2,1)}), bf16[16,256,256]{2,1,0:T(8,128)(2,1)S(1)}, u32[]{:S(2)}, u32[]{:S(2)}) async-start(bf16[16,256,256]{2,1,0:T(8,128)(2,1)} %copy-done.9), calls=%async_computation.4 | async-start | bytes 4194304 | tf_op jit(solution)/shard_map/all_to_all | solution.py:349
  77.7 1.3 copy-start.8
  117.7 1.3 copy-start.4
  119.0 81.2 %all-to-all-start = ((bf16[16,256,256]{2,1,0:T(8,128)(2,1)}), bf16[16,256,256]{2,1,0:T(8,128)(2,1)S(1)}, u32[]{:S(2)}, u32[]{:S(2)}) async-start(bf16[16,256,256]{2,1,0:T(8,128)(2,1)} %copy-done.8), calls=%async_computation | async-start | bytes 4194304 | tf_op jit(solution)/shard_map/all_to_all | solution.py:349
  124.2 66.2 %copy-start.18 = (f32[256,256]{1,0:T(8,128)S(1)}, f32[256,256]{1,0:T(8,128)}, u32[]{:S(2)}) copy-start(f32[256,256]{1,0:T(8,128)} %axial_ref.9) | copy-start | bytes 786436
  124.2 66.2 %copy-start.21 = (bf16[256,512]{1,0:T(8,128)(2,1)S(1)}, bf16[256,512]{1,0:T(8,128)(2,1)}, u32[]{:S(2)}) copy-start(bf16[256,512]{1,0:T(8,128)(2,1)} %constant.18.clone.table_upper_ref) | copy-start | bytes 786436
  124.2 66.2 %copy-start.24 = (bf16[256,512]{1,0:T(8,128)(2,1)S(1)}, bf16[256,512]{1,0:T(8,128)(2,1)}, u32[]{:S(2)}) copy-start(bf16[256,512]{1,0:T(8,128)(2,1)} %constant.19.clone.table_lower_ref) | copy-start | bytes 786436
  190.4 1.6 copy-start.7
  199.2 1.0 copy-start.17
  200.2 1.3 copy-start.2
  201.6 32.6 %all-to-all-start.3 = ((bf16[32,64,256]{2,1,0:T(8,128)(2,1)}), bf16[32,64,256]{2,1,0:T(8,128)(2,1)S(1)}, u32[]{:S(2)}, u32[]{:S(2)}) async-start(bf16[32,64,256]{2,1,0:T(8,128)(2,1)} %copy-done.17), calls=%async_computation.3 | async-start | bytes 2097152 | tf_op jit(solution)/shard_map/all_to_all | solution.py:349
  209.0 1.6 copy-start.5
  210.6 0.9 copy-start.22
  211.5 0.9 copy-start.25
  212.5 58.2 %copy-start.33 = (f32[4,256]{1,0:T(4,128)S(1)}, f32[4,256]{1,0:T(4,128)}, u32[]{:S(2)}) copy-start(f32[4,256]{1,0:T(4,128)} %param.19) | copy-start | bytes 12292
  212.5 58.2 %copy-start = (f32[4,256,256]{2,1,0:T(8,128)S(1)}, f32[4,256,256]{2,1,0:T(8,128)}, u32[]{:S(2)}) copy-start(f32[4,256,256]{2,1,0:T(8,128)} %forward_ref.5) | copy-start | bytes 3145732
  212.5 58.2 %copy-start.1 = (f32[4,256,256]{2,1,0:T(8,128)S(1)}, f32[4,256,256]{2,1,0:T(8,128)}, u32[]{:S(2)}) copy-start(f32[4,256,256]{2,1,0:T(8,128)} %backward_ref.5) | copy-start | bytes 3145732
  212.5 58.2 %copy-start.31 = (f32[256]{0:T(256)S(1)}, f32[256]{0:T(256)}, u32[]{:S(2)}) copy-start(f32[256]{0:T(256)} %param.16) | copy-start | bytes 3076
  212.5 58.2 %copy-start.32 = (f32[3]{0:T(128)S(1)}, f32[3]{0:T(128)}, u32[]{:S(2)}) copy-start(f32[3]{0:T(128)} %diffusion_ref.5) | copy-start | bytes 40
  219.7 1.0 copy-start.16
  234.1 1.0 copy-start.13
  235.1 29.9 %all-to-all-start.5 = ((bf16[32,64,256]{2,1,0:T(8,128)(2,1)}), bf16[32,64,256]{2,1,0:T(8,128)(2,1)S(1)}, u32[]{:S(2)}, u32[]{:S(2)}) async-start(bf16[32,64,256]{2,1,0:T(8,128)(2,1)} %copy-done.16), calls=%async_computation.5 | async-start | bytes 2097152 | tf_op jit(solution)/shard_map/all_to_all | solution.py:349
  239.8 1.6 copy-start.3
  241.4 0.9 copy-start.23
  242.4 0.9 copy-start.26
  250.5 1.0 copy-start.15
  265.0 1.0 copy-start.11
  265.9 34.7 %all-to-all-start.1 = ((bf16[32,64,256]{2,1,0:T(8,128)(2,1)}), bf16[32,64,256]{2,1,0:T(8,128)(2,1)S(1)}, u32[]{:S(2)}, u32[]{:S(2)}) async-start(bf16[32,64,256]{2,1,0:T(8,128)(2,1)} %copy-done.15), calls=%async_computation.1 | async-start | bytes 2097152 | tf_op jit(solution)/shard_map/all_to_all | solution.py:349
  270.7 1.2 copy-start.14
  272.0 0.9 copy-start.19
  279.7 19.3 %collective-permute-start = (bf16[4,272,256]{2,1,0:T(8,128)(2,1)S(1)}, bf16[4,272,256]{2,1,0:T(8,128)(2,1)S(1)}, u32[]{:S(2)}, u32[]{:S(2)}) collective-permute-start(bf16[4,272,256]{2,1,0:T(8,128)(2,1)S(1)} %get-tuple-element.11), channel_id=1, source_target_pairs={{0,1},{1,0},{2,3},{3,2},{4,5},{5,4},{6,7},{7,6},{8,9},{9,8},{10,11... | collective-permute-start | bytes 1671176 | tf_op jit(solution)/shard_map/ppermute | solution.py:356
  280.9 1.2 copy-start.12
  288.9 22.1 %collective-permute-start.2 = (bf16[4,272,256]{2,1,0:T(8,128)(2,1)}, bf16[4,272,256]{2,1,0:T(8,128)(2,1)}, u32[]{:S(2)}, u32[]{:S(2)}) collective-permute-start(bf16[4,272,256]{2,1,0:T(8,128)(2,1)} %get-tuple-element.15), channel_id=1, source_target_pairs={{0,1},{1,0},{2,3},{3,2},{4,5},{5,4},{6,7},{7,6},{8,9},{9,8},{10,11... | collective-permute-start | bytes 1671176 | tf_op jit(solution)/shard_map/ppermute | solution.py:356
  299.0 1.6 copy-start.20
  307.4 15.4 %collective-permute-start.1 = (bf16[4,272,256]{2,1,0:T(8,128)(2,1)S(1)}, bf16[4,272,256]{2,1,0:T(8,128)(2,1)S(1)}, u32[]{:S(2)}, u32[]{:S(2)}) collective-permute-start(bf16[4,272,256]{2,1,0:T(8,128)(2,1)S(1)} %get-tuple-element.14), channel_id=1, source_target_pairs={{0,1},{1,0},{2,3},{3,2},{4,5},{5,4},{6,7},{7,6},{8,9},{9,8},{10,11... | collective-permute-start | bytes 1671176 | tf_op jit(solution)/shard_map/ppermute | solution.py:356

commit v2 on v1

--- a/solution.py
+++ b/solution.py
@@ -11,7 +11,7 @@
 
 BF16 = jnp.bfloat16
 F32 = jnp.float32
-VMEM_BYTES = 48 * 1024 * 1024
+VMEM_BYTES = 60 * 1024 * 1024
 
 CODE_SPAN = 126.0
 CODE_MID = 0.5
@@ -19,9 +19,6 @@
 DECODE_SLOPE = 1.0 / (LN2 * CODE_SPAN)
 DECODE_SHIFT = CODE_MID / CODE_SPAN
 TINY = 1e-35
-LOG_BASE = 125.0
-LOG_RANGE = 250.0
-UNIT_PART = 2.0**-6
 
 
 def code_scale(largest):
@@ -37,28 +34,10 @@
     return scale * (jnp.log(coded) * DECODE_SLOPE - DECODE_SHIFT)
 
 
-def log_gain(bound):
-    return LOG_RANGE / math.log2(1.0 + bound / UNIT_PART)
-
-
-def log_encode(values, unit, gain):
-    inverse = jnp.where(unit > TINY, 1.0 / jnp.maximum(unit, TINY), 0.0)
-    magnitude = jnp.exp2(jnp.log(1.0 + jnp.abs(values) * inverse) * (gain / LN2) - LOG_BASE)
-    return jnp.where(values < 0.0, -magnitude, magnitude)
-
-
-def log_decode(coded, unit, gain):
-    magnitude = jnp.exp2(jnp.log(jnp.abs(coded)) * (1.0 / (LN2 * gain)) + LOG_BASE / gain)
-    magnitude = unit * (magnitude - 1.0)
-    return jnp.where(coded < 0.0, -magnitude, magnitude)
-
-
-def window_basis(window, total, retained, rank):
+def window_basis(window, total, band, rank):
     points = np.arange(window)
     inner = np.arange(1, window)
-    diagonal = np.cos(np.pi * (2 * points - window + 1) / total) * np.cos(
-        np.pi * (2 * retained - 1) / total
-    )
+    diagonal = np.cos(np.pi * (2 * points - window + 1) / total) * np.cos(np.pi * band / total)
     beside = -np.sin(np.pi * inner / total) * np.sin(np.pi * (window - inner) / total)
     _, vectors = np.linalg.eigh(np.diag(diagonal) + np.diag(beside, 1) + np.diag(beside, -1))
     basis = vectors[:, :rank]
@@ -66,11 +45,38 @@
     return basis * signs
 
 
-def mode_rows(total, retained):
-    phase = np.arange(retained)[:, None] * np.arange(total)[None, :] % total
-    radians = phase * (2.0 * np.pi / total)
-    rows = np.stack([np.cos(radians), -np.sin(radians)], axis=1) / np.sqrt(total)
-    return rows.reshape(2 * retained, total)
+def waves(modes, points, total):
+    return np.exp(-2j * np.pi * (modes[:, None] * points[None, :] % total) / total)
+
+
+def interleave(values):
+    return np.stack([values.real, values.imag], axis=1).reshape(-1, values.shape[-1])
+
+
+def half_tables(total, retained, slab, basis, sent):
+    half, own = total // 2, retained // 2
+    rank = basis.shape[1]
+    envelope = window_basis(half, total, own, (sent - 1) // 2)
+    local, join = [], []
+    for side in range(2):
+        points = side * half + np.arange(half)
+        away = (1 - side) * own + np.arange(own)
+        centre = (1 - side) * own + 0.5 * (own - 1)
+        direct = waves(side * own + np.arange(own), points, total) / np.sqrt(total)
+        carried = np.exp(-2j * np.pi * centre * points / total)[None, :] * envelope.T
+        rows = np.concatenate([interleave(direct), interleave(carried)])
+        rows = rows.reshape(rows.shape[0], -1, slab) @ basis
+        table = np.zeros((2 * own + sent, half // slab, rank + 1))
+        table[: rows.shape[0], :, :rank] = rows
+        local.append(table.reshape(table.shape[0], -1))
+        offsets = np.exp(-2j * np.pi * (away - centre)[:, None] * points[None, :] / total)
+        weights = (offsets @ envelope) / np.sqrt(total)
+        parts = np.zeros((own, 2, sent))
+        count = 2 * weights.shape[1]
+        parts[:, 0, 0:count:2], parts[:, 0, 1:count:2] = weights.real, -weights.imag
+        parts[:, 1, 0:count:2], parts[:, 1, 1:count:2] = weights.imag, weights.real
+        join.append(parts.reshape(2 * own, sent))
+    return np.stack(local), np.stack(join[::-1])
 
 
 def halves(table):
@@ -91,6 +97,18 @@
 
 
 ROWS_BY_ROWS = ((1,), (1,))
+
+
+def encode_columns(values, kept):
+    scale = code_scale(jnp.max(jnp.abs(values), axis=1, keepdims=True))
+    place = lax.broadcasted_iota(jnp.int32, values.shape, 1)
+    return jnp.where(place == kept - 1, scale, linear_encode(values, scale))
+
+
+def decode_columns(coded, kept):
+    values = linear_decode(coded, coded[:, kept - 1 : kept, :])
+    place = lax.broadcasted_iota(jnp.int32, values.shape, 1)
+    return jnp.where(place == kept - 1, 0.0, values)
 
 
 def encode_body(upper_ref, lower_ref, forcing_ref, out_ref, *, group, kept):
@@ -101,37 +119,50 @@
         piece = piece.astype(BF16)
         coefficients = jnp.dot(upper_ref[...], piece, preferred_element_type=F32)
         coefficients += jnp.dot(lower_ref[...], piece, preferred_element_type=F32)
-        coefficients = coefficients.reshape(group, kept, width)
-        scale = code_scale(jnp.max(jnp.abs(coefficients), axis=1, keepdims=True))
-        coded = linear_encode(coefficients, scale)
-        place = lax.broadcasted_iota(jnp.int32, coded.shape, 1)
-        coded = jnp.where(place == kept - 1, scale, coded)
-        out_ref[part] = coded.reshape(group * kept, width).astype(BF16)
-
-
-def middle_body(
-    unit_ref, table_upper_ref, table_lower_ref, axial_ref, in_ref, out_ref, *, kept, rows, gain, field
-):
+        coded = encode_columns(coefficients.reshape(group, kept, width), kept)
+        place = part * group * kept
+        out_ref[0, place : place + group * kept, :] = coded.reshape(group * kept, width).astype(BF16)
+
+
+def gather_body(_, upper_ref, lower_ref, in_ref, own_ref, send_ref, *, kept, sent, rows):
     sources, _, width = in_ref.shape
-    axial = split(axial_ref[...])
-    table = (table_upper_ref[...], table_lower_ref[...])
-    owners = out_ref.shape[0]
-    parts = []
+    table = (upper_ref[0], lower_ref[0])
+    own = own_ref.shape[1]
     for row in range(rows):
         coded = in_ref[:, row * kept : (row + 1) * kept, :].astype(F32)
-        values = linear_decode(coded, coded[:, kept - 1 : kept, :])
-        place = lax.broadcasted_iota(jnp.int32, values.shape, 1)
-        values = jnp.where(place == kept - 1, 0.0, values).reshape(sources * kept, width)
-        spectrum = dot3(table, split(values))
-        axial_coef = dot3(split(spectrum), axial, ROWS_BY_ROWS)
-        coded = log_encode(axial_coef, unit_ref[field], gain)
-        parts.append(coded.reshape(owners, -1, width))
-    out_ref[...] = jnp.concatenate(parts, axis=1).astype(BF16)
+        values = decode_columns(coded, kept).reshape(sources * kept, width)
+        sums = dot3(table, split(values))
+        own_ref[row] = sums[:own]
+        send_ref[row * sent : (row + 1) * sent, :] = encode_columns(sums[None, own:], sent)[0].astype(BF16)
+
+
+def join_body(_, upper_ref, lower_ref, axial_ref, own_ref, in_ref, out_ref, held_ref, *, sent, rows):
+    step = pl.program_id(0)
+    width = in_ref.shape[1]
+    owners, coded_rows = out_ref.shape[:2]
+    block = coded_rows - 16
+    table = (upper_ref[0], lower_ref[0])
+    axial = split(axial_ref[...])
+    for row in range(rows):
+        coded = in_ref[row * sent : (row + 1) * sent, :].astype(F32)
+        values = decode_columns(coded[None], sent)[0]
+        spectrum = own_ref[row] + dot3(table, split(values))
+        axial_coef = dot3(split(spectrum), axial, ROWS_BY_ROWS).reshape(owners, -1, width)
+        each = axial_coef.shape[1]
+        place = pl.multiple_of((step * rows + row) * each, each)
+        held_ref[:, pl.ds(place, each), :] = axial_coef
+
+    @pl.when(step == pl.num_programs(0) - 1)
+    def _():
+        for owner in range(owners):
+            values = held_ref[owner]
+            scale = code_scale(jnp.max(jnp.abs(values), axis=0, keepdims=True))
+            out_ref[owner, :block, :] = linear_encode(values, scale).astype(BF16)
+            out_ref[owner, block:, :] = jnp.broadcast_to(scale, (16, width)).astype(BF16)
 
 
 def solve_body(
     place_ref,
-    unit_ref,
     diffusion_ref,
     axial_eigen_ref,
     radial_eigen_ref,
@@ -140,13 +171,13 @@
     backward_ref,
     in_ref,
     *rest,
-    gain,
     field,
     radial_devices,
 ):
     out_ref, send_ref, held_ref = rest[-3:]
     mode = pl.program_id(0)
-    devices, rows, width = in_ref.shape
+    devices, coded_rows, width = in_ref.shape
+    rows = coded_rows - 16
     per_group = devices // radial_devices
     stride = 2 * pl.num_programs(0)
 
@@ -154,7 +185,8 @@
     def _():
         for source in range(devices):
             target = (source % radial_devices) * per_group + source // radial_devices
-            values = log_decode(in_ref[source].astype(F32), unit_ref[field], gain)
+            coded = in_ref[source].astype(F32)
+            values = linear_decode(coded[:rows], coded[rows : rows + 1])
             for lane in range(width // 128):
                 held_ref[lane, target * rows : (target + 1) * rows, :] = values[
                     :, lane * 128 : (lane + 1) * 128
@@ -196,6 +228,12 @@
     )
 
 
+def cost(microseconds):
+    return pl.CostEstimate(
+        flops=int(microseconds * 3e8), bytes_accessed=int(microseconds * 3e6), transcendentals=0
+    )
+
+
 def whole(shape):
     return pl.BlockSpec(shape, lambda *_: (0,) * len(shape))
 
@@ -219,63 +257,93 @@
     total, radial = slab * processors, radial_block * radial_devices
     own_modes = radial_forward.shape[0]
     retained = own_modes * devices
-    group = radial_block // processors
-    kept = slab // 2
-    rank = kept - 1
-    axes = ("modes", "rad")
-
-    basis = window_basis(slab, total, retained, rank)
+    near = processors // 2
+    owners = near * radial_devices
+    rows = radial_block // near
+    group, kept, sent = 8, slab // 2, 96
+    per_owner = 2 * own_modes
+    side = lax.axis_index("modes") // near
+    place = jnp.stack([lax.axis_index("rad"), side]).astype(jnp.int32)
+
+    basis = window_basis(slab, total, 2 * retained - 1, kept - 1)
     spread = np.zeros((group, kept, slab, group))
     for row in range(group):
-        spread[row, :rank, :, row] = basis.T
+        spread[row, : kept - 1, :, row] = basis.T
     spread_upper, spread_lower = halves(spread.reshape(group * kept, slab * group))
-    combine = np.zeros((2 * retained, processors, kept))
-    modes = mode_rows(total, retained).reshape(2 * retained, processors, slab)
-    combine[:, :, :rank] = modes @ basis
-    table_upper, table_lower = halves(combine.reshape(2 * retained, processors * kept))
-
-    bound = math.sqrt(total) * 0.375 * width
-    gain = log_gain(bound)
-    largest = jnp.max(jnp.abs(forcing), axis=(1, 2, 3)).astype(F32)
-    unit = lax.pmax(largest, axes) * UNIT_PART
-    place = lax.axis_index("rad").astype(jnp.int32).reshape(1)
+    local, join_table = half_tables(total, retained, slab, basis, sent)
+    local_upper, local_lower = halves(local)
+    join_upper, join_lower = halves(join_table)
     axial_eigen = axial_eigenvalues.reshape(1, width)
     radial_eigen = radial_eigenvalues.reshape(own_modes, 1, radial)
 
+    def of_side(table):
+        return pl.BlockSpec((1,) + table.shape[1:], lambda i, p: (p[1], 0, 0))
+
     def encode(field):
-        steps = processors // 2
         return pl.pallas_call(
             functools.partial(encode_body, group=group, kept=kept),
-            grid=(steps,),
+            grid=(near,),
             in_specs=[
                 whole(spread_upper.shape),
                 whole(spread_lower.shape),
-                pl.BlockSpec((1, slab, 2 * group, width), lambda i: (field, 0, i, 0)),
+                pl.BlockSpec((1, slab, rows, width), lambda i: (field, 0, i, 0)),
             ],
-            out_specs=pl.BlockSpec((2, group * kept, width), lambda i: (i, 0, 0)),
-            out_shape=jax.ShapeDtypeStruct((processors, group * kept, width), BF16),
+            out_specs=pl.BlockSpec((1, rows * kept, width), lambda i: (i, 0, 0)),
+            out_shape=jax.ShapeDtypeStruct((near, rows * kept, width), BF16),
             compiler_params=params(),
+            cost_estimate=cost(7),
             name="window_coefficients",
         )(jnp.asarray(spread_upper), jnp.asarray(spread_lower), forcing)
 
-    def middle(field, received):
-        rows = 2
-        per_owner = 2 * own_modes
+    def gather(received):
+        step = 2
         return pl.pallas_call(
-            functools.partial(middle_body, kept=kept, rows=rows, gain=gain, field=field),
-            grid=(group // rows,),
-            in_specs=[
-                SMEM,
-                whole(table_upper.shape),
-                whole(table_lower.shape),
-                whole(axial_forward.shape),
-                pl.BlockSpec((processors, rows * kept, width), lambda i: (0, i, 0)),
+            functools.partial(gather_body, kept=kept, sent=sent, rows=step),
+            grid_spec=pltpu.PrefetchScalarGridSpec(
+                num_scalar_prefetch=1,
+                grid=(rows // step,),
+                in_specs=[
+                    of_side(local_upper),
+                    of_side(local_lower),
+                    pl.BlockSpec((near, step * kept, width), lambda i, _: (0, i, 0)),
+                ],
+                out_specs=[
+                    pl.BlockSpec((step, retained, width), lambda i, _: (i, 0, 0)),
+                    pl.BlockSpec((step * sent, width), lambda i, _: (i, 0)),
+                ],
+            ),
+            out_shape=[
+                jax.ShapeDtypeStruct((rows, retained, width), F32),
+                jax.ShapeDtypeStruct((rows * sent, width), BF16),
             ],
-            out_specs=pl.BlockSpec((devices, rows * per_owner, width), lambda i: (0, i, 0)),
-            out_shape=jax.ShapeDtypeStruct((devices, group * per_owner, width), BF16),
             compiler_params=params(),
+            cost_estimate=cost(5),
+            name="half_sums",
+        )(place, jnp.asarray(local_upper), jnp.asarray(local_lower), received)
+
+    def join(own, received):
+        step = 2
+        block = rows * per_owner
+        return pl.pallas_call(
+            functools.partial(join_body, sent=sent, rows=step),
+            grid_spec=pltpu.PrefetchScalarGridSpec(
+                num_scalar_prefetch=1,
+                grid=(rows // step,),
+                in_specs=[
+                    of_side(join_upper),
+                    of_side(join_lower),
+                    whole(axial_forward.shape),
+                    pl.BlockSpec((step, retained, width), lambda i, _: (i, 0, 0)),
+                    pl.BlockSpec((step * sent, width), lambda i, _: (i, 0)),
+                ],
+                out_specs=whole((owners, block + 16, width)),
+                scratch_shapes=[pltpu.VMEM((owners, block, width), F32)],
+            ),
+            out_shape=jax.ShapeDtypeStruct((owners, block + 16, width), BF16),
+            compiler_params=params(),
+            cost_estimate=cost(6),
             name="modal_axial_coefficients",
-        )(unit, jnp.asarray(table_upper), jnp.asarray(table_lower), axial_forward, received)
+        )(place, jnp.asarray(join_upper), jnp.asarray(join_lower), axial_forward, own, received)
 
     out_shape = jax.ShapeDtypeStruct((fields, own_modes * radial_devices, 2, radial_block, width), F32)
     out_block = (1, 1, 2, radial_block, width)
@@ -283,14 +351,13 @@
 
     def solve(field, received, out):
         carried = [] if out is None else [out]
-        first = 9
+        first = 8
         return pl.pallas_call(
-            functools.partial(solve_body, gain=gain, field=field, radial_devices=radial_devices),
+            functools.partial(solve_body, field=field, radial_devices=radial_devices),
             grid_spec=pltpu.PrefetchScalarGridSpec(
                 num_scalar_prefetch=1,
                 grid=(own_modes,),
                 in_specs=[
-                    SMEM,
                     SMEM,
                     whole(axial_eigen.shape),
                     pl.BlockSpec((1, 1, radial), lambda i, _: (i, 0, 0)),
@@ -305,16 +372,16 @@
                     pl.BlockSpec((1, send_rows, width), lambda i, _: (i, 0, 0)),
                 ],
                 scratch_shapes=[
-                    pltpu.VMEM((width // 128, received.shape[0] * received.shape[1], 128), F32)
+                    pltpu.VMEM((width // 128, radial * per_owner, 128), F32)
                 ],
             ),
             out_shape=[out_shape, jax.ShapeDtypeStruct((own_modes, send_rows, width), BF16)],
             input_output_aliases={first: 0} if carried else {},
             compiler_params=params(),
+            cost_estimate=cost(7),
             name="radial_solve",
         )(
             place,
-            unit,
             diffusion,
             axial_eigen,
             radial_eigen,
@@ -342,21 +409,35 @@
             out_shape=out_shape,
             input_output_aliases={2: 0},
             compiler_params=params(),
+            cost_estimate=cost(2),
             name="partner_rows",
         )(place, received, out)
 
-    def exchange(values, names):
-        return lax.all_to_all(values, names, split_axis=0, concat_axis=0, tiled=True)
-
-    windows = [exchange(encode(field), "modes") for field in range(fields)]
-    spectra = [exchange(middle(field, windows[field]), axes) for field in range(fields)]
-    out, sent = None, []
+    sides = [list(range(near)), list(range(near, processors))]
+    side_owners = [
+        [m * radial_devices + y for m in members for y in range(radial_devices)] for members in sides
+    ]
+
+    def exchange(values, names, groups):
+        return lax.all_to_all(
+            values, names, split_axis=0, concat_axis=0, tiled=True, axis_index_groups=groups
+        )
+
+    def across(values):
+        return lax.ppermute(values, "modes", [(i, (i + near) % processors) for i in range(processors)])
+
+    windows = [exchange(encode(field), "modes", sides) for field in range(fields)]
+    halves_of = [gather(windows[field]) for field in range(fields)]
+    spectra = [
+        exchange(join(own, across(send)), ("modes", "rad"), side_owners) for own, send in halves_of
+    ]
+    out, sent_rows = None, []
     for field in range(fields):
         out, send = solve(field, spectra[field], out)
-        sent.append(lax.ppermute(send, "rad", [(0, 1), (1, 0)]))
+        sent_rows.append(lax.ppermute(send, "rad", [(0, 1), (1, 0)]))
         if field:
-            out = finish(field - 1, sent[field - 1], out)
-    return finish(fields - 1, sent[fields - 1], out)
+            out = finish(field - 1, sent_rows[field - 1], out)
+    return finish(fields - 1, sent_rows[fields - 1], out)
 
 
 def azimuthal_tables(retained, points):
@@ -432,6 +513,7 @@
     own_modes = maps[2].shape[0]
     paired = (
         radial_devices == 2
+        and processors % 2 == 0
         and radial_block == 8 * processors
         and width % 128 == 0
         and own_modes == 4

time: 327 us -> 325 us (level)
  blocking collectives: 59.2 us -> 0 us
  Pallas kernels: 69.9 us -> 113 us
  waiting for transfers between devices: 126 us -> 156 us
  local copies, waits for them, and re-layouts: 26.8 us -> 10.4 us
  other arithmetic: 6.95 us -> 0.65 us
  starting transfers between devices: 35.2 us -> 40.7 us
    ppermute x3 -> x6, waiting for transfers between devices: 21.9 us -> 123 us  [the longest x3 103 us: across(): lax.ppermute(values, 'modes', [(i, (i + near) % processors) for i in rang...]
    all_to_all x6, waiting for transfers between devices: 104 us -> 33.2 us  [exchange(): lax.all_to_all(values, names, split_axis=0, concat_axis=0, tiled=True, ax...]
    pmax x1 -> x0, blocking collectives: 59.2 us -> none  [paired_plan(): unit = lax.pmax(largest, axes) * UNIT_PART]
    pallas_call x6 -> x9, Pallas kernels: 41.9 us -> 76.6 us  [the longest x3 27.5 us: join(): pl.pallas_call(functools.partial(join_body, sent=sent, rows=step), grid_s...]
    unnamed x68 -> x26, local copies, waits for them, and re-layouts: 26.8 us -> 9.82 us
    reduce_max x1 -> x0, other arithmetic: 6.94 us -> none  [paired_plan(): largest = jnp.max(jnp.abs(forcing), axis=(1, 2, 3)).astype(F32)]
    pallas_call x3, Pallas kernels: 6.56 us -> 12.1 us  [finish(): pl.pallas_call(finish_body, grid_spec=pltpu.PrefetchScalarGridSpec(num_sc...]
    all_to_all x6, starting transfers between devices: 33.7 us -> 38.8 us  [exchange(): lax.all_to_all(values, names, split_axis=0, concat_axis=0, tiled=True, ax...]
  transfers between devices with their start and end apart: 9 -> 12, of which waited for: 7 -> 7; matrix products, arithmetic and copies ran while one was open for 2% -> 0% of each run, Pallas kernels for 19% -> 31%
where the time goes in v2:
time: 325 us; the launch traced here: 322 us
  waiting for transfers between devices  156 us (48%)
  Pallas kernels  113 us (35%)
  starting transfers between devices  40.7 us (13%)
  local copies, waits for them, and re-layouts  10.4 us (3%)
    ppermute x3, waiting for transfers between devices, across(): lax.ppermute(values, 'modes', [(i, (i + near) % processors) for i in rang...  103 us
    all_to_all x6, starting transfers between devices, exchange(): lax.all_to_all(values, names, split_axis=0, concat_axis=0, tiled=True, ax...  38.8 us
    all_to_all x6, waiting for transfers between devices, exchange(): lax.all_to_all(values, names, split_axis=0, concat_axis=0, tiled=True, ax...  33.2 us
    pallas_call x3, Pallas kernels, join(): pl.pallas_call(functools.partial(join_body, sent=sent, rows=step), grid_s...  27.5 us
    pallas_call x3, Pallas kernels, encode(): pl.pallas_call(functools.partial(encode_body, group=group, kept=kept), gr...  24.8 us
    pallas_call x3, Pallas kernels, solve(): pl.pallas_call(functools.partial(solve_body, field=field, radial_devices=...  24.7 us
    pallas_call x3, Pallas kernels, gather(): pl.pallas_call(functools.partial(gather_body, kept=kept, sent=sent, rows=...  24.4 us
    ppermute x3, waiting for transfers between devices, paired_plan(): sent_rows.append(lax.ppermute(send, 'rad', [(0, 1), (1, 0)]))  20.6 us
  transfers between devices with their start and end apart: 12, of which 7 were waited for; matrix products, arithmetic and copies ran while one was open for 0% of the time, Pallas kernels for 31%

profile of v2, /device:TPU:17, one launch (start us, length us, event | category | flops | bytes accessed | tf_op | source)
XLA Modules:
  0.0 321.6 jit_solution(1545700272477946369)
XLA Ops:
  0.0 8.3 %window_coefficients.4 = bf16[8,512,256]{2,1,0:T(8,128)(2,1)} custom-call(bf16[256,512]{1,0:T(8,128)(2,1)} %constant.36.clone.upper_ref, bf16[256,512]{1,0:T(8,128)(2,1)} %constant.37.clone.lower_ref, bf16[3,64,128,256]{3,2,1,0:T(8,128)(2,1)} %forcing_ref.5), custom_call_target="tpu_custom_call" | custom-call | flops 2100000000 | bytes 21000000 | tf_op jit(solution)/shard_map/window_coefficients/pallas_call | solution.py:283
  8.3 4.4 %all-to-all-start.2 = ((bf16[8,512,256]{2,1,0:T(8,128)(2,1)}), bf16[8,512,256]{2,1,0:T(8,128)(2,1)S(1)}, u32[]{:S(2)}, u32[]{:S(2)}) async-start(bf16[8,512,256]{2,1,0:T(8,128)(2,1)} %window_coefficients.4), calls=%async_computation.2 | async-start | bytes 4194304 | tf_op jit(solution)/shard_map/all_to_all | solution.py:422
  12.7 8.2 %window_coefficients.5 = bf16[8,512,256]{2,1,0:T(8,128)(2,1)} custom-call(bf16[256,512]{1,0:T(8,128)(2,1)} %constant.36.clone.upper_ref, bf16[256,512]{1,0:T(8,128)(2,1)} %constant.37.clone.lower_ref, bf16[3,64,128,256]{3,2,1,0:T(8,128)(2,1)} %forcing_ref.5), custom_call_target="tpu_custom_call" | custom-call | flops 2100000000 | bytes 21000000 | tf_op jit(solution)/shard_map/window_coefficients/pallas_call | solution.py:283
  20.9 16.6 %all-to-all-done.2.in_ref = bf16[8,512,256]{2,1,0:T(8,128)(2,1)S(1)} async-done(((bf16[8,512,256]{2,1,0:T(8,128)(2,1)}), bf16[8,512,256]{2,1,0:T(8,128)(2,1)S(1)}, u32[]{:S(2)}, u32[]{:S(2)}) %all-to-all-start.2) | async-done | bytes 2097184 | tf_op jit(solution)/shard_map/all_to_all | solution.py:422
  37.5 1.3 copy-done.4
  38.9 4.4 %all-to-all-start.4 = ((bf16[8,512,256]{2,1,0:T(8,128)(2,1)}), bf16[8,512,256]{2,1,0:T(8,128)(2,1)S(1)}, u32[]{:S(2)}, u32[]{:S(2)}) async-start(bf16[8,512,256]{2,1,0:T(8,128)(2,1)} %window_coefficients.5), calls=%async_computation.4 | async-start | bytes 4194304 | tf_op jit(solution)/shard_map/all_to_all | solution.py:422
  43.3 8.3 %window_coefficients.3 = bf16[8,512,256]{2,1,0:T(8,128)(2,1)} custom-call(bf16[256,512]{1,0:T(8,128)(2,1)} %constant.36.clone.upper_ref, bf16[256,512]{1,0:T(8,128)(2,1)} %constant.37.clone.lower_ref, bf16[3,64,128,256]{3,2,1,0:T(8,128)(2,1)} %forcing_ref.5), custom_call_target="tpu_custom_call" | custom-call | flops 2100000000 | bytes 21000000 | tf_op jit(solution)/shard_map/window_coefficients/pallas_call | solution.py:283
  51.5 16.6 %all-to-all-done.4.in_ref = bf16[8,512,256]{2,1,0:T(8,128)(2,1)S(1)} async-done(((bf16[8,512,256]{2,1,0:T(8,128)(2,1)}), bf16[8,512,256]{2,1,0:T(8,128)(2,1)S(1)}, u32[]{:S(2)}, u32[]{:S(2)}) %all-to-all-start.4) | async-done | bytes 2097184 | tf_op jit(solution)/shard_map/all_to_all | solution.py:422
  68.1 1.4 copy-done.3
  69.5 4.4 %all-to-all-start = ((bf16[8,512,256]{2,1,0:T(8,128)(2,1)}), bf16[8,512,256]{2,1,0:T(8,128)(2,1)S(1)}, u32[]{:S(2)}, u32[]{:S(2)}) async-start(bf16[8,512,256]{2,1,0:T(8,128)(2,1)} %window_coefficients.3), calls=%async_computation | async-start | bytes 4194304 | tf_op jit(solution)/shard_map/all_to_all | solution.py:422
  73.8 0.6 pad_add_fusion._.place_ref
  74.5 8.2 %half_sums.4 = (f32[16,128,256]{2,1,0:T(8,128)}, bf16[1536,256]{1,0:T(8,128)(2,1)}) custom-call(s32[2]{0:T(128)} %pad_add_fusion._.place_ref, bf16[2,224,256]{2,1,0:T(8,128)(2,1)} %constant.38.clone.upper_ref, bf16[2,224,256]{2,1,0:T(8,128)(2,1)} %constant.39.clone.lower_ref, bf16[8,512,256]{2,1,0:T(8,128)(2,1)} %copy-done.4), custom_call_target="tpu_custom_call" | custom-call | flops 1500000000 | bytes 15000000 | tf_op jit(solution)/shard_map/half_sums/pallas_call | solution.py:300
  82.6 0.1 collective-permute-start.1
  82.7 34.1 %collective-permute-done.1.in_ref = bf16[1536,256]{1,0:T(8,128)(2,1)S(1)} collective-permute-done((bf16[1536,256]{1,0:T(8,128)(2,1)}, bf16[1536,256]{1,0:T(8,128)(2,1)S(1)}, u32[]{:S(2)}, u32[]{:S(2)}) %collective-permute-start.1) | collective-permute-done | bytes 786464 | tf_op jit(solution)/shard_map/ppermute | solution.py:427
  116.8 0.9 copy-done.11
  117.7 9.2 %modal_axial_coefficients.4 = bf16[16,144,256]{2,1,0:T(8,128)(2,1)} custom-call(s32[2]{0:T(128)} %pad_add_fusion._.place_ref, bf16[2,128,96]{2,1,0:T(8,128)(2,1)} %constant.40.clone.upper_ref, bf16[2,128,96]{2,1,0:T(8,128)(2,1)} %constant.41.clone.lower_ref, f32[256,256]{1,0:T(8,128)} %axial_ref.9, f32[16,128,256]{2,1,0:T(8,128)} %get-tuple-element.19.own_ref, ...), custom_call_target="tpu_custom_call" | custom-call | flops 1800000000 | bytes 18000000 | tf_op jit(solution)/shard_map/modal_axial_coefficients/pallas_call | solution.py:327
  126.9 0.0 all-to-all-done.in_ref
  126.9 8.6 %all-to-all-start.3 = ((bf16[16,144,256]{2,1,0:T(8,128)(2,1)}), bf16[16,144,256]{2,1,0:T(8,128)(2,1)S(1)}, u32[]{:S(2)}, u32[]{:S(2)}) async-start(bf16[16,144,256]{2,1,0:T(8,128)(2,1)} %modal_axial_coefficients.4), calls=%async_computation.3 | async-start | bytes 2359296 | tf_op jit(solution)/shard_map/all_to_all | solution.py:422
  135.5 8.1 %half_sums.5 = (f32[16,128,256]{2,1,0:T(8,128)}, bf16[1536,256]{1,0:T(8,128)(2,1)}) custom-call(s32[2]{0:T(128)} %pad_add_fusion._.place_ref, bf16[2,224,256]{2,1,0:T(8,128)(2,1)} %constant.38.clone.upper_ref, bf16[2,224,256]{2,1,0:T(8,128)(2,1)} %constant.39.clone.lower_ref, bf16[8,512,256]{2,1,0:T(8,128)(2,1)} %copy-done.3), custom_call_target="tpu_custom_call" | custom-call | flops 1500000000 | bytes 15000000 | tf_op jit(solution)/shard_map/half_sums/pallas_call | solution.py:300
  143.7 0.0 collective-permute-start.3
  143.7 34.3 %collective-permute-done.3.in_ref = bf16[1536,256]{1,0:T(8,128)(2,1)S(1)} collective-permute-done((bf16[1536,256]{1,0:T(8,128)(2,1)}, bf16[1536,256]{1,0:T(8,128)(2,1)S(1)}, u32[]{:S(2)}, u32[]{:S(2)}) %collective-permute-start.3) | collective-permute-done | bytes 786464 | tf_op jit(solution)/shard_map/ppermute | solution.py:427
  177.9 0.9 copy-done.12
  178.8 9.1 %modal_axial_coefficients.5 = bf16[16,144,256]{2,1,0:T(8,128)(2,1)} custom-call(s32[2]{0:T(128)} %pad_add_fusion._.place_ref, bf16[2,128,96]{2,1,0:T(8,128)(2,1)} %constant.40.clone.upper_ref, bf16[2,128,96]{2,1,0:T(8,128)(2,1)} %constant.41.clone.lower_ref, f32[256,256]{1,0:T(8,128)} %axial_ref.9, f32[16,128,256]{2,1,0:T(8,128)} %get-tuple-element.22.own_ref, ...), custom_call_target="tpu_custom_call" | custom-call | flops 1800000000 | bytes 18000000 | tf_op jit(solution)/shard_map/modal_axial_coefficients/pallas_call | solution.py:327
  188.0 1.0 copy-done.5
  189.0 8.5 %all-to-all-start.5 = ((bf16[16,144,256]{2,1,0:T(8,128)(2,1)}), bf16[16,144,256]{2,1,0:T(8,128)(2,1)S(1)}, u32[]{:S(2)}, u32[]{:S(2)}) async-start(bf16[16,144,256]{2,1,0:T(8,128)(2,1)} %modal_axial_coefficients.5), calls=%async_computation.5 | async-start | bytes 2359296 | tf_op jit(solution)/shard_map/all_to_all | solution.py:422
  197.4 8.1 %half_sums.3 = (f32[16,128,256]{2,1,0:T(8,128)}, bf16[1536,256]{1,0:T(8,128)(2,1)}) custom-call(s32[2]{0:T(128)} %pad_add_fusion._.place_ref, bf16[2,224,256]{2,1,0:T(8,128)(2,1)} %constant.38.clone.upper_ref, bf16[2,224,256]{2,1,0:T(8,128)(2,1)} %constant.39.clone.lower_ref, bf16[8,512,256]{2,1,0:T(8,128)(2,1)} %copy-done.2), custom_call_target="tpu_custom_call" | custom-call | flops 1500000000 | bytes 15000000 | tf_op jit(solution)/shard_map/half_sums/pallas_call | solution.py:300
  205.6 0.0 collective-permute-start
  205.6 34.3 %collective-permute-done.in_ref = bf16[1536,256]{1,0:T(8,128)(2,1)S(1)} collective-permute-done((bf16[1536,256]{1,0:T(8,128)(2,1)}, bf16[1536,256]{1,0:T(8,128)(2,1)S(1)}, u32[]{:S(2)}, u32[]{:S(2)}) %collective-permute-start) | collective-permute-done | bytes 786464 | tf_op jit(solution)/shard_map/ppermute | solution.py:427
  239.9 0.9 copy-done.10
  240.7 9.2 %modal_axial_coefficients.3 = bf16[16,144,256]{2,1,0:T(8,128)(2,1)} custom-call(s32[2]{0:T(128)} %pad_add_fusion._.place_ref, bf16[2,128,96]{2,1,0:T(8,128)(2,1)} %constant.40.clone.upper_ref, bf16[2,128,96]{2,1,0:T(8,128)(2,1)} %constant.41.clone.lower_ref, f32[256,256]{1,0:T(8,128)} %axial_ref.9, f32[16,128,256]{2,1,0:T(8,128)} %get-tuple-element.17.own_ref, ...), custom_call_target="tpu_custom_call" | custom-call | flops 1800000000 | bytes 18000000 | tf_op jit(solution)/shard_map/modal_axial_coefficients/pallas_call | solution.py:327
  249.9 8.5 %all-to-all-start.1 = ((bf16[16,144,256]{2,1,0:T(8,128)(2,1)}), bf16[16,144,256]{2,1,0:T(8,128)(2,1)S(1)}, u32[]{:S(2)}, u32[]{:S(2)}) async-start(bf16[16,144,256]{2,1,0:T(8,128)(2,1)} %modal_axial_coefficients.3), calls=%async_computation.1 | async-start | bytes 2359296 | tf_op jit(solution)/shard_map/all_to_all | solution.py:422
  258.4 0.6 reshape.7.radial_eigen_ref
  259.0 8.2 %radial_solve.3 = (f32[3,8,2,128,256]{4,3,2,1,0:T(8,128)}, bf16[4,272,256]{2,1,0:T(8,128)(2,1)}) custom-call(s32[2]{0:T(128)} %pad_add_fusion._.place_ref, f32[3]{0:T(128)} %diffusion_ref.5, f32[1,256]{1,0:T(1,128)} %bitcast.3, f32[4,1,256]{2,1,0:T(1,128)} %reshape.7.radial_eigen_ref, f32[256,256]{1,0:T(8,128)} %axial_ref.11, f32[4,256,256]{2,1,0:T(8,128)} %forward_ref.5, ...), custom_call_target="tpu_custom_call" | custom-call | flops 2100000000 | bytes 21000000 | tf_op jit(solution)/shard_map/radial_solve/pallas_call | solution.py:355
  267.2 1.4 collective-permute-start.2
  268.7 8.2 %radial_solve.4 = (f32[3,8,2,128,256]{4,3,2,1,0:T(8,128)}, bf16[4,272,256]{2,1,0:T(8,128)(2,1)}) custom-call(s32[2]{0:T(128)} %pad_add_fusion._.place_ref, f32[3]{0:T(128)} %diffusion_ref.5, f32[1,256]{1,0:T(1,128)} %bitcast.4, f32[4,1,256]{2,1,0:T(1,128)} %reshape.7.radial_eigen_ref, f32[256,256]{1,0:T(8,128)} %axial_ref.11, ...), custom_call_target="tpu_custom_call", output_to_operand_aliasing={{0}: (8, {})} | custom-call | flops 2100000000 | bytes 21000000 | tf_op jit(solution)/shard_map/radial_solve/pallas_call | solution.py:355
  276.9 0.1 collective-permute-start.5
  277.0 11.8 %collective-permute-done.2.in_ref = bf16[4,272,256]{2,1,0:T(8,128)(2,1)S(1)} collective-permute-done((bf16[4,272,256]{2,1,0:T(8,128)(2,1)}, bf16[4,272,256]{2,1,0:T(8,128)(2,1)S(1)}, u32[]{:S(2)}, u32[]{:S(2)}) %collective-permute-start.2) | collective-permute-done | bytes 557088 | tf_op jit(solution)/shard_map/ppermute | solution.py:437
  288.8 0.8 copy-done.7
  289.6 4.0 %partner_rows.3.rest_0_ = f32[3,8,2,128,256]{4,3,2,1,0:T(8,128)} custom-call(s32[2]{0:T(128)} %pad_add_fusion._.place_ref, bf16[4,272,256]{2,1,0:T(8,128)(2,1)} %copy-done.7, f32[3,8,2,128,256]{4,3,2,1,0:T(8,128)} %get-tuple-element.25._), custom_call_target="tpu_custom_call", output_to_operand_aliasing={{}: (2, {})} | custom-call | flops 600000000 | bytes 6000000 | tf_op jit(solution)/shard_map/partner_rows/pallas_call | solution.py:396
  293.6 1.0 copy-done.1
  294.6 8.2 %radial_solve.5 = (f32[3,8,2,128,256]{4,3,2,1,0:T(8,128)}, bf16[4,272,256]{2,1,0:T(8,128)(2,1)}) custom-call(s32[2]{0:T(128)} %pad_add_fusion._.place_ref, f32[3]{0:T(128)} %diffusion_ref.5, f32[1,256]{1,0:T(1,128)} %bitcast.5, f32[4,1,256]{2,1,0:T(1,128)} %reshape.7.radial_eigen_ref, f32[256,256]{1,0:T(8,128)} %axial_ref.11, ...), custom_call_target="tpu_custom_call", output_to_operand_aliasing={{0}: (8, {})} | custom-call | flops 2100000000 | bytes 21000000 | tf_op jit(solution)/shard_map/radial_solve/pallas_call | solution.py:355
  302.9 0.2 collective-permute-start.4
  303.1 0.0 collective-permute-done.5.in_ref
  303.1 0.8 copy-done.6
  304.0 4.0 %partner_rows.4._ = f32[3,8,2,128,256]{4,3,2,1,0:T(8,128)} custom-call(s32[2]{0:T(128)} %pad_add_fusion._.place_ref, bf16[4,272,256]{2,1,0:T(8,128)(2,1)} %copy-done.6, f32[3,8,2,128,256]{4,3,2,1,0:T(8,128)} %get-tuple-element.28._), custom_call_target="tpu_custom_call", output_to_operand_aliasing={{}: (2, {})} | custom-call | flops 600000000 | bytes 6000000 | tf_op jit(solution)/shard_map/partner_rows/pallas_call | solution.py:396
  308.0 8.8 %collective-permute-done.4.in_ref = bf16[4,272,256]{2,1,0:T(8,128)(2,1)S(1)} collective-permute-done((bf16[4,272,256]{2,1,0:T(8,128)(2,1)}, bf16[4,272,256]{2,1,0:T(8,128)(2,1)S(1)}, u32[]{:S(2)}, u32[]{:S(2)}) %collective-permute-start.4) | collective-permute-done | bytes 557088 | tf_op jit(solution)/shard_map/ppermute | solution.py:437
  316.8 0.8 copy-done.8
  317.6 4.0 %partner_rows.5 = f32[3,8,2,128,256]{4,3,2,1,0:T(8,128)} custom-call(s32[2]{0:T(128)} %pad_add_fusion._.place_ref, bf16[4,272,256]{2,1,0:T(8,128)(2,1)} %copy-done.8, f32[3,8,2,128,256]{4,3,2,1,0:T(8,128)} %partner_rows.4._), custom_call_target="tpu_custom_call", output_to_operand_aliasing={{}: (2, {})} | custom-call | flops 600000000 | bytes 6000000 | tf_op jit(solution)/shard_map/partner_rows/pallas_call | solution.py:396
  (19 shorter events, 0.0 us)
Async XLA Ops:
  8.3 29.3 %all-to-all-start.2 = ((bf16[8,512,256]{2,1,0:T(8,128)(2,1)}), bf16[8,512,256]{2,1,0:T(8,128)(2,1)S(1)}, u32[]{:S(2)}, u32[]{:S(2)}) async-start(bf16[8,512,256]{2,1,0:T(8,128)(2,1)} %window_coefficients.4), calls=%async_computation.2 | async-start | bytes 4194304 | tf_op jit(solution)/shard_map/all_to_all | solution.py:422
  37.5 1.3 copy-start.4
  38.9 29.2 %all-to-all-start.4 = ((bf16[8,512,256]{2,1,0:T(8,128)(2,1)}), bf16[8,512,256]{2,1,0:T(8,128)(2,1)S(1)}, u32[]{:S(2)}, u32[]{:S(2)}) async-start(bf16[8,512,256]{2,1,0:T(8,128)(2,1)} %window_coefficients.5), calls=%async_computation.4 | async-start | bytes 4194304 | tf_op jit(solution)/shard_map/all_to_all | solution.py:422
  68.1 1.4 copy-start.3
  69.5 57.4 %all-to-all-start = ((bf16[8,512,256]{2,1,0:T(8,128)(2,1)}), bf16[8,512,256]{2,1,0:T(8,128)(2,1)S(1)}, u32[]{:S(2)}, u32[]{:S(2)}) async-start(bf16[8,512,256]{2,1,0:T(8,128)(2,1)} %window_coefficients.3), calls=%async_computation | async-start | bytes 4194304 | tf_op jit(solution)/shard_map/all_to_all | solution.py:422
  82.6 34.2 %collective-permute-start.1 = (bf16[1536,256]{1,0:T(8,128)(2,1)}, bf16[1536,256]{1,0:T(8,128)(2,1)S(1)}, u32[]{:S(2)}, u32[]{:S(2)}) collective-permute-start(bf16[1536,256]{1,0:T(8,128)(2,1)} %get-tuple-element.20), channel_id=1, source_target_pairs={{0,16},{2,18},{4,20},{6,22},{8,24},{10,26},{12,28},{14,30},{16,0},... | collective-permute-start | bytes 2359304 | tf_op jit(solution)/shard_map/ppermute | solution.py:427
  116.8 0.9 copy-start.11
  126.9 16.8 %copy-start.2 = (bf16[8,512,256]{2,1,0:T(8,128)(2,1)}, bf16[8,512,256]{2,1,0:T(8,128)(2,1)S(1)}, u32[]{:S(2)}) copy-start(bf16[8,512,256]{2,1,0:T(8,128)(2,1)S(1)} %all-to-all-done.in_ref) | copy-start | bytes 6291460
  126.9 61.1 %all-to-all-start.3 = ((bf16[16,144,256]{2,1,0:T(8,128)(2,1)}), bf16[16,144,256]{2,1,0:T(8,128)(2,1)S(1)}, u32[]{:S(2)}, u32[]{:S(2)}) async-start(bf16[16,144,256]{2,1,0:T(8,128)(2,1)} %modal_axial_coefficients.4), calls=%async_computation.3 | async-start | bytes 2359296 | tf_op jit(solution)/shard_map/all_to_all | solution.py:422
  143.7 34.3 %collective-permute-start.3 = (bf16[1536,256]{1,0:T(8,128)(2,1)}, bf16[1536,256]{1,0:T(8,128)(2,1)S(1)}, u32[]{:S(2)}, u32[]{:S(2)}) collective-permute-start(bf16[1536,256]{1,0:T(8,128)(2,1)} %get-tuple-element.23), channel_id=1, source_target_pairs={{0,16},{2,18},{4,20},{6,22},{8,24},{10,26},{12,28},{14,30},{16,0},... | collective-permute-start | bytes 2359304 | tf_op jit(solution)/shard_map/ppermute | solution.py:427
  177.9 0.9 copy-start.12
  188.0 1.0 copy-start.5
  189.0 60.9 %all-to-all-start.5 = ((bf16[16,144,256]{2,1,0:T(8,128)(2,1)}), bf16[16,144,256]{2,1,0:T(8,128)(2,1)S(1)}, u32[]{:S(2)}, u32[]{:S(2)}) async-start(bf16[16,144,256]{2,1,0:T(8,128)(2,1)} %modal_axial_coefficients.5), calls=%async_computation.5 | async-start | bytes 2359296 | tf_op jit(solution)/shard_map/all_to_all | solution.py:422
  205.6 34.3 %collective-permute-start = (bf16[1536,256]{1,0:T(8,128)(2,1)}, bf16[1536,256]{1,0:T(8,128)(2,1)S(1)}, u32[]{:S(2)}, u32[]{:S(2)}) collective-permute-start(bf16[1536,256]{1,0:T(8,128)(2,1)} %get-tuple-element.18), channel_id=1, source_target_pairs={{0,16},{2,18},{4,20},{6,22},{8,24},{10,26},{12,28},{14,30},{16,0},... | collective-permute-start | bytes 2359304 | tf_op jit(solution)/shard_map/ppermute | solution.py:427
  239.9 0.9 copy-start.10
  249.9 8.5 %copy-start.9 = (f32[4,256]{1,0:T(4,128)S(1)}, f32[4,256]{1,0:T(4,128)}, u32[]{:S(2)}) copy-start(f32[4,256]{1,0:T(4,128)} %param.21) | copy-start | bytes 12292
  249.9 17.3 %copy-start = (bf16[16,144,256]{2,1,0:T(8,128)(2,1)}, bf16[16,144,256]{2,1,0:T(8,128)(2,1)S(1)}, u32[]{:S(2)}) copy-start(bf16[16,144,256]{2,1,0:T(8,128)(2,1)S(1)} %all-to-all-done.5.in_ref) | copy-start | bytes 3538948
  249.9 43.7 %all-to-all-start.1 = ((bf16[16,144,256]{2,1,0:T(8,128)(2,1)}), bf16[16,144,256]{2,1,0:T(8,128)(2,1)S(1)}, u32[]{:S(2)}, u32[]{:S(2)}) async-start(bf16[16,144,256]{2,1,0:T(8,128)(2,1)} %modal_axial_coefficients.3), calls=%async_computation.1 | async-start | bytes 2359296 | tf_op jit(solution)/shard_map/all_to_all | solution.py:422
  267.2 21.6 %collective-permute-start.2 = (bf16[4,272,256]{2,1,0:T(8,128)(2,1)}, bf16[4,272,256]{2,1,0:T(8,128)(2,1)S(1)}, u32[]{:S(2)}, u32[]{:S(2)}) collective-permute-start(bf16[4,272,256]{2,1,0:T(8,128)(2,1)} %get-tuple-element.21), channel_id=1, source_target_pairs={{0,1},{1,0},{2,3},{3,2},{4,5},{5,4},{6,7},{7,6},{8,9},{9,8},{10,11... | collective-permute-start | bytes 1671176 | tf_op jit(solution)/shard_map/ppermute | solution.py:437
  276.9 26.2 %collective-permute-start.5 = (bf16[4,272,256]{2,1,0:T(8,128)(2,1)}, bf16[4,272,256]{2,1,0:T(8,128)(2,1)S(1)}, u32[]{:S(2)}, u32[]{:S(2)}) collective-permute-start(bf16[4,272,256]{2,1,0:T(8,128)(2,1)} %get-tuple-element.27), channel_id=1, source_target_pairs={{0,1},{1,0},{2,3},{3,2},{4,5},{5,4},{6,7},{7,6},{8,9},{9,8},{10,11... | collective-permute-start | bytes 1671176 | tf_op jit(solution)/shard_map/ppermute | solution.py:437
  288.8 0.8 copy-start.7
  293.6 1.0 copy-start.1
  302.9 13.9 %collective-permute-start.4 = (bf16[4,272,256]{2,1,0:T(8,128)(2,1)}, bf16[4,272,256]{2,1,0:T(8,128)(2,1)S(1)}, u32[]{:S(2)}, u32[]{:S(2)}) collective-permute-start(bf16[4,272,256]{2,1,0:T(8,128)(2,1)} %get-tuple-element.26), channel_id=1, source_target_pairs={{0,1},{1,0},{2,3},{3,2},{4,5},{5,4},{6,7},{7,6},{8,9},{9,8},{10,11... | collective-permute-start | bytes 1671176 | tf_op jit(solution)/shard_map/ppermute | solution.py:437
  303.1 0.8 copy-start.6
  316.8 0.8 copy-start.8

commit v3 on v2

--- a/solution.py
+++ b/solution.py
@@ -111,7 +111,7 @@
     return jnp.where(place == kept - 1, 0.0, values)
 
 
-def encode_body(upper_ref, lower_ref, forcing_ref, out_ref, *, group, kept):
+def encode_body(upper_ref, lower_ref, forcing_ref, _, out_ref, *, group, kept):
     points, rows, width = forcing_ref.shape[1:]
     block = forcing_ref[0].astype(F32)
     for part in range(rows // group):
@@ -124,7 +124,7 @@
         out_ref[0, place : place + group * kept, :] = coded.reshape(group * kept, width).astype(BF16)
 
 
-def gather_body(_, upper_ref, lower_ref, in_ref, own_ref, send_ref, *, kept, sent, rows):
+def gather_body(_, upper_ref, lower_ref, in_ref, __, own_ref, send_ref, *, kept, sent, rows):
     sources, _, width = in_ref.shape
     table = (upper_ref[0], lower_ref[0])
     own = own_ref.shape[1]
@@ -136,7 +136,9 @@
         send_ref[row * sent : (row + 1) * sent, :] = encode_columns(sums[None, own:], sent)[0].astype(BF16)
 
 
-def join_body(_, upper_ref, lower_ref, axial_ref, own_ref, in_ref, out_ref, held_ref, *, sent, rows):
+def join_body(
+    _, upper_ref, lower_ref, axial_ref, own_ref, in_ref, __, out_ref, held_ref, *, sent, rows
+):
     step = pl.program_id(0)
     width = in_ref.shape[1]
     owners, coded_rows = out_ref.shape[:2]
@@ -215,7 +217,7 @@
     send_ref[0, radial:, :] = jnp.broadcast_to(scale, (16, width)).astype(BF16)
 
 
-def finish_body(place_ref, in_ref, _, out_ref):
+def finish_body(place_ref, in_ref, _, __, out_ref):
     radial, width = out_ref.shape[2] * out_ref.shape[3], out_ref.shape[4]
     coded = in_ref[0].astype(F32)
     values = linear_decode(coded[:radial], coded[radial : radial + 1])
@@ -230,7 +232,7 @@
 
 def cost(microseconds):
     return pl.CostEstimate(
-        flops=int(microseconds * 3e8), bytes_accessed=int(microseconds * 3e6), transcendentals=0
+        flops=int(microseconds * 3e10), bytes_accessed=int(microseconds * 3e8), transcendentals=0
     )
 
 
@@ -239,6 +241,7 @@
 
 
 SMEM = pl.BlockSpec(memory_space=pltpu.SMEM)
+ANY = pl.BlockSpec(memory_space=pl.ANY)
 
 
 def paired_plan(
@@ -279,7 +282,7 @@
     def of_side(table):
         return pl.BlockSpec((1,) + table.shape[1:], lambda i, p: (p[1], 0, 0))
 
-    def encode(field):
+    def encode(field, after):
         return pl.pallas_call(
             functools.partial(encode_body, group=group, kept=kept),
             grid=(near,),
@@ -287,16 +290,17 @@
                 whole(spread_upper.shape),
                 whole(spread_lower.shape),
                 pl.BlockSpec((1, slab, rows, width), lambda i: (field, 0, i, 0)),
+                ANY,
             ],
             out_specs=pl.BlockSpec((1, rows * kept, width), lambda i: (i, 0, 0)),
             out_shape=jax.ShapeDtypeStruct((near, rows * kept, width), BF16),
             compiler_params=params(),
             cost_estimate=cost(7),
             name="window_coefficients",
-        )(jnp.asarray(spread_upper), jnp.asarray(spread_lower), forcing)
-
-    def gather(received):
-        step = 2
+        )(jnp.asarray(spread_upper), jnp.asarray(spread_lower), forcing, after)
+
+    def gather(received, after):
+        step = 4
         return pl.pallas_call(
             functools.partial(gather_body, kept=kept, sent=sent, rows=step),
             grid_spec=pltpu.PrefetchScalarGridSpec(
@@ -306,6 +310,7 @@
                     of_side(local_upper),
                     of_side(local_lower),
                     pl.BlockSpec((near, step * kept, width), lambda i, _: (0, i, 0)),
+                    ANY,
                 ],
                 out_specs=[
                     pl.BlockSpec((step, retained, width), lambda i, _: (i, 0, 0)),
@@ -319,10 +324,10 @@
             compiler_params=params(),
             cost_estimate=cost(5),
             name="half_sums",
-        )(place, jnp.asarray(local_upper), jnp.asarray(local_lower), received)
-
-    def join(own, received):
-        step = 2
+        )(place, jnp.asarray(local_upper), jnp.asarray(local_lower), received, after)
+
+    def join(own, received, after):
+        step = 4
         block = rows * per_owner
         return pl.pallas_call(
             functools.partial(join_body, sent=sent, rows=step),
@@ -335,6 +340,7 @@
                     whole(axial_forward.shape),
                     pl.BlockSpec((step, retained, width), lambda i, _: (i, 0, 0)),
                     pl.BlockSpec((step * sent, width), lambda i, _: (i, 0)),
+                    ANY,
                 ],
                 out_specs=whole((owners, block + 16, width)),
                 scratch_shapes=[pltpu.VMEM((owners, block, width), F32)],
@@ -343,15 +349,15 @@
             compiler_params=params(),
             cost_estimate=cost(6),
             name="modal_axial_coefficients",
-        )(place, jnp.asarray(join_upper), jnp.asarray(join_lower), axial_forward, own, received)
+        )(place, jnp.asarray(join_upper), jnp.asarray(join_lower), axial_forward, own, received, after)
 
     out_shape = jax.ShapeDtypeStruct((fields, own_modes * radial_devices, 2, radial_block, width), F32)
     out_block = (1, 1, 2, radial_block, width)
     send_rows = radial + 16
 
-    def solve(field, received, out):
+    def solve(field, received, out, after):
         carried = [] if out is None else [out]
-        first = 8
+        first = 9
         return pl.pallas_call(
             functools.partial(solve_body, field=field, radial_devices=radial_devices),
             grid_spec=pltpu.PrefetchScalarGridSpec(
@@ -366,7 +372,7 @@
                     pl.BlockSpec((1, radial, radial), lambda i, _: (i, 0, 0)),
                     whole(received.shape),
                 ]
-                + [pl.BlockSpec(memory_space=pl.ANY) for _ in carried],
+                + [ANY] * (1 + len(carried)),
                 out_specs=[
                     pl.BlockSpec(out_block, lambda i, y: (field, y[0] * own_modes + i, 0, 0, 0)),
                     pl.BlockSpec((1, send_rows, width), lambda i, _: (i, 0, 0)),
@@ -389,10 +395,11 @@
             radial_forward,
             radial_backward,
             received,
+            after,
             *carried,
         )
 
-    def finish(field, received, out):
+    def finish(field, received, out, after):
         return pl.pallas_call(
             finish_body,
             grid_spec=pltpu.PrefetchScalarGridSpec(
@@ -400,7 +407,8 @@
                 grid=(own_modes,),
                 in_specs=[
                     pl.BlockSpec((1, send_rows, width), lambda i, _: (i, 0, 0)),
-                    pl.BlockSpec(memory_space=pl.ANY),
+                    ANY,
+                    ANY,
                 ],
                 out_specs=pl.BlockSpec(
                     out_block, lambda i, y: (field, (1 - y[0]) * own_modes + i, 0, 0, 0)
@@ -411,7 +419,7 @@
             compiler_params=params(),
             cost_estimate=cost(2),
             name="partner_rows",
-        )(place, received, out)
+        )(place, received, out, after)
 
     sides = [list(range(near)), list(range(near, processors))]
     side_owners = [
@@ -426,18 +434,33 @@
     def across(values):
         return lax.ppermute(values, "modes", [(i, (i + near) % processors) for i in range(processors)])
 
-    windows = [exchange(encode(field), "modes", sides) for field in range(fields)]
-    halves_of = [gather(windows[field]) for field in range(fields)]
-    spectra = [
-        exchange(join(own, across(send)), ("modes", "rad"), side_owners) for own, send in halves_of
-    ]
-    out, sent_rows = None, []
-    for field in range(fields):
-        out, send = solve(field, spectra[field], out)
-        sent_rows.append(lax.ppermute(send, "rad", [(0, 1), (1, 0)]))
-        if field:
-            out = finish(field - 1, sent_rows[field - 1], out)
-    return finish(fields - 1, sent_rows[fields - 1], out)
+    def partner(values):
+        return lax.ppermute(values, "rad", [(0, 1), (1, 0)])
+
+    windows, own, away, spectra, partners = {}, {}, {}, {}, {}
+    last, out = diffusion, None
+    steps = (
+        ["e0", "e1", "h0", "e2", "h1"]
+        + ["j0", "h2", "j1", "s0", "j2"]
+        + ["s1", "f0", "s2", "f1", "f2"]
+    )
+    for step in steps:
+        field = int(step[1])
+        if step[0] == "e":
+            last = encode(field, last)
+            windows[field] = exchange(last, "modes", sides)
+        elif step[0] == "h":
+            own[field], last = gather(windows[field], last)
+            away[field] = across(last)
+        elif step[0] == "j":
+            last = join(own[field], away[field], last)
+            spectra[field] = exchange(last, ("modes", "rad"), side_owners)
+        elif step[0] == "s":
+            out, last = solve(field, spectra[field], out, last)
+            partners[field] = partner(last)
+        else:
+            out = finish(field, partners[field], out, last)
+    return out
 
 
 def azimuthal_tables(retained, points):

time: 325 us -> 243 us (0.75)
  waiting for transfers between devices: 156 us -> 89.9 us
  Pallas kernels: 113 us -> 102 us
  local copies, waits for them, and re-layouts: 10.4 us -> 1.41 us
  starting transfers between devices: 40.7 us -> 44.9 us
    ppermute x3, waiting for transfers between devices: 103 us -> 4.41 us  [across(): lax.ppermute(values, 'modes', [(i, (i + near) % processors) for i in rang...]
    all_to_all x6, waiting for transfers between devices: 33.2 us -> 74.2 us  [exchange(): lax.all_to_all(values, names, split_axis=0, concat_axis=0, tiled=True, ax...]
    ppermute x3, waiting for transfers between devices: 20.6 us -> 11.2 us  [partner(): return lax.ppermute(values, 'rad', [(0, 1), (1, 0)])]
    unnamed x26 -> x4, local copies, waits for them, and re-layouts: 9.82 us -> 0.82 us
    pallas_call x3, Pallas kernels: 24.4 us -> 18 us  [gather(): pl.pallas_call(functools.partial(gather_body, kept=kept, sent=sent, rows=...]
    pallas_call x3, Pallas kernels: 27.5 us -> 22 us  [join(): pl.pallas_call(functools.partial(join_body, sent=sent, rows=step), grid_s...]
    ppermute x3, starting transfers between devices: 0.1 us -> 5.35 us  [across(): lax.ppermute(values, 'modes', [(i, (i + near) % processors) for i in rang...]
  transfers between devices with their start and end apart: 12 -> 12, of which waited for: 7 -> 9; matrix products, arithmetic and copies ran while one was open for 0% -> 1% of each run, Pallas kernels for 31% -> 37%
where the time goes in v3:
time: 243 us; the launch traced here: 238 us
  Pallas kernels  102 us (42%)
  waiting for transfers between devices  89.9 us (37%)
  starting transfers between devices  44.9 us (18%)
    all_to_all x6, waiting for transfers between devices, exchange(): lax.all_to_all(values, names, split_axis=0, concat_axis=0, tiled=True, ax...  74.2 us
    all_to_all x6, starting transfers between devices, exchange(): lax.all_to_all(values, names, split_axis=0, concat_axis=0, tiled=True, ax...  36.4 us
    pallas_call x3, Pallas kernels, encode(): pl.pallas_call(functools.partial(encode_body, group=group, kept=kept), gr...  24.8 us
    pallas_call x3, Pallas kernels, solve(): pl.pallas_call(functools.partial(solve_body, field=field, radial_devices=...  24.7 us
    pallas_call x3, Pallas kernels, join(): pl.pallas_call(functools.partial(join_body, sent=sent, rows=step), grid_s...  22 us
    pallas_call x3, Pallas kernels, gather(): pl.pallas_call(functools.partial(gather_body, kept=kept, sent=sent, rows=...  18 us
    pallas_call x3, Pallas kernels, finish(): pl.pallas_call(finish_body, grid_spec=pltpu.PrefetchScalarGridSpec(num_sc...  12.1 us
    ppermute x3, waiting for transfers between devices, partner(): return lax.ppermute(values, 'rad', [(0, 1), (1, 0)])  11.2 us
  transfers between devices with their start and end apart: 12, of which 9 were waited for; matrix products, arithmetic and copies ran while one was open for 1% of the time, Pallas kernels for 37%

profile of v3, /device:TPU:17, one launch (start us, length us, event | category | flops | bytes accessed | tf_op | source)
XLA Modules:
  0.0 238.4 jit_solution(17475673703758127408)
XLA Ops:
  0.0 8.3 %window_coefficients.3._ = bf16[8,512,256]{2,1,0:T(8,128)(2,1)} custom-call(bf16[256,512]{1,0:T(8,128)(2,1)} %constant.36.clone.upper_ref, bf16[256,512]{1,0:T(8,128)(2,1)} %constant.37.clone.lower_ref, bf16[3,64,128,256]{3,2,1,0:T(8,128)(2,1)} %forcing_ref.5, f32[3]{0:T(128)} %diffusion_ref.5), custom_call_target="tpu_custom_call" | custom-call | flops 210000003072 | bytes 2100000000 | tf_op jit(solution)/shard_map/window_coefficients/pallas_call | solution.py:286
  8.3 4.9 %all-to-all-start = ((bf16[8,512,256]{2,1,0:T(8,128)(2,1)}), bf16[8,512,256]{2,1,0:T(8,128)(2,1)}, u32[]{:S(2)}, u32[]{:S(2)}) async-start(bf16[8,512,256]{2,1,0:T(8,128)(2,1)} %window_coefficients.3._), calls=%async_computation | async-start | bytes 4194304 | tf_op jit(solution)/shard_map/all_to_all | solution.py:430
  13.2 0.0 copy-start
  13.2 8.3 %window_coefficients.4.__ = bf16[8,512,256]{2,1,0:T(8,128)(2,1)} custom-call(bf16[256,512]{1,0:T(8,128)(2,1)} %constant.36.clone.upper_ref, bf16[256,512]{1,0:T(8,128)(2,1)} %constant.37.clone.lower_ref, bf16[3,64,128,256]{3,2,1,0:T(8,128)(2,1)} %forcing_ref.5, bf16[8,512,256]{2,1,0:T(8,128)(2,1)} %window_coefficients.3._), custom_call_target="tpu_custom_call" | custom-call | flops 210000003072 | bytes 2100000000 | tf_op jit(solution)/shard_map/window_coefficients/pallas_call | solution.py:286
  21.4 0.0 copy-done
  21.4 0.6 reshape.7.radial_eigen_ref
  22.0 0.7 pad_add_fusion._.place_ref
  22.7 15.4 %all-to-all-done.in_ref = bf16[8,512,256]{2,1,0:T(8,128)(2,1)} async-done(((bf16[8,512,256]{2,1,0:T(8,128)(2,1)}), bf16[8,512,256]{2,1,0:T(8,128)(2,1)}, u32[]{:S(2)}, u32[]{:S(2)}) %all-to-all-start) | async-done | bytes 2097184 | tf_op jit(solution)/shard_map/all_to_all | solution.py:430
  38.1 5.1 %all-to-all-start.2 = ((bf16[8,512,256]{2,1,0:T(8,128)(2,1)}), bf16[8,512,256]{2,1,0:T(8,128)(2,1)}, u32[]{:S(2)}, u32[]{:S(2)}) async-start(bf16[8,512,256]{2,1,0:T(8,128)(2,1)} %window_coefficients.4.__), calls=%async_computation.2 | async-start | bytes 4194304 | tf_op jit(solution)/shard_map/all_to_all | solution.py:430
  43.2 6.0 %half_sums.3 = (f32[16,128,256]{2,1,0:T(8,128)}, bf16[1536,256]{1,0:T(8,128)(2,1)}) custom-call(s32[2]{0:T(128)} %pad_add_fusion._.place_ref, bf16[2,224,256]{2,1,0:T(8,128)(2,1)} %constant.38.clone.upper_ref, bf16[2,224,256]{2,1,0:T(8,128)(2,1)} %constant.39.clone.lower_ref, bf16[8,512,256]{2,1,0:T(8,128)(2,1)} %all-to-all-done.in_ref, ...), custom_call_target="tpu_custom_call" | custom-call | flops 149999992832 | bytes 1500000000 | tf_op jit(solution)/shard_map/half_sums/pallas_call | solution.py:304
  49.2 0.0 collective-permute-start
  49.2 8.3 %window_coefficients.5.__ = bf16[8,512,256]{2,1,0:T(8,128)(2,1)} custom-call(bf16[256,512]{1,0:T(8,128)(2,1)} %constant.36.clone.upper_ref, bf16[256,512]{1,0:T(8,128)(2,1)} %constant.37.clone.lower_ref, bf16[3,64,128,256]{3,2,1,0:T(8,128)(2,1)} %forcing_ref.5, bf16[1536,256]{1,0:T(8,128)(2,1)} %get-tuple-element.17._), custom_call_target="tpu_custom_call" | custom-call | flops 210000003072 | bytes 2100000000 | tf_op jit(solution)/shard_map/window_coefficients/pallas_call | solution.py:286
  57.5 22.5 %all-to-all-done.2.in_ref = bf16[8,512,256]{2,1,0:T(8,128)(2,1)} async-done(((bf16[8,512,256]{2,1,0:T(8,128)(2,1)}), bf16[8,512,256]{2,1,0:T(8,128)(2,1)}, u32[]{:S(2)}, u32[]{:S(2)}) %all-to-all-start.2) | async-done | bytes 2097184 | tf_op jit(solution)/shard_map/all_to_all | solution.py:430
  79.9 5.6 %all-to-all-start.1 = ((bf16[8,512,256]{2,1,0:T(8,128)(2,1)}), bf16[8,512,256]{2,1,0:T(8,128)(2,1)}, u32[]{:S(2)}, u32[]{:S(2)}) async-start(bf16[8,512,256]{2,1,0:T(8,128)(2,1)} %window_coefficients.5.__), calls=%async_computation.1 | async-start | bytes 4194304 | tf_op jit(solution)/shard_map/all_to_all | solution.py:430
  85.5 6.0 %half_sums.4 = (f32[16,128,256]{2,1,0:T(8,128)}, bf16[1536,256]{1,0:T(8,128)(2,1)}) custom-call(s32[2]{0:T(128)} %pad_add_fusion._.place_ref, bf16[2,224,256]{2,1,0:T(8,128)(2,1)} %constant.38.clone.upper_ref, bf16[2,224,256]{2,1,0:T(8,128)(2,1)} %constant.39.clone.lower_ref, bf16[8,512,256]{2,1,0:T(8,128)(2,1)} %all-to-all-done.2.in_ref, ...), custom_call_target="tpu_custom_call" | custom-call | flops 149999992832 | bytes 1500000000 | tf_op jit(solution)/shard_map/half_sums/pallas_call | solution.py:304
  91.5 4.2 %collective-permute-start.2 = (bf16[1536,256]{1,0:T(8,128)(2,1)}, bf16[1536,256]{1,0:T(8,128)(2,1)}, u32[]{:S(2)}, u32[]{:S(2)}) collective-permute-start(bf16[1536,256]{1,0:T(8,128)(2,1)} %get-tuple-element.19.__), channel_id=1, source_target_pairs={{0,16},{2,18},{4,20},{6,22},{8,24},{10,26},{12,28},{14,30},{16,0},... | collective-permute-start | bytes 2359304 | tf_op jit(solution)/shard_map/ppermute | solution.py:435
  95.7 0.0 collective-permute-done.in_ref
  95.7 7.4 %modal_axial_coefficients.3.__ = bf16[16,144,256]{2,1,0:T(8,128)(2,1)} custom-call(s32[2]{0:T(128)} %pad_add_fusion._.place_ref, bf16[2,128,96]{2,1,0:T(8,128)(2,1)} %constant.40.clone.upper_ref, bf16[2,128,96]{2,1,0:T(8,128)(2,1)} %constant.41.clone.lower_ref, f32[256,256]{1,0:T(8,128)} %axial_ref.9, f32[16,128,256]{2,1,0:T(8,128)} %get-tuple-element.18.own_ref, ...), custom_call_target="tpu_custom_call" | custom-call | flops 179999997952 | bytes 1800000000 | tf_op jit(solution)/shard_map/modal_axial_coefficients/pallas_call | solution.py:332
  103.1 21.9 %all-to-all-done.1.in_ref = bf16[8,512,256]{2,1,0:T(8,128)(2,1)} async-done(((bf16[8,512,256]{2,1,0:T(8,128)(2,1)}), bf16[8,512,256]{2,1,0:T(8,128)(2,1)}, u32[]{:S(2)}, u32[]{:S(2)}) %all-to-all-start.1) | async-done | bytes 2097184 | tf_op jit(solution)/shard_map/all_to_all | solution.py:430
  125.0 7.0 %all-to-all-start.3 = ((bf16[16,144,256]{2,1,0:T(8,128)(2,1)}), bf16[16,144,256]{2,1,0:T(8,128)(2,1)}, u32[]{:S(2)}, u32[]{:S(2)}) async-start(bf16[16,144,256]{2,1,0:T(8,128)(2,1)} %modal_axial_coefficients.3.__), calls=%async_computation.3 | async-start | bytes 2359296 | tf_op jit(solution)/shard_map/all_to_all | solution.py:430
  132.0 6.0 %half_sums.5 = (f32[16,128,256]{2,1,0:T(8,128)}, bf16[1536,256]{1,0:T(8,128)(2,1)}) custom-call(s32[2]{0:T(128)} %pad_add_fusion._.place_ref, bf16[2,224,256]{2,1,0:T(8,128)(2,1)} %constant.38.clone.upper_ref, bf16[2,224,256]{2,1,0:T(8,128)(2,1)} %constant.39.clone.lower_ref, bf16[8,512,256]{2,1,0:T(8,128)(2,1)} %all-to-all-done.1.in_ref, ...), custom_call_target="tpu_custom_call" | custom-call | flops 149999992832 | bytes 1500000000 | tf_op jit(solution)/shard_map/half_sums/pallas_call | solution.py:304
  138.0 1.1 collective-permute-start.1
  139.1 0.0 collective-permute-done.2.in_ref
  139.1 7.3 %modal_axial_coefficients.4.rest_0_ = bf16[16,144,256]{2,1,0:T(8,128)(2,1)} custom-call(s32[2]{0:T(128)} %pad_add_fusion._.place_ref, bf16[2,128,96]{2,1,0:T(8,128)(2,1)} %constant.40.clone.upper_ref, bf16[2,128,96]{2,1,0:T(8,128)(2,1)} %constant.41.clone.lower_ref, f32[256,256]{1,0:T(8,128)} %axial_ref.9, f32[16,128,256]{2,1,0:T(8,128)} %get-tuple-element.22.own_ref, ...), custom_call_target="tpu_custom_call" | custom-call | flops 179999997952 | bytes 1800000000 | tf_op jit(solution)/shard_map/modal_axial_coefficients/pallas_call | solution.py:332
  146.4 6.3 %all-to-all-done.3.in_ref = bf16[16,144,256]{2,1,0:T(8,128)(2,1)} async-done(((bf16[16,144,256]{2,1,0:T(8,128)(2,1)}), bf16[16,144,256]{2,1,0:T(8,128)(2,1)}, u32[]{:S(2)}, u32[]{:S(2)}) %all-to-all-start.3) | async-done | bytes 1179680 | tf_op jit(solution)/shard_map/all_to_all | solution.py:430
  152.7 6.2 %all-to-all-start.5 = ((bf16[16,144,256]{2,1,0:T(8,128)(2,1)}), bf16[16,144,256]{2,1,0:T(8,128)(2,1)}, u32[]{:S(2)}, u32[]{:S(2)}) async-start(bf16[16,144,256]{2,1,0:T(8,128)(2,1)} %modal_axial_coefficients.4.rest_0_), calls=%async_computation.5 | async-start | bytes 2359296 | tf_op jit(solution)/shard_map/all_to_all | solution.py:430
  159.0 8.3 %radial_solve.3 = (f32[3,8,2,128,256]{4,3,2,1,0:T(8,128)}, bf16[4,272,256]{2,1,0:T(8,128)(2,1)}) custom-call(s32[2]{0:T(128)} %pad_add_fusion._.place_ref, f32[3]{0:T(128)} %diffusion_ref.5, f32[1,256]{1,0:T(1,128)} %bitcast.3, f32[4,1,256]{2,1,0:T(1,128)} %reshape.7.radial_eigen_ref, f32[256,256]{1,0:T(8,128)} %axial_ref.11, f32[4,256,256]{2,1,0:T(8,128)} %forward_ref.5, ...), custom_call_target="tpu_custom_call" | custom-call | flops 210000003072 | bytes 2100000000 | tf_op jit(solution)/shard_map/radial_solve/pallas_call | solution.py:361
  167.2 1.4 collective-permute-start.3
  168.6 4.4 %collective-permute-done.1.in_ref = bf16[1536,256]{1,0:T(8,128)(2,1)} collective-permute-done((bf16[1536,256]{1,0:T(8,128)(2,1)}, bf16[1536,256]{1,0:T(8,128)(2,1)}, u32[]{:S(2)}, u32[]{:S(2)}) %collective-permute-start.1) | collective-permute-done | bytes 786464 | tf_op jit(solution)/shard_map/ppermute | solution.py:435
  173.0 7.3 %modal_axial_coefficients.5.rest_0_ = bf16[16,144,256]{2,1,0:T(8,128)(2,1)} custom-call(s32[2]{0:T(128)} %pad_add_fusion._.place_ref, bf16[2,128,96]{2,1,0:T(8,128)(2,1)} %constant.40.clone.upper_ref, bf16[2,128,96]{2,1,0:T(8,128)(2,1)} %constant.41.clone.lower_ref, f32[256,256]{1,0:T(8,128)} %axial_ref.9, f32[16,128,256]{2,1,0:T(8,128)} %get-tuple-element.20.own_ref, ...), custom_call_target="tpu_custom_call" | custom-call | flops 179999997952 | bytes 1800000000 | tf_op jit(solution)/shard_map/modal_axial_coefficients/pallas_call | solution.py:332
  180.3 3.4 %all-to-all-done.5.in_ref = bf16[16,144,256]{2,1,0:T(8,128)(2,1)} async-done(((bf16[16,144,256]{2,1,0:T(8,128)(2,1)}), bf16[16,144,256]{2,1,0:T(8,128)(2,1)}, u32[]{:S(2)}, u32[]{:S(2)}) %all-to-all-start.5) | async-done | bytes 1179680 | tf_op jit(solution)/shard_map/all_to_all | solution.py:430
  183.7 7.6 %all-to-all-start.4 = ((bf16[16,144,256]{2,1,0:T(8,128)(2,1)}), bf16[16,144,256]{2,1,0:T(8,128)(2,1)}, u32[]{:S(2)}, u32[]{:S(2)}) async-start(bf16[16,144,256]{2,1,0:T(8,128)(2,1)} %modal_axial_coefficients.5.rest_0_), calls=%async_computation.4 | async-start | bytes 2359296 | tf_op jit(solution)/shard_map/all_to_all | solution.py:430
  191.3 8.2 %radial_solve.4 = (f32[3,8,2,128,256]{4,3,2,1,0:T(8,128)}, bf16[4,272,256]{2,1,0:T(8,128)(2,1)}) custom-call(s32[2]{0:T(128)} %pad_add_fusion._.place_ref, f32[3]{0:T(128)} %diffusion_ref.5, f32[1,256]{1,0:T(1,128)} %bitcast.4, f32[4,1,256]{2,1,0:T(1,128)} %reshape.7.radial_eigen_ref, f32[256,256]{1,0:T(8,128)} %axial_ref.11, ...), custom_call_target="tpu_custom_call", output_to_operand_aliasing={{0}: (9, {})} | custom-call | flops 210000003072 | bytes 2100000000 | tf_op jit(solution)/shard_map/radial_solve/pallas_call | solution.py:361
  199.5 1.4 collective-permute-start.5
  200.9 0.0 collective-permute-done.3.in_ref
  200.9 4.0 %partner_rows.3.rest_1_ = f32[3,8,2,128,256]{4,3,2,1,0:T(8,128)} custom-call(s32[2]{0:T(128)} %pad_add_fusion._.place_ref, bf16[4,272,256]{2,1,0:T(8,128)(2,1)} %collective-permute-done.3.in_ref, f32[3,8,2,128,256]{4,3,2,1,0:T(8,128)} %get-tuple-element.26._, bf16[4,272,256]{2,1,0:T(8,128)(2,1)} %get-tuple-element.25.__.rest_0_), custom_call_target="tpu_custom_call", output_to_operand_aliasing={{}: (2, {})} | custom-call | flops 60000002048 | bytes 600000000 | tf_op jit(solution)/shard_map/partner_rows/pallas_call | solution.py:403
  204.9 4.8 %all-to-all-done.4.in_ref = bf16[16,144,256]{2,1,0:T(8,128)(2,1)} async-done(((bf16[16,144,256]{2,1,0:T(8,128)(2,1)}), bf16[16,144,256]{2,1,0:T(8,128)(2,1)}, u32[]{:S(2)}, u32[]{:S(2)}) %all-to-all-start.4) | async-done | bytes 1179680 | tf_op jit(solution)/shard_map/all_to_all | solution.py:430
  209.7 8.2 %radial_solve.5 = (f32[3,8,2,128,256]{4,3,2,1,0:T(8,128)}, bf16[4,272,256]{2,1,0:T(8,128)(2,1)}) custom-call(s32[2]{0:T(128)} %pad_add_fusion._.place_ref, f32[3]{0:T(128)} %diffusion_ref.5, f32[1,256]{1,0:T(1,128)} %bitcast.5, f32[4,1,256]{2,1,0:T(1,128)} %reshape.7.radial_eigen_ref, f32[256,256]{1,0:T(8,128)} %axial_ref.11, ...), custom_call_target="tpu_custom_call", output_to_operand_aliasing={{0}: (9, {})} | custom-call | flops 210000003072 | bytes 2100000000 | tf_op jit(solution)/shard_map/radial_solve/pallas_call | solution.py:361
  217.9 0.4 collective-permute-start.4
  218.3 3.4 %collective-permute-done.5.in_ref = bf16[4,272,256]{2,1,0:T(8,128)(2,1)} collective-permute-done((bf16[4,272,256]{2,1,0:T(8,128)(2,1)}, bf16[4,272,256]{2,1,0:T(8,128)(2,1)}, u32[]{:S(2)}, u32[]{:S(2)}) %collective-permute-start.5) | collective-permute-done | bytes 557088 | tf_op jit(solution)/shard_map/ppermute | solution.py:438
  221.8 4.0 %partner_rows.4._ = f32[3,8,2,128,256]{4,3,2,1,0:T(8,128)} custom-call(s32[2]{0:T(128)} %pad_add_fusion._.place_ref, bf16[4,272,256]{2,1,0:T(8,128)(2,1)} %collective-permute-done.5.in_ref, f32[3,8,2,128,256]{4,3,2,1,0:T(8,128)} %get-tuple-element.28._, bf16[4,272,256]{2,1,0:T(8,128)(2,1)} %get-tuple-element.27.__), custom_call_target="tpu_custom_call", output_to_operand_aliasing={{}: (2, {})} | custom-call | flops 60000002048 | bytes 600000000 | tf_op jit(solution)/shard_map/partner_rows/pallas_call | solution.py:403
  225.8 7.8 %collective-permute-done.4.in_ref = bf16[4,272,256]{2,1,0:T(8,128)(2,1)S(1)} collective-permute-done((bf16[4,272,256]{2,1,0:T(8,128)(2,1)}, bf16[4,272,256]{2,1,0:T(8,128)(2,1)S(1)}, u32[]{:S(2)}, u32[]{:S(2)}) %collective-permute-start.4) | collective-permute-done | bytes 557088 | tf_op jit(solution)/shard_map/ppermute | solution.py:438
  233.6 0.0 copy-start.1
  233.6 0.8 copy-done.1
  234.4 4.0 %partner_rows.5 = f32[3,8,2,128,256]{4,3,2,1,0:T(8,128)} custom-call(s32[2]{0:T(128)} %pad_add_fusion._.place_ref, bf16[4,272,256]{2,1,0:T(8,128)(2,1)} %copy-done.1, f32[3,8,2,128,256]{4,3,2,1,0:T(8,128)} %partner_rows.4._, bf16[4,272,256]{2,1,0:T(8,128)(2,1)} %get-tuple-element.27.__), custom_call_target="tpu_custom_call", output_to_operand_aliasing={{}: (2, {})} | custom-call | flops 60000002048 | bytes 600000000 | tf_op jit(solution)/shard_map/partner_rows/pallas_call | solution.py:403
Async XLA Ops:
  8.3 29.8 %all-to-all-start = ((bf16[8,512,256]{2,1,0:T(8,128)(2,1)}), bf16[8,512,256]{2,1,0:T(8,128)(2,1)}, u32[]{:S(2)}, u32[]{:S(2)}) async-start(bf16[8,512,256]{2,1,0:T(8,128)(2,1)} %window_coefficients.3._), calls=%async_computation | async-start | bytes 4194304 | tf_op jit(solution)/shard_map/all_to_all | solution.py:430
  13.2 8.3 %copy-start = (f32[4,256]{1,0:T(4,128)S(1)}, f32[4,256]{1,0:T(4,128)}, u32[]{:S(2)}) copy-start(f32[4,256]{1,0:T(4,128)} %param.21) | copy-start | bytes 12292
  38.1 41.8 %all-to-all-start.2 = ((bf16[8,512,256]{2,1,0:T(8,128)(2,1)}), bf16[8,512,256]{2,1,0:T(8,128)(2,1)}, u32[]{:S(2)}, u32[]{:S(2)}) async-start(bf16[8,512,256]{2,1,0:T(8,128)(2,1)} %window_coefficients.4.__), calls=%async_computation.2 | async-start | bytes 4194304 | tf_op jit(solution)/shard_map/all_to_all | solution.py:430
  49.2 46.5 %collective-permute-start = (bf16[1536,256]{1,0:T(8,128)(2,1)}, bf16[1536,256]{1,0:T(8,128)(2,1)}, u32[]{:S(2)}, u32[]{:S(2)}) collective-permute-start(bf16[1536,256]{1,0:T(8,128)(2,1)} %get-tuple-element.17._), channel_id=1, source_target_pairs={{0,16},{2,18},{4,20},{6,22},{8,24},{10,26},{12,28},{14,30},{16,0},... | collective-permute-start | bytes 2359304 | tf_op jit(solution)/shard_map/ppermute | solution.py:435
  79.9 45.1 %all-to-all-start.1 = ((bf16[8,512,256]{2,1,0:T(8,128)(2,1)}), bf16[8,512,256]{2,1,0:T(8,128)(2,1)}, u32[]{:S(2)}, u32[]{:S(2)}) async-start(bf16[8,512,256]{2,1,0:T(8,128)(2,1)} %window_coefficients.5.__), calls=%async_computation.1 | async-start | bytes 4194304 | tf_op jit(solution)/shard_map/all_to_all | solution.py:430
  91.5 47.6 %collective-permute-start.2 = (bf16[1536,256]{1,0:T(8,128)(2,1)}, bf16[1536,256]{1,0:T(8,128)(2,1)}, u32[]{:S(2)}, u32[]{:S(2)}) collective-permute-start(bf16[1536,256]{1,0:T(8,128)(2,1)} %get-tuple-element.19.__), channel_id=1, source_target_pairs={{0,16},{2,18},{4,20},{6,22},{8,24},{10,26},{12,28},{14,30},{16,0},... | collective-permute-start | bytes 2359304 | tf_op jit(solution)/shard_map/ppermute | solution.py:435
  125.0 27.7 %all-to-all-start.3 = ((bf16[16,144,256]{2,1,0:T(8,128)(2,1)}), bf16[16,144,256]{2,1,0:T(8,128)(2,1)}, u32[]{:S(2)}, u32[]{:S(2)}) async-start(bf16[16,144,256]{2,1,0:T(8,128)(2,1)} %modal_axial_coefficients.3.__), calls=%async_computation.3 | async-start | bytes 2359296 | tf_op jit(solution)/shard_map/all_to_all | solution.py:430
  138.0 35.1 %collective-permute-start.1 = (bf16[1536,256]{1,0:T(8,128)(2,1)}, bf16[1536,256]{1,0:T(8,128)(2,1)}, u32[]{:S(2)}, u32[]{:S(2)}) collective-permute-start(bf16[1536,256]{1,0:T(8,128)(2,1)} %get-tuple-element.21.__), channel_id=1, source_target_pairs={{0,16},{2,18},{4,20},{6,22},{8,24},{10,26},{12,28},{14,30},{16,0},... | collective-permute-start | bytes 2359304 | tf_op jit(solution)/shard_map/ppermute | solution.py:435
  152.7 30.9 %all-to-all-start.5 = ((bf16[16,144,256]{2,1,0:T(8,128)(2,1)}), bf16[16,144,256]{2,1,0:T(8,128)(2,1)}, u32[]{:S(2)}, u32[]{:S(2)}) async-start(bf16[16,144,256]{2,1,0:T(8,128)(2,1)} %modal_axial_coefficients.4.rest_0_), calls=%async_computation.5 | async-start | bytes 2359296 | tf_op jit(solution)/shard_map/all_to_all | solution.py:430
  167.2 33.7 %collective-permute-start.3 = (bf16[4,272,256]{2,1,0:T(8,128)(2,1)}, bf16[4,272,256]{2,1,0:T(8,128)(2,1)}, u32[]{:S(2)}, u32[]{:S(2)}) collective-permute-start(bf16[4,272,256]{2,1,0:T(8,128)(2,1)} %get-tuple-element.23.__), channel_id=1, source_target_pairs={{0,1},{1,0},{2,3},{3,2},{4,5},{5,4},{6,7},{7,6},{8,9},{9,8},{10,11... | collective-permute-start | bytes 1671176 | tf_op jit(solution)/shard_map/ppermute | solution.py:438
  183.7 26.0 %all-to-all-start.4 = ((bf16[16,144,256]{2,1,0:T(8,128)(2,1)}), bf16[16,144,256]{2,1,0:T(8,128)(2,1)}, u32[]{:S(2)}, u32[]{:S(2)}) async-start(bf16[16,144,256]{2,1,0:T(8,128)(2,1)} %modal_axial_coefficients.5.rest_0_), calls=%async_computation.4 | async-start | bytes 2359296 | tf_op jit(solution)/shard_map/all_to_all | solution.py:430
  199.5 22.3 %collective-permute-start.5 = (bf16[4,272,256]{2,1,0:T(8,128)(2,1)}, bf16[4,272,256]{2,1,0:T(8,128)(2,1)}, u32[]{:S(2)}, u32[]{:S(2)}) collective-permute-start(bf16[4,272,256]{2,1,0:T(8,128)(2,1)} %get-tuple-element.25.__.rest_0_), channel_id=1, source_target_pairs={{0,1},{1,0},{2,3},{3,2},{4,5},{5,4},{6,7},{7,6},{8,9},{9,8},{10,11... | collective-permute-start | bytes 1671176 | tf_op jit(solution)/shard_map/ppermute | solution.py:438
  217.9 15.7 %collective-permute-start.4 = (bf16[4,272,256]{2,1,0:T(8,128)(2,1)}, bf16[4,272,256]{2,1,0:T(8,128)(2,1)S(1)}, u32[]{:S(2)}, u32[]{:S(2)}) collective-permute-start(bf16[4,272,256]{2,1,0:T(8,128)(2,1)} %get-tuple-element.27.__), channel_id=1, source_target_pairs={{0,1},{1,0},{2,3},{3,2},{4,5},{5,4},{6,7},{7,6},{8,9},{9,8},{10,11... | collective-permute-start | bytes 1671176 | tf_op jit(solution)/shard_map/ppermute | solution.py:438
  233.6 0.8 copy-start.1

commit v4 on v3

--- a/solution.py
+++ b/solution.py
@@ -53,7 +53,8 @@
     return np.stack([values.real, values.imag], axis=1).reshape(-1, values.shape[-1])
 
 
-def half_tables(total, retained, slab, basis, sent):
+def half_tables(total, retained, basis, sent):
+    window = basis.shape[0]
     half, own = total // 2, retained // 2
     rank = basis.shape[1]
     envelope = window_basis(half, total, own, (sent - 1) // 2)
@@ -65,10 +66,10 @@
         direct = waves(side * own + np.arange(own), points, total) / np.sqrt(total)
         carried = np.exp(-2j * np.pi * centre * points / total)[None, :] * envelope.T
         rows = np.concatenate([interleave(direct), interleave(carried)])
-        rows = rows.reshape(rows.shape[0], -1, slab) @ basis
-        table = np.zeros((2 * own + sent, half // slab, rank + 1))
+        rows = rows.reshape(rows.shape[0], -1, window) @ basis
+        table = np.zeros((2 * own + sent, half // window, rank + 1))
         table[: rows.shape[0], :, :rank] = rows
-        local.append(table.reshape(table.shape[0], -1))
+        local.append(table)
         offsets = np.exp(-2j * np.pi * (away - centre)[:, None] * points[None, :] / total)
         weights = (offsets @ envelope) / np.sqrt(total)
         parts = np.zeros((own, 2, sent))
@@ -111,26 +112,44 @@
     return jnp.where(place == kept - 1, 0.0, values)
 
 
-def encode_body(upper_ref, lower_ref, forcing_ref, _, out_ref, *, group, kept):
-    points, rows, width = forcing_ref.shape[1:]
-    block = forcing_ref[0].astype(F32)
+def rows_body(_, forcing_ref, __, out_ref):
+    out_ref[...] = forcing_ref[0]
+
+
+def encode_body(
+    _, own_upper, own_lower, other_upper, other_lower, own_ref, other_ref, __, *out_refs, group, kept
+):
+    step = pl.program_id(0)
+    points, rows, width = other_ref.shape
+    blocks = (own_ref[0].astype(F32), other_ref[...].astype(F32))
+    tables = ((own_upper[0], own_lower[0]), (other_upper[0], other_lower[0]))
+    parts = []
     for part in range(rows // group):
-        piece = block[:, part * group : (part + 1) * group, :].reshape(points * group, width)
-        piece = piece.astype(BF16)
-        coefficients = jnp.dot(upper_ref[...], piece, preferred_element_type=F32)
-        coefficients += jnp.dot(lower_ref[...], piece, preferred_element_type=F32)
-        coded = encode_columns(coefficients.reshape(group, kept, width), kept)
-        place = part * group * kept
-        out_ref[0, place : place + group * kept, :] = coded.reshape(group * kept, width).astype(BF16)
-
-
-def gather_body(_, upper_ref, lower_ref, in_ref, __, own_ref, send_ref, *, kept, sent, rows):
-    sources, _, width = in_ref.shape
+        sums = None
+        for block, table in zip(blocks, tables):
+            piece = block[:, part * group : (part + 1) * group, :].reshape(points * group, width)
+            piece = piece.astype(BF16)
+            for half in table:
+                term = jnp.dot(half, piece, preferred_element_type=F32)
+                sums = term if sums is None else sums + term
+        coded = encode_columns(sums.reshape(group, kept, width), kept)
+        parts.append(coded.reshape(group * kept, width).astype(BF16))
+    coded = jnp.concatenate(parts, axis=0)
+    for place, out_ref in enumerate(out_refs):
+
+        @pl.when(step == place)
+        def _(out_ref=out_ref):
+            out_ref[...] = coded
+
+
+def gather_body(_, upper_ref, lower_ref, *refs, kept, sent, rows):
+    *in_refs, __, own_ref, send_ref = refs
+    width = send_ref.shape[1]
     table = (upper_ref[0], lower_ref[0])
     own = own_ref.shape[1]
     for row in range(rows):
-        coded = in_ref[:, row * kept : (row + 1) * kept, :].astype(F32)
-        values = decode_columns(coded, kept).reshape(sources * kept, width)
+        coded = [ref[row * kept : (row + 1) * kept, :].astype(F32) for ref in in_refs]
+        values = decode_columns(jnp.stack(coded), kept).reshape(len(in_refs) * kept, width)
         sums = dot3(table, split(values))
         own_ref[row] = sums[:own]
         send_ref[row * sent : (row + 1) * sent, :] = encode_columns(sums[None, own:], sent)[0].astype(BF16)
@@ -175,18 +194,21 @@
     *rest,
     field,
     radial_devices,
+    modes,
 ):
     out_ref, send_ref, held_ref = rest[-3:]
-    mode = pl.program_id(0)
+    step = pl.program_id(0)
+    each = forward_ref.shape[0]
     devices, coded_rows, width = in_ref.shape
     rows = coded_rows - 16
-    per_group = devices // radial_devices
-    stride = 2 * pl.num_programs(0)
-
-    @pl.when(mode == 0)
+    chips = devices // radial_devices // 2
+    stride = 2 * modes
+
+    @pl.when(step == 0)
     def _():
         for source in range(devices):
-            target = (source % radial_devices) * per_group + source // radial_devices
+            chip, core, block = source // radial_devices // 2, source // radial_devices % 2, source % radial_devices
+            target = (block * 2 + core) * chips + chip
             coded = in_ref[source].astype(F32)
             values = linear_decode(coded[:rows], coded[rows : rows + 1])
             for lane in range(width // 128):
@@ -195,33 +217,37 @@
                 ]
 
     radial = devices * rows // stride
-    pieces = []
-    for part in range(2):
-        for lane in range(width // 128):
-            pieces.append(held_ref[lane, pl.ds(mode * 2 + part, radial, stride=stride), :])
-    values = jnp.concatenate(pieces, axis=1)
-    values = dot3(split(forward_ref[0]), split(values))
-    eigen = jnp.broadcast_to(radial_eigen_ref[0], (128, radial)).T[:, :1]
-    denominator = 1.0 + diffusion_ref[field] * (eigen + axial_eigen_ref[...])
-    inverse = 1.0 / denominator
-    values = jnp.concatenate([values[:, :width] * inverse, values[:, width:] * inverse], axis=1)
-    values = dot3(split(backward_ref[0]), split(values))
-    values = jnp.concatenate([values[:, :width], values[:, width:]], axis=0)
-    values = dot3(split(values), split(axial_ref[...]), ROWS_BY_ROWS)
-    values = values.reshape(2, radial_devices, radial // radial_devices, width)
+    axial = split(axial_ref[...])
     first = place_ref[0] == 0
-    out_ref[0, 0] = jnp.where(first, values[:, 0], values[:, 1])
-    other = jnp.where(first, values[:, 1], values[:, 0]).reshape(radial, width)
-    scale = code_scale(jnp.max(jnp.abs(other), axis=0, keepdims=True))
-    send_ref[0, :radial, :] = linear_encode(other, scale).astype(BF16)
-    send_ref[0, radial:, :] = jnp.broadcast_to(scale, (16, width)).astype(BF16)
+    for mode in range(each):
+        pieces = []
+        for part in range(2):
+            for lane in range(width // 128):
+                start = (step * each + mode) * 2 + part
+                pieces.append(held_ref[lane, pl.ds(start, radial, stride=stride), :])
+        values = jnp.concatenate(pieces, axis=1)
+        values = dot3(split(forward_ref[mode]), split(values))
+        eigen = jnp.broadcast_to(radial_eigen_ref[mode], (128, radial)).T[:, :1]
+        denominator = 1.0 + diffusion_ref[field] * (eigen + axial_eigen_ref[...])
+        inverse = 1.0 / denominator
+        values = jnp.concatenate([values[:, :width] * inverse, values[:, width:] * inverse], axis=1)
+        values = dot3(split(backward_ref[mode]), split(values))
+        values = jnp.concatenate([values[:, :width], values[:, width:]], axis=0)
+        values = dot3(split(values), axial, ROWS_BY_ROWS)
+        values = values.reshape(2, radial_devices, radial // radial_devices, width)
+        out_ref[0, mode] = jnp.where(first, values[:, 0], values[:, 1])
+        other = jnp.where(first, values[:, 1], values[:, 0]).reshape(radial, width)
+        scale = code_scale(jnp.max(jnp.abs(other), axis=0, keepdims=True))
+        send_ref[mode, :radial, :] = linear_encode(other, scale).astype(BF16)
+        send_ref[mode, radial:, :] = jnp.broadcast_to(scale, (16, width)).astype(BF16)
 
 
 def finish_body(place_ref, in_ref, _, __, out_ref):
-    radial, width = out_ref.shape[2] * out_ref.shape[3], out_ref.shape[4]
-    coded = in_ref[0].astype(F32)
-    values = linear_decode(coded[:radial], coded[radial : radial + 1])
-    out_ref[0, 0] = values.reshape(out_ref.shape[2:])
+    radial = out_ref.shape[2] * out_ref.shape[3]
+    for mode in range(in_ref.shape[0]):
+        coded = in_ref[mode].astype(F32)
+        values = linear_decode(coded[:radial], coded[radial : radial + 1])
+        out_ref[0, mode] = values.reshape(out_ref.shape[2:])
 
 
 def params():
@@ -263,41 +289,64 @@
     near = processors // 2
     owners = near * radial_devices
     rows = radial_block // near
-    group, kept, sent = 8, slab // 2, 96
+    group, kept, sent = 8, slab * 3 // 4, 96
     per_owner = 2 * own_modes
-    side = lax.axis_index("modes") // near
-    place = jnp.stack([lax.axis_index("rad"), side]).astype(jnp.int32)
-
-    basis = window_basis(slab, total, 2 * retained - 1, kept - 1)
-    spread = np.zeros((group, kept, slab, group))
+    chips = near // 2
+    position = lax.axis_index("modes")
+    core, chip, side = position % 2, position // 2 % chips, position // near
+    place = jnp.stack([lax.axis_index("rad"), side, core, chip, side * chips + chip]).astype(jnp.int32)
+
+    window = 2 * slab
+    basis = window_basis(window, total, 2 * retained - 1, kept - 1)
+    spread = np.zeros((2, group, kept, slab, group))
     for row in range(group):
-        spread[row, : kept - 1, :, row] = basis.T
-    spread_upper, spread_lower = halves(spread.reshape(group * kept, slab * group))
-    local, join_table = half_tables(total, retained, slab, basis, sent)
-    local_upper, local_lower = halves(local)
+        spread[:, row, : kept - 1, :, row] = basis.reshape(2, slab, kept - 1).transpose(0, 2, 1)
+    spread_upper, spread_lower = halves(spread.reshape(2, group * kept, slab * group))
+    local, join_table = half_tables(total, retained, basis, sent)
+    seen = [[here ^ step for step in range(chips)] for here in range(chips)]
+    local = np.stack([table[:, order] for table in local for order in seen])
+    local_upper, local_lower = halves(local.reshape(2 * chips, retained + sent, chips * kept))
     join_upper, join_lower = halves(join_table)
     axial_eigen = axial_eigenvalues.reshape(1, width)
     radial_eigen = radial_eigenvalues.reshape(own_modes, 1, radial)
 
-    def of_side(table):
-        return pl.BlockSpec((1,) + table.shape[1:], lambda i, p: (p[1], 0, 0))
-
-    def encode(field, after):
+    def chosen(table, index):
+        return pl.BlockSpec((1,) + table.shape[1:], lambda i, p: (index(p), 0, 0))
+
+    def encode(field, other, after):
+        message = (rows * kept, width)
         return pl.pallas_call(
             functools.partial(encode_body, group=group, kept=kept),
-            grid=(near,),
-            in_specs=[
-                whole(spread_upper.shape),
-                whole(spread_lower.shape),
-                pl.BlockSpec((1, slab, rows, width), lambda i: (field, 0, i, 0)),
-                ANY,
-            ],
-            out_specs=pl.BlockSpec((1, rows * kept, width), lambda i: (i, 0, 0)),
-            out_shape=jax.ShapeDtypeStruct((near, rows * kept, width), BF16),
+            grid_spec=pltpu.PrefetchScalarGridSpec(
+                num_scalar_prefetch=1,
+                grid=(chips,),
+                in_specs=[
+                    chosen(spread_upper, lambda p: p[2]),
+                    chosen(spread_lower, lambda p: p[2]),
+                    chosen(spread_upper, lambda p: 1 - p[2]),
+                    chosen(spread_lower, lambda p: 1 - p[2]),
+                    pl.BlockSpec(
+                        (1, slab, rows, width), lambda i, p: (field, 0, p[2] * chips + (p[3] ^ i), 0)
+                    ),
+                    pl.BlockSpec((slab, rows, width), lambda i, p: (0, p[3] ^ i, 0)),
+                    ANY,
+                ],
+                out_specs=[whole(message)] * chips,
+            ),
+            out_shape=[jax.ShapeDtypeStruct(message, BF16)] * chips,
             compiler_params=params(),
             cost_estimate=cost(7),
             name="window_coefficients",
-        )(jnp.asarray(spread_upper), jnp.asarray(spread_lower), forcing, after)
+        )(
+            place,
+            jnp.asarray(spread_upper),
+            jnp.asarray(spread_lower),
+            jnp.asarray(spread_upper),
+            jnp.asarray(spread_lower),
+            forcing,
+            other,
+            after,
+        )
 
     def gather(received, after):
         step = 4
@@ -306,12 +355,9 @@
             grid_spec=pltpu.PrefetchScalarGridSpec(
                 num_scalar_prefetch=1,
                 grid=(rows // step,),
-                in_specs=[
-                    of_side(local_upper),
-                    of_side(local_lower),
-                    pl.BlockSpec((near, step * kept, width), lambda i, _: (0, i, 0)),
-                    ANY,
-                ],
+                in_specs=[chosen(local_upper, lambda p: p[4]), chosen(local_lower, lambda p: p[4])]
+                + [pl.BlockSpec((step * kept, width), lambda i, _: (i, 0))] * chips
+                + [ANY],
                 out_specs=[
                     pl.BlockSpec((step, retained, width), lambda i, _: (i, 0, 0)),
                     pl.BlockSpec((step * sent, width), lambda i, _: (i, 0)),
@@ -324,7 +370,7 @@
             compiler_params=params(),
             cost_estimate=cost(5),
             name="half_sums",
-        )(place, jnp.asarray(local_upper), jnp.asarray(local_lower), received, after)
+        )(place, jnp.asarray(local_upper), jnp.asarray(local_lower), *received, after)
 
     def join(own, received, after):
         step = 4
@@ -335,8 +381,8 @@
                 num_scalar_prefetch=1,
                 grid=(rows // step,),
                 in_specs=[
-                    of_side(join_upper),
-                    of_side(join_lower),
+                    chosen(join_upper, lambda p: p[1]),
+                    chosen(join_lower, lambda p: p[1]),
                     whole(axial_forward.shape),
                     pl.BlockSpec((step, retained, width), lambda i, _: (i, 0, 0)),
                     pl.BlockSpec((step * sent, width), lambda i, _: (i, 0)),
@@ -352,30 +398,34 @@
         )(place, jnp.asarray(join_upper), jnp.asarray(join_lower), axial_forward, own, received, after)
 
     out_shape = jax.ShapeDtypeStruct((fields, own_modes * radial_devices, 2, radial_block, width), F32)
-    out_block = (1, 1, 2, radial_block, width)
+    each = 2
+    turns = own_modes // each
+    out_block = (1, each, 2, radial_block, width)
     send_rows = radial + 16
 
     def solve(field, received, out, after):
         carried = [] if out is None else [out]
         first = 9
         return pl.pallas_call(
-            functools.partial(solve_body, field=field, radial_devices=radial_devices),
+            functools.partial(
+                solve_body, field=field, radial_devices=radial_devices, modes=own_modes
+            ),
             grid_spec=pltpu.PrefetchScalarGridSpec(
                 num_scalar_prefetch=1,
-                grid=(own_modes,),
+                grid=(turns,),
                 in_specs=[
                     SMEM,
                     whole(axial_eigen.shape),
-                    pl.BlockSpec((1, 1, radial), lambda i, _: (i, 0, 0)),
+                    pl.BlockSpec((each, 1, radial), lambda i, _: (i, 0, 0)),
                     whole(axial_inverse_map.shape),
-                    pl.BlockSpec((1, radial, radial), lambda i, _: (i, 0, 0)),
-                    pl.BlockSpec((1, radial, radial), lambda i, _: (i, 0, 0)),
+                    pl.BlockSpec((each, radial, radial), lambda i, _: (i, 0, 0)),
+                    pl.BlockSpec((each, radial, radial), lambda i, _: (i, 0, 0)),
                     whole(received.shape),
                 ]
                 + [ANY] * (1 + len(carried)),
                 out_specs=[
-                    pl.BlockSpec(out_block, lambda i, y: (field, y[0] * own_modes + i, 0, 0, 0)),
-                    pl.BlockSpec((1, send_rows, width), lambda i, _: (i, 0, 0)),
+                    pl.BlockSpec(out_block, lambda i, y: (field, y[0] * turns + i, 0, 0, 0)),
+                    pl.BlockSpec((each, send_rows, width), lambda i, _: (i, 0, 0)),
                 ],
                 scratch_shapes=[
                     pltpu.VMEM((width // 128, radial * per_owner, 128), F32)
@@ -404,14 +454,14 @@
             finish_body,
             grid_spec=pltpu.PrefetchScalarGridSpec(
                 num_scalar_prefetch=1,
-                grid=(own_modes,),
+                grid=(turns,),
                 in_specs=[
-                    pl.BlockSpec((1, send_rows, width), lambda i, _: (i, 0, 0)),
+                    pl.BlockSpec((each, send_rows, width), lambda i, _: (i, 0, 0)),
                     ANY,
                     ANY,
                 ],
                 out_specs=pl.BlockSpec(
-                    out_block, lambda i, y: (field, (1 - y[0]) * own_modes + i, 0, 0, 0)
+                    out_block, lambda i, y: (field, (1 - y[0]) * turns + i, 0, 0, 0)
                 ),
             ),
             out_shape=out_shape,
@@ -421,37 +471,60 @@
             name="partner_rows",
         )(place, received, out, after)
 
-    sides = [list(range(near)), list(range(near, processors))]
-    side_owners = [
-        [m * radial_devices + y for m in members for y in range(radial_devices)] for members in sides
-    ]
+    side_owners = [list(range(owners)), list(range(owners, 2 * owners))]
 
     def exchange(values, names, groups):
         return lax.all_to_all(
             values, names, split_axis=0, concat_axis=0, tiled=True, axis_index_groups=groups
         )
 
-    def across(values):
-        return lax.ppermute(values, "modes", [(i, (i + near) % processors) for i in range(processors)])
+    def flip(values, bits):
+        return lax.ppermute(values, "modes", [(i, i ^ bits) for i in range(processors)])
+
+    def other_rows(field, after):
+        shape = (slab, radial_block // 2, width)
+        return pl.pallas_call(
+            rows_body,
+            grid_spec=pltpu.PrefetchScalarGridSpec(
+                num_scalar_prefetch=1,
+                grid=(4,),
+                in_specs=[
+                    pl.BlockSpec(
+                        (1, slab // 4) + shape[1:], lambda i, p: (field, i, 1 - p[2], 0)
+                    ),
+                    ANY,
+                ],
+                out_specs=pl.BlockSpec((slab // 4,) + shape[1:], lambda i, _: (i, 0, 0)),
+            ),
+            out_shape=jax.ShapeDtypeStruct(shape, BF16),
+            compiler_params=params(),
+            cost_estimate=cost(2),
+            name="other_core_rows",
+        )(place, forcing, after)
 
     def partner(values):
         return lax.ppermute(values, "rad", [(0, 1), (1, 0)])
 
     windows, own, away, spectra, partners = {}, {}, {}, {}, {}
+    swapped = {}
     last, out = diffusion, None
     steps = (
-        ["e0", "e1", "h0", "e2", "h1"]
+        ["c0", "c1", "e0", "c2", "e1", "h0", "e2", "h1"]
         + ["j0", "h2", "j1", "s0", "j2"]
         + ["s1", "f0", "s2", "f1", "f2"]
     )
     for step in steps:
         field = int(step[1])
-        if step[0] == "e":
-            last = encode(field, last)
-            windows[field] = exchange(last, "modes", sides)
+        if step[0] == "c":
+            last = other_rows(field, last)
+            swapped[field] = flip(last, 1)
+        elif step[0] == "e":
+            made = encode(field, swapped[field], last)
+            last = made[0]
+            windows[field] = [last] + [flip(made[j], 2 * j) for j in range(1, chips)]
         elif step[0] == "h":
             own[field], last = gather(windows[field], last)
-            away[field] = across(last)
+            away[field] = flip(last, near)
         elif step[0] == "j":
             last = join(own[field], away[field], last)
             spectra[field] = exchange(last, ("modes", "rad"), side_owners)
@@ -536,7 +609,8 @@
     own_modes = maps[2].shape[0]
     paired = (
         radial_devices == 2
-        and processors % 2 == 0
+        and processors >= 8
+        and processors & (processors - 1) == 0
         and radial_block == 8 * processors
         and width % 128 == 0
         and own_modes == 4

time: 243 us -> 215 us (0.88); the launches traced: 238 us -> 213 us
  waiting for transfers between devices: 89.9 us -> 54.2 us
  Pallas kernels: 102 us -> 111 us
    all_to_all x6 -> x3, waiting for transfers between devices: 74.2 us -> 16.8 us  [exchange(): lax.all_to_all(values, names, split_axis=0, concat_axis=0, tiled=True, ax...]
    ppermute x3 -> x15, waiting for transfers between devices: 4.41 us -> 24.8 us  [flip(): lax.ppermute(values, 'modes', [(i, i ^ bits) for i in range(processors)])]
    pallas_call x0 -> x3, Pallas kernels: none -> 13.4 us  [other_rows(): pl.pallas_call(rows_body, grid_spec=pltpu.PrefetchScalarGridSpec(num_scal...]
    all_to_all x6 -> x3, starting transfers between devices: 36.4 us -> 26.7 us  [exchange(): lax.all_to_all(values, names, split_axis=0, concat_axis=0, tiled=True, ax...]
    ppermute x3 -> x15, starting transfers between devices: 5.35 us -> 14.6 us  [flip(): lax.ppermute(values, 'modes', [(i, i ^ bits) for i in range(processors)])]
    pallas_call x3, Pallas kernels: 12.1 us -> 8.12 us  [finish(): pl.pallas_call(finish_body, grid_spec=pltpu.PrefetchScalarGridSpec(num_sc...]
  transfers between devices with their start and end apart: 12 -> 21, of which waited for: 9 -> 10; matrix products, arithmetic and copies ran while one was open for 1% -> 0% of each run, Pallas kernels for 37% -> 49%
where the time goes in v4:
time: 215 us; the launch traced here: 213 us
  Pallas kernels  111 us (52%)
  waiting for transfers between devices  54.2 us (25%)
  starting transfers between devices  44.4 us (21%)
  local copies, waits for them, and re-layouts  3.31 us (2%)
    all_to_all x3, starting transfers between devices, exchange(): lax.all_to_all(values, names, split_axis=0, concat_axis=0, tiled=True, ax...  26.7 us
    pallas_call x3, Pallas kernels, solve(): pl.pallas_call(functools.partial(solve_body, field=field, radial_devices=...  25.1 us
    pallas_call x3, Pallas kernels, encode(): pl.pallas_call(functools.partial(encode_body, group=group, kept=kept), gr...  25 us
    ppermute x15, waiting for transfers between devices, flip(): lax.ppermute(values, 'modes', [(i, i ^ bits) for i in range(processors)])  24.8 us
    pallas_call x3, Pallas kernels, join(): pl.pallas_call(functools.partial(join_body, sent=sent, rows=step), grid_s...  21.9 us
    pallas_call x3, Pallas kernels, gather(): pl.pallas_call(functools.partial(gather_body, kept=kept, sent=sent, rows=...  17.8 us
    all_to_all x3, waiting for transfers between devices, exchange(): lax.all_to_all(values, names, split_axis=0, concat_axis=0, tiled=True, ax...  16.8 us
    ppermute x15, starting transfers between devices, flip(): lax.ppermute(values, 'modes', [(i, i ^ bits) for i in range(processors)])  14.6 us
  transfers between devices with their start and end apart: 21, of which 10 were waited for; matrix products, arithmetic and copies ran while one was open for 0% of the time, Pallas kernels for 49%

profile of v4, /device:TPU:17, one launch (start us, length us, event | category | flops | bytes accessed | tf_op | source)
XLA Modules:
  0.0 213.1 jit_solution(15947118260518124421)
XLA Ops:
  0.0 0.6 stack.23._.place_ref
  0.6 4.5 %other_core_rows.3.__ = bf16[64,64,256]{2,1,0:T(8,128)(2,1)} custom-call(s32[5]{0:T(128)} %stack.23._.place_ref, bf16[3,64,128,256]{3,2,1,0:T(8,128)(2,1)} %own_ref.5, f32[3]{0:T(128)} %diffusion_ref.5), custom_call_target="tpu_custom_call" | custom-call | flops 60000002048 | bytes 600000000 | tf_op jit(solution)/shard_map/other_core_rows/pallas_call | solution.py:486
  5.0 0.7 collective-permute-start
  5.7 4.5 %other_core_rows.4.__ = bf16[64,64,256]{2,1,0:T(8,128)(2,1)} custom-call(s32[5]{0:T(128)} %stack.23._.place_ref, bf16[3,64,128,256]{3,2,1,0:T(8,128)(2,1)} %own_ref.5, bf16[64,64,256]{2,1,0:T(8,128)(2,1)} %other_core_rows.3.__), custom_call_target="tpu_custom_call" | custom-call | flops 60000002048 | bytes 600000000 | tf_op jit(solution)/shard_map/other_core_rows/pallas_call | solution.py:486
  10.3 0.6 reshape.7.radial_eigen_ref
  10.9 1.3 copy-done.1
  12.3 8.4 %window_coefficients.3 = (bf16[768,256]{1,0:T(8,128)(2,1)}, bf16[768,256]{1,0:T(8,128)(2,1)}, bf16[768,256]{1,0:T(8,128)(2,1)}, bf16[768,256]{1,0:T(8,128)(2,1)}) custom-call(s32[5]{0:T(128)} %stack.23._.place_ref, bf16[2,384,512]{2,1,0:T(8,128)(2,1)} %constant.64.clone.own_upper.other_upper, bf16[2,384,512]{2,1,0:T(8,128)(2,1)} %constant.65.clone.own_lower.other_lower, ...), custom_call_target="tpu_custom_call" | custom-call | flops 210000003072 | bytes 2100000000 | tf_op jit(solution)/shard_map/window_coefficients/pallas_call | solution.py:318
  20.6 1.2 collective-permute-start.2
  21.8 1.3 collective-permute-start.3
  23.3 4.5 %other_core_rows.5.__ = bf16[64,64,256]{2,1,0:T(8,128)(2,1)} custom-call(s32[5]{0:T(128)} %stack.23._.place_ref, bf16[3,64,128,256]{3,2,1,0:T(8,128)(2,1)} %own_ref.5, bf16[768,256]{1,0:T(8,128)(2,1)} %get-tuple-element.29.__.refs_0_), custom_call_target="tpu_custom_call" | custom-call | flops 60000002048 | bytes 600000000 | tf_op jit(solution)/shard_map/other_core_rows/pallas_call | solution.py:486
  27.7 1.2 collective-permute-start.1
  29.0 8.3 %window_coefficients.4 = (bf16[768,256]{1,0:T(8,128)(2,1)}, bf16[768,256]{1,0:T(8,128)(2,1)}, bf16[768,256]{1,0:T(8,128)(2,1)}, bf16[768,256]{1,0:T(8,128)(2,1)}) custom-call(s32[5]{0:T(128)} %stack.23._.place_ref, bf16[2,384,512]{2,1,0:T(8,128)(2,1)} %constant.64.clone.own_upper.other_upper, bf16[2,384,512]{2,1,0:T(8,128)(2,1)} %constant.65.clone.own_lower.other_lower, ...), custom_call_target="tpu_custom_call" | custom-call | flops 210000003072 | bytes 2100000000 | tf_op jit(solution)/shard_map/window_coefficients/pallas_call | solution.py:318
  37.3 1.2 collective-permute-start.10
  38.4 1.3 collective-permute-start.11
  39.9 0.6 collective-permute-done.4.refs_3_
  40.5 5.9 %half_sums.3 = (f32[16,128,256]{2,1,0:T(8,128)}, bf16[1536,256]{1,0:T(8,128)(2,1)}) custom-call(s32[5]{0:T(128)} %stack.23._.place_ref, bf16[8,224,192]{2,1,0:T(8,128)(2,1)} %constant.66.clone.upper_ref, bf16[8,224,192]{2,1,0:T(8,128)(2,1)} %constant.67.clone.lower_ref, bf16[768,256]{1,0:T(8,128)(2,1)} %get-tuple-element.29.__.refs_0_, ...), custom_call_target="tpu_custom_call" | custom-call | flops 149999992832 | bytes 1500000000 | tf_op jit(solution)/shard_map/half_sums/pallas_call | solution.py:353
  46.7 8.3 %window_coefficients.5 = (bf16[768,256]{1,0:T(8,128)(2,1)}, bf16[768,256]{1,0:T(8,128)(2,1)}, bf16[768,256]{1,0:T(8,128)(2,1)}, bf16[768,256]{1,0:T(8,128)(2,1)}) custom-call(s32[5]{0:T(128)} %stack.23._.place_ref, bf16[2,384,512]{2,1,0:T(8,128)(2,1)} %constant.64.clone.own_upper.other_upper, bf16[2,384,512]{2,1,0:T(8,128)(2,1)} %constant.65.clone.own_lower.other_lower, ...), custom_call_target="tpu_custom_call" | custom-call | flops 210000003072 | bytes 2100000000 | tf_op jit(solution)/shard_map/window_coefficients/pallas_call | solution.py:318
  55.0 1.1 collective-permute-start.6
  56.1 1.4 collective-permute-start.7
  57.6 7.6 %collective-permute-done.12.refs_3_ = bf16[768,256]{1,0:T(8,128)(2,1)} collective-permute-done((bf16[768,256]{1,0:T(8,128)(2,1)}, bf16[768,256]{1,0:T(8,128)(2,1)}, u32[]{:S(2)}, u32[]{:S(2)}) %collective-permute-start.12) | collective-permute-done | bytes 393248 | tf_op jit(solution)/shard_map/ppermute | solution.py:482
  65.2 5.9 %half_sums.4 = (f32[16,128,256]{2,1,0:T(8,128)}, bf16[1536,256]{1,0:T(8,128)(2,1)}) custom-call(s32[5]{0:T(128)} %stack.23._.place_ref, bf16[8,224,192]{2,1,0:T(8,128)(2,1)} %constant.66.clone.upper_ref, bf16[8,224,192]{2,1,0:T(8,128)(2,1)} %constant.67.clone.lower_ref, bf16[768,256]{1,0:T(8,128)(2,1)} %get-tuple-element.33.refs_4_.refs_0_, ...), custom_call_target="tpu_custom_call" | custom-call | flops 149999992832 | bytes 1500000000 | tf_op jit(solution)/shard_map/half_sums/pallas_call | solution.py:353
  71.1 2.2 %collective-permute-start.14 = (bf16[1536,256]{1,0:T(8,128)(2,1)}, bf16[1536,256]{1,0:T(8,128)(2,1)}, u32[]{:S(2)}, u32[]{:S(2)}) collective-permute-start(bf16[1536,256]{1,0:T(8,128)(2,1)} %get-tuple-element.43.__), channel_id=1, source_target_pairs={{0,16},{2,18},{4,20},{6,22},{8,24},{10,26},{12,28},{14,30},{16,0},... | collective-permute-start | bytes 2359304 | tf_op jit(solution)/shard_map/ppermute | solution.py:482
  73.3 6.1 %collective-permute-done.9.in_ref = bf16[1536,256]{1,0:T(8,128)(2,1)} collective-permute-done((bf16[1536,256]{1,0:T(8,128)(2,1)}, bf16[1536,256]{1,0:T(8,128)(2,1)}, u32[]{:S(2)}, u32[]{:S(2)}) %collective-permute-start.9) | collective-permute-done | bytes 786464 | tf_op jit(solution)/shard_map/ppermute | solution.py:482
  79.5 7.3 %modal_axial_coefficients.3.refs_4_ = bf16[16,144,256]{2,1,0:T(8,128)(2,1)} custom-call(s32[5]{0:T(128)} %stack.23._.place_ref, bf16[2,128,96]{2,1,0:T(8,128)(2,1)} %constant.68.clone.upper_ref, bf16[2,128,96]{2,1,0:T(8,128)(2,1)} %constant.69.clone.lower_ref, f32[256,256]{1,0:T(8,128)} %axial_ref.9, f32[16,128,256]{2,1,0:T(8,128)} %get-tuple-element.39.own_ref, ...), custom_call_target="tpu_custom_call" | custom-call | flops 179999997952 | bytes 1800000000 | tf_op jit(solution)/shard_map/modal_axial_coefficients/pallas_call | solution.py:378
  86.7 12.1 %all-to-all-start = ((bf16[16,144,256]{2,1,0:T(8,128)(2,1)}), bf16[16,144,256]{2,1,0:T(8,128)(2,1)}, u32[]{:S(2)}, u32[]{:S(2)}) async-start(bf16[16,144,256]{2,1,0:T(8,128)(2,1)} %modal_axial_coefficients.3.refs_4_), calls=%async_computation | async-start | bytes 2359296 | tf_op jit(solution)/shard_map/all_to_all | solution.py:477
  98.9 5.9 %half_sums.5 = (f32[16,128,256]{2,1,0:T(8,128)}, bf16[1536,256]{1,0:T(8,128)(2,1)}) custom-call(s32[5]{0:T(128)} %stack.23._.place_ref, bf16[8,224,192]{2,1,0:T(8,128)(2,1)} %constant.66.clone.upper_ref, bf16[8,224,192]{2,1,0:T(8,128)(2,1)} %constant.67.clone.lower_ref, bf16[768,256]{1,0:T(8,128)(2,1)} %get-tuple-element.35.refs_4_.refs_0_, ...), custom_call_target="tpu_custom_call" | custom-call | flops 149999992832 | bytes 1500000000 | tf_op jit(solution)/shard_map/half_sums/pallas_call | solution.py:353
  104.9 2.2 %collective-permute-start.13 = (bf16[1536,256]{1,0:T(8,128)(2,1)}, bf16[1536,256]{1,0:T(8,128)(2,1)}, u32[]{:S(2)}, u32[]{:S(2)}) collective-permute-start(bf16[1536,256]{1,0:T(8,128)(2,1)} %get-tuple-element.45.__), channel_id=1, source_target_pairs={{0,16},{2,18},{4,20},{6,22},{8,24},{10,26},{12,28},{14,30},{16,0},... | collective-permute-start | bytes 2359304 | tf_op jit(solution)/shard_map/ppermute | solution.py:482
  107.1 6.1 %collective-permute-done.14.in_ref = bf16[1536,256]{1,0:T(8,128)(2,1)} collective-permute-done((bf16[1536,256]{1,0:T(8,128)(2,1)}, bf16[1536,256]{1,0:T(8,128)(2,1)}, u32[]{:S(2)}, u32[]{:S(2)}) %collective-permute-start.14) | collective-permute-done | bytes 786464 | tf_op jit(solution)/shard_map/ppermute | solution.py:482
  113.2 7.3 %modal_axial_coefficients.4.rest_0_ = bf16[16,144,256]{2,1,0:T(8,128)(2,1)} custom-call(s32[5]{0:T(128)} %stack.23._.place_ref, bf16[2,128,96]{2,1,0:T(8,128)(2,1)} %constant.68.clone.upper_ref, bf16[2,128,96]{2,1,0:T(8,128)(2,1)} %constant.69.clone.lower_ref, f32[256,256]{1,0:T(8,128)} %axial_ref.9, f32[16,128,256]{2,1,0:T(8,128)} %get-tuple-element.46.own_ref, ...), custom_call_target="tpu_custom_call" | custom-call | flops 179999997952 | bytes 1800000000 | tf_op jit(solution)/shard_map/modal_axial_coefficients/pallas_call | solution.py:378
  120.5 5.9 %all-to-all-done.in_ref = bf16[16,144,256]{2,1,0:T(8,128)(2,1)} async-done(((bf16[16,144,256]{2,1,0:T(8,128)(2,1)}), bf16[16,144,256]{2,1,0:T(8,128)(2,1)}, u32[]{:S(2)}, u32[]{:S(2)}) %all-to-all-start) | async-done | bytes 1179680 | tf_op jit(solution)/shard_map/all_to_all | solution.py:477
  126.4 6.5 %all-to-all-start.2 = ((bf16[16,144,256]{2,1,0:T(8,128)(2,1)}), bf16[16,144,256]{2,1,0:T(8,128)(2,1)}, u32[]{:S(2)}, u32[]{:S(2)}) async-start(bf16[16,144,256]{2,1,0:T(8,128)(2,1)} %modal_axial_coefficients.4.rest_0_), calls=%async_computation.2 | async-start | bytes 2359296 | tf_op jit(solution)/shard_map/all_to_all | solution.py:477
  132.9 8.4 %radial_solve.3 = (f32[3,8,2,128,256]{4,3,2,1,0:T(8,128)}, bf16[4,272,256]{2,1,0:T(8,128)(2,1)}) custom-call(s32[5]{0:T(128)} %stack.23._.place_ref, f32[3]{0:T(128)} %diffusion_ref.5, f32[1,256]{1,0:T(1,128)} %bitcast.6, f32[4,1,256]{2,1,0:T(1,128)} %reshape.7.radial_eigen_ref, f32[256,256]{1,0:T(8,128)} %axial_ref.11, f32[4,256,256]{2,1,0:T(8,128)} %forward_ref.5, ...), custom_call_target="tpu_custom_call" | custom-call | flops 210000003072 | bytes 2100000000 | tf_op jit(solution)/shard_map/radial_solve/pallas_call | solution.py:409
  141.3 1.4 collective-permute-start.15
  142.7 4.3 %collective-permute-done.13.in_ref = bf16[1536,256]{1,0:T(8,128)(2,1)} collective-permute-done((bf16[1536,256]{1,0:T(8,128)(2,1)}, bf16[1536,256]{1,0:T(8,128)(2,1)}, u32[]{:S(2)}, u32[]{:S(2)}) %collective-permute-start.13) | collective-permute-done | bytes 786464 | tf_op jit(solution)/shard_map/ppermute | solution.py:482
  147.0 7.3 %modal_axial_coefficients.5.rest_0_ = bf16[16,144,256]{2,1,0:T(8,128)(2,1)} custom-call(s32[5]{0:T(128)} %stack.23._.place_ref, bf16[2,128,96]{2,1,0:T(8,128)(2,1)} %constant.68.clone.upper_ref, bf16[2,128,96]{2,1,0:T(8,128)(2,1)} %constant.69.clone.lower_ref, f32[256,256]{1,0:T(8,128)} %axial_ref.9, f32[16,128,256]{2,1,0:T(8,128)} %get-tuple-element.44.own_ref, ...), custom_call_target="tpu_custom_call" | custom-call | flops 179999997952 | bytes 1800000000 | tf_op jit(solution)/shard_map/modal_axial_coefficients/pallas_call | solution.py:378
  154.3 4.9 %all-to-all-done.2.in_ref = bf16[16,144,256]{2,1,0:T(8,128)(2,1)} async-done(((bf16[16,144,256]{2,1,0:T(8,128)(2,1)}), bf16[16,144,256]{2,1,0:T(8,128)(2,1)}, u32[]{:S(2)}, u32[]{:S(2)}) %all-to-all-start.2) | async-done | bytes 1179680 | tf_op jit(solution)/shard_map/all_to_all | solution.py:477
  159.2 8.1 %all-to-all-start.1 = ((bf16[16,144,256]{2,1,0:T(8,128)(2,1)}), bf16[16,144,256]{2,1,0:T(8,128)(2,1)}, u32[]{:S(2)}, u32[]{:S(2)}) async-start(bf16[16,144,256]{2,1,0:T(8,128)(2,1)} %modal_axial_coefficients.5.rest_0_), calls=%async_computation.1 | async-start | bytes 2359296 | tf_op jit(solution)/shard_map/all_to_all | solution.py:477
  167.3 8.4 %radial_solve.4 = (f32[3,8,2,128,256]{4,3,2,1,0:T(8,128)}, bf16[4,272,256]{2,1,0:T(8,128)(2,1)}) custom-call(s32[5]{0:T(128)} %stack.23._.place_ref, f32[3]{0:T(128)} %diffusion_ref.5, f32[1,256]{1,0:T(1,128)} %bitcast.7, f32[4,1,256]{2,1,0:T(1,128)} %reshape.7.radial_eigen_ref, f32[256,256]{1,0:T(8,128)} %axial_ref.11, ...), custom_call_target="tpu_custom_call", output_to_operand_aliasing={{0}: (9, {})} | custom-call | flops 210000003072 | bytes 2100000000 | tf_op jit(solution)/shard_map/radial_solve/pallas_call | solution.py:409
  175.7 1.4 collective-permute-start.17
  177.0 2.7 %partner_rows.3.rest_1_ = f32[3,8,2,128,256]{4,3,2,1,0:T(8,128)} custom-call(s32[5]{0:T(128)} %stack.23._.place_ref, bf16[4,272,256]{2,1,0:T(8,128)(2,1)} %collective-permute-done.15.in_ref, f32[3,8,2,128,256]{4,3,2,1,0:T(8,128)} %get-tuple-element.50._, bf16[4,272,256]{2,1,0:T(8,128)(2,1)} %get-tuple-element.49.__.rest_0_), custom_call_target="tpu_custom_call", output_to_operand_aliasing={{}: (2, {})} | custom-call | flops 60000002048 | bytes 600000000 | tf_op jit(solution)/shard_map/partner_rows/pallas_call | solution.py:453
  179.7 6.0 %all-to-all-done.1.in_ref = bf16[16,144,256]{2,1,0:T(8,128)(2,1)} async-done(((bf16[16,144,256]{2,1,0:T(8,128)(2,1)}), bf16[16,144,256]{2,1,0:T(8,128)(2,1)}, u32[]{:S(2)}, u32[]{:S(2)}) %all-to-all-start.1) | async-done | bytes 1179680 | tf_op jit(solution)/shard_map/all_to_all | solution.py:477
  185.7 8.3 %radial_solve.5 = (f32[3,8,2,128,256]{4,3,2,1,0:T(8,128)}, bf16[4,272,256]{2,1,0:T(8,128)(2,1)}) custom-call(s32[5]{0:T(128)} %stack.23._.place_ref, f32[3]{0:T(128)} %diffusion_ref.5, f32[1,256]{1,0:T(1,128)} %bitcast.8, f32[4,1,256]{2,1,0:T(1,128)} %reshape.7.radial_eigen_ref, f32[256,256]{1,0:T(8,128)} %axial_ref.11, ...), custom_call_target="tpu_custom_call", output_to_operand_aliasing={{0}: (9, {})} | custom-call | flops 210000003072 | bytes 2100000000 | tf_op jit(solution)/shard_map/radial_solve/pallas_call | solution.py:409
  194.1 0.3 collective-permute-start.16
  194.4 3.4 %collective-permute-done.17.in_ref = bf16[4,272,256]{2,1,0:T(8,128)(2,1)} collective-permute-done((bf16[4,272,256]{2,1,0:T(8,128)(2,1)}, bf16[4,272,256]{2,1,0:T(8,128)(2,1)}, u32[]{:S(2)}, u32[]{:S(2)}) %collective-permute-start.17) | collective-permute-done | bytes 557088 | tf_op jit(solution)/shard_map/ppermute | solution.py:506
  197.8 2.7 %partner_rows.4._ = f32[3,8,2,128,256]{4,3,2,1,0:T(8,128)} custom-call(s32[5]{0:T(128)} %stack.23._.place_ref, bf16[4,272,256]{2,1,0:T(8,128)(2,1)} %collective-permute-done.17.in_ref, f32[3,8,2,128,256]{4,3,2,1,0:T(8,128)} %get-tuple-element.52._, bf16[4,272,256]{2,1,0:T(8,128)(2,1)} %get-tuple-element.51.__), custom_call_target="tpu_custom_call", output_to_operand_aliasing={{}: (2, {})} | custom-call | flops 60000002048 | bytes 600000000 | tf_op jit(solution)/shard_map/partner_rows/pallas_call | solution.py:453
  200.5 9.1 %collective-permute-done.16.in_ref = bf16[4,272,256]{2,1,0:T(8,128)(2,1)S(1)} collective-permute-done((bf16[4,272,256]{2,1,0:T(8,128)(2,1)}, bf16[4,272,256]{2,1,0:T(8,128)(2,1)S(1)}, u32[]{:S(2)}, u32[]{:S(2)}) %collective-permute-start.16) | collective-permute-done | bytes 557088 | tf_op jit(solution)/shard_map/ppermute | solution.py:506
  209.6 0.8 copy-done.2
  210.4 2.7 %partner_rows.5 = f32[3,8,2,128,256]{4,3,2,1,0:T(8,128)} custom-call(s32[5]{0:T(128)} %stack.23._.place_ref, bf16[4,272,256]{2,1,0:T(8,128)(2,1)} %copy-done.2, f32[3,8,2,128,256]{4,3,2,1,0:T(8,128)} %partner_rows.4._, bf16[4,272,256]{2,1,0:T(8,128)(2,1)} %get-tuple-element.51.__), custom_call_target="tpu_custom_call", output_to_operand_aliasing={{}: (2, {})} | custom-call | flops 60000002048 | bytes 600000000 | tf_op jit(solution)/shard_map/partner_rows/pallas_call | solution.py:453
  (20 shorter events, 1.0 us)
Async XLA Ops:
  5.0 5.3 %copy-start = (f32[4,256]{1,0:T(4,128)S(1)}, f32[4,256]{1,0:T(4,128)}, u32[]{:S(2)}) copy-start(f32[4,256]{1,0:T(4,128)} %param.21) | copy-start | bytes 12292
  5.0 5.9 %collective-permute-start = (bf16[64,64,256]{2,1,0:T(8,128)(2,1)}, bf16[64,64,256]{2,1,0:T(8,128)(2,1)S(1)}, u32[]{:S(2)}, u32[]{:S(2)}) collective-permute-start(bf16[64,64,256]{2,1,0:T(8,128)(2,1)} %other_core_rows.3.__), channel_id=1, source_target_pairs={{0,2},{2,0},{4,6},{6,4},{8,10},{10,8},{12,14},{14,12},{16,18},{18,... | collective-permute-start | bytes 6291464 | tf_op jit(solution)/shard_map/ppermute | solution.py:482
  10.2 18.8 %collective-permute-start.5 = (bf16[64,64,256]{2,1,0:T(8,128)(2,1)}, bf16[64,64,256]{2,1,0:T(8,128)(2,1)}, u32[]{:S(2)}, u32[]{:S(2)}) collective-permute-start(bf16[64,64,256]{2,1,0:T(8,128)(2,1)} %other_core_rows.4.__), channel_id=1, source_target_pairs={{0,2},{2,0},{4,6},{6,4},{8,10},{10,8},{12,14},{14,12},{16,18},{18,... | collective-permute-start | bytes 6291464 | tf_op jit(solution)/shard_map/ppermute | solution.py:482
  10.9 1.3 copy-start.1
  20.6 17.8 %collective-permute-start.2 = (bf16[768,256]{1,0:T(8,128)(2,1)}, bf16[768,256]{1,0:T(8,128)(2,1)}, u32[]{:S(2)}, u32[]{:S(2)}) collective-permute-start(bf16[768,256]{1,0:T(8,128)(2,1)} %get-tuple-element.30), channel_id=1, source_target_pairs={{0,4},{2,6},{4,0},{6,2},{8,12},{10,14},{12,8},{14,10},{16,20},{18,... | collective-permute-start | bytes 1179656 | tf_op jit(solution)/shard_map/ppermute | solution.py:482
  21.8 17.9 %collective-permute-start.3 = (bf16[768,256]{1,0:T(8,128)(2,1)}, bf16[768,256]{1,0:T(8,128)(2,1)}, u32[]{:S(2)}, u32[]{:S(2)}) collective-permute-start(bf16[768,256]{1,0:T(8,128)(2,1)} %get-tuple-element.31), channel_id=1, source_target_pairs={{0,8},{2,10},{4,12},{6,14},{8,0},{10,2},{12,4},{14,6},{16,24},{18,... | collective-permute-start | bytes 1179656 | tf_op jit(solution)/shard_map/ppermute | solution.py:482
  23.1 17.4 %collective-permute-start.4 = (bf16[768,256]{1,0:T(8,128)(2,1)}, bf16[768,256]{1,0:T(8,128)(2,1)}, u32[]{:S(2)}, u32[]{:S(2)}) collective-permute-start(bf16[768,256]{1,0:T(8,128)(2,1)} %get-tuple-element.32), channel_id=1, source_target_pairs={{0,12},{2,14},{4,8},{6,10},{8,4},{10,6},{12,0},{14,2},{16,28},{18,... | collective-permute-start | bytes 1179656 | tf_op jit(solution)/shard_map/ppermute | solution.py:482
  27.7 18.9 %collective-permute-start.1 = (bf16[64,64,256]{2,1,0:T(8,128)(2,1)}, bf16[64,64,256]{2,1,0:T(8,128)(2,1)}, u32[]{:S(2)}, u32[]{:S(2)}) collective-permute-start(bf16[64,64,256]{2,1,0:T(8,128)(2,1)} %other_core_rows.5.__), channel_id=1, source_target_pairs={{0,2},{2,0},{4,6},{6,4},{8,10},{10,8},{12,14},{14,12},{16,18},{18,... | collective-permute-start | bytes 6291464 | tf_op jit(solution)/shard_map/ppermute | solution.py:482
  37.3 18.8 %collective-permute-start.10 = (bf16[768,256]{1,0:T(8,128)(2,1)}, bf16[768,256]{1,0:T(8,128)(2,1)}, u32[]{:S(2)}, u32[]{:S(2)}) collective-permute-start(bf16[768,256]{1,0:T(8,128)(2,1)} %get-tuple-element.40), channel_id=1, source_target_pairs={{0,4},{2,6},{4,0},{6,2},{8,12},{10,14},{12,8},{14,10},{16,20},{18,... | collective-permute-start | bytes 1179656 | tf_op jit(solution)/shard_map/ppermute | solution.py:482
  38.4 19.0 %collective-permute-start.11 = (bf16[768,256]{1,0:T(8,128)(2,1)}, bf16[768,256]{1,0:T(8,128)(2,1)}, u32[]{:S(2)}, u32[]{:S(2)}) collective-permute-start(bf16[768,256]{1,0:T(8,128)(2,1)} %get-tuple-element.41), channel_id=1, source_target_pairs={{0,8},{2,10},{4,12},{6,14},{8,0},{10,2},{12,4},{14,6},{16,24},{18,... | collective-permute-start | bytes 1179656 | tf_op jit(solution)/shard_map/ppermute | solution.py:482
  39.7 25.5 %collective-permute-start.12 = (bf16[768,256]{1,0:T(8,128)(2,1)}, bf16[768,256]{1,0:T(8,128)(2,1)}, u32[]{:S(2)}, u32[]{:S(2)}) collective-permute-start(bf16[768,256]{1,0:T(8,128)(2,1)} %get-tuple-element.42), channel_id=1, source_target_pairs={{0,12},{2,14},{4,8},{6,10},{8,4},{10,6},{12,0},{14,2},{16,28},{18,... | collective-permute-start | bytes 1179656 | tf_op jit(solution)/shard_map/ppermute | solution.py:482
  46.5 33.0 %collective-permute-start.9 = (bf16[1536,256]{1,0:T(8,128)(2,1)}, bf16[1536,256]{1,0:T(8,128)(2,1)}, u32[]{:S(2)}, u32[]{:S(2)}) collective-permute-start(bf16[1536,256]{1,0:T(8,128)(2,1)} %get-tuple-element.34.__), channel_id=1, source_target_pairs={{0,16},{2,18},{4,20},{6,22},{8,24},{10,26},{12,28},{14,30},{16,0},... | collective-permute-start | bytes 2359304 | tf_op jit(solution)/shard_map/ppermute | solution.py:482
  55.0 43.9 %collective-permute-start.6 = (bf16[768,256]{1,0:T(8,128)(2,1)}, bf16[768,256]{1,0:T(8,128)(2,1)}, u32[]{:S(2)}, u32[]{:S(2)}) collective-permute-start(bf16[768,256]{1,0:T(8,128)(2,1)} %get-tuple-element.36), channel_id=1, source_target_pairs={{0,4},{2,6},{4,0},{6,2},{8,12},{10,14},{12,8},{14,10},{16,20},{18,... | collective-permute-start | bytes 1179656 | tf_op jit(solution)/shard_map/ppermute | solution.py:482
  56.1 42.8 %collective-permute-start.7 = (bf16[768,256]{1,0:T(8,128)(2,1)}, bf16[768,256]{1,0:T(8,128)(2,1)}, u32[]{:S(2)}, u32[]{:S(2)}) collective-permute-start(bf16[768,256]{1,0:T(8,128)(2,1)} %get-tuple-element.37), channel_id=1, source_target_pairs={{0,8},{2,10},{4,12},{6,14},{8,0},{10,2},{12,4},{14,6},{16,24},{18,... | collective-permute-start | bytes 1179656 | tf_op jit(solution)/shard_map/ppermute | solution.py:482
  57.4 41.5 %collective-permute-start.8 = (bf16[768,256]{1,0:T(8,128)(2,1)}, bf16[768,256]{1,0:T(8,128)(2,1)}, u32[]{:S(2)}, u32[]{:S(2)}) collective-permute-start(bf16[768,256]{1,0:T(8,128)(2,1)} %get-tuple-element.38), channel_id=1, source_target_pairs={{0,12},{2,14},{4,8},{6,10},{8,4},{10,6},{12,0},{14,2},{16,28},{18,... | collective-permute-start | bytes 1179656 | tf_op jit(solution)/shard_map/ppermute | solution.py:482
  71.1 42.1 %collective-permute-start.14 = (bf16[1536,256]{1,0:T(8,128)(2,1)}, bf16[1536,256]{1,0:T(8,128)(2,1)}, u32[]{:S(2)}, u32[]{:S(2)}) collective-permute-start(bf16[1536,256]{1,0:T(8,128)(2,1)} %get-tuple-element.43.__), channel_id=1, source_target_pairs={{0,16},{2,18},{4,20},{6,22},{8,24},{10,26},{12,28},{14,30},{16,0},... | collective-permute-start | bytes 2359304 | tf_op jit(solution)/shard_map/ppermute | solution.py:482
  86.7 39.7 %all-to-all-start = ((bf16[16,144,256]{2,1,0:T(8,128)(2,1)}), bf16[16,144,256]{2,1,0:T(8,128)(2,1)}, u32[]{:S(2)}, u32[]{:S(2)}) async-start(bf16[16,144,256]{2,1,0:T(8,128)(2,1)} %modal_axial_coefficients.3.refs_4_), calls=%async_computation | async-start | bytes 2359296 | tf_op jit(solution)/shard_map/all_to_all | solution.py:477
  104.9 42.1 %collective-permute-start.13 = (bf16[1536,256]{1,0:T(8,128)(2,1)}, bf16[1536,256]{1,0:T(8,128)(2,1)}, u32[]{:S(2)}, u32[]{:S(2)}) collective-permute-start(bf16[1536,256]{1,0:T(8,128)(2,1)} %get-tuple-element.45.__), channel_id=1, source_target_pairs={{0,16},{2,18},{4,20},{6,22},{8,24},{10,26},{12,28},{14,30},{16,0},... | collective-permute-start | bytes 2359304 | tf_op jit(solution)/shard_map/ppermute | solution.py:482
  126.4 32.7 %all-to-all-start.2 = ((bf16[16,144,256]{2,1,0:T(8,128)(2,1)}), bf16[16,144,256]{2,1,0:T(8,128)(2,1)}, u32[]{:S(2)}, u32[]{:S(2)}) async-start(bf16[16,144,256]{2,1,0:T(8,128)(2,1)} %modal_axial_coefficients.4.rest_0_), calls=%async_computation.2 | async-start | bytes 2359296 | tf_op jit(solution)/shard_map/all_to_all | solution.py:477
  141.3 35.8 %collective-permute-start.15 = (bf16[4,272,256]{2,1,0:T(8,128)(2,1)}, bf16[4,272,256]{2,1,0:T(8,128)(2,1)}, u32[]{:S(2)}, u32[]{:S(2)}) collective-permute-start(bf16[4,272,256]{2,1,0:T(8,128)(2,1)} %get-tuple-element.47.__), channel_id=1, source_target_pairs={{0,1},{1,0},{2,3},{3,2},{4,5},{5,4},{6,7},{7,6},{8,9},{9,8},{10,11... | collective-permute-start | bytes 1671176 | tf_op jit(solution)/shard_map/ppermute | solution.py:506
  159.2 26.6 %all-to-all-start.1 = ((bf16[16,144,256]{2,1,0:T(8,128)(2,1)}), bf16[16,144,256]{2,1,0:T(8,128)(2,1)}, u32[]{:S(2)}, u32[]{:S(2)}) async-start(bf16[16,144,256]{2,1,0:T(8,128)(2,1)} %modal_axial_coefficients.5.rest_0_), calls=%async_computation.1 | async-start | bytes 2359296 | tf_op jit(solution)/shard_map/all_to_all | solution.py:477
  175.7 22.1 %collective-permute-start.17 = (bf16[4,272,256]{2,1,0:T(8,128)(2,1)}, bf16[4,272,256]{2,1,0:T(8,128)(2,1)}, u32[]{:S(2)}, u32[]{:S(2)}) collective-permute-start(bf16[4,272,256]{2,1,0:T(8,128)(2,1)} %get-tuple-element.49.__.rest_0_), channel_id=1, source_target_pairs={{0,1},{1,0},{2,3},{3,2},{4,5},{5,4},{6,7},{7,6},{8,9},{9,8},{10,11... | collective-permute-start | bytes 1671176 | tf_op jit(solution)/shard_map/ppermute | solution.py:506
  194.1 15.6 %collective-permute-start.16 = (bf16[4,272,256]{2,1,0:T(8,128)(2,1)}, bf16[4,272,256]{2,1,0:T(8,128)(2,1)S(1)}, u32[]{:S(2)}, u32[]{:S(2)}) collective-permute-start(bf16[4,272,256]{2,1,0:T(8,128)(2,1)} %get-tuple-element.51.__), channel_id=1, source_target_pairs={{0,1},{1,0},{2,3},{3,2},{4,5},{5,4},{6,7},{7,6},{8,9},{9,8},{10,11... | collective-permute-start | bytes 1671176 | tf_op jit(solution)/shard_map/ppermute | solution.py:506
  209.6 0.8 copy-start.2

commit v5 on v4

--- a/solution.py
+++ b/solution.py
@@ -11,7 +11,7 @@
 
 BF16 = jnp.bfloat16
 F32 = jnp.float32
-VMEM_BYTES = 60 * 1024 * 1024
+VMEM_BYTES = 40 * 1024 * 1024
 
 CODE_SPAN = 126.0
 CODE_MID = 0.5
@@ -57,7 +57,7 @@
     window = basis.shape[0]
     half, own = total // 2, retained // 2
     rank = basis.shape[1]
-    envelope = window_basis(half, total, own, (sent - 1) // 2)
+    envelope = window_basis(half, total, own, sent // 2)
     local, join = [], []
     for side in range(2):
         points = side * half + np.arange(half)
@@ -117,14 +117,14 @@
 
 
 def encode_body(
-    _, own_upper, own_lower, other_upper, other_lower, own_ref, other_ref, __, *out_refs, group, kept
+    _, own_upper, own_lower, other_upper, other_lower, own_ref, other_ref, __, *out_refs, group, kept, parts
 ):
     step = pl.program_id(0)
-    points, rows, width = other_ref.shape
+    points, _, width = other_ref.shape
     blocks = (own_ref[0].astype(F32), other_ref[...].astype(F32))
     tables = ((own_upper[0], own_lower[0]), (other_upper[0], other_lower[0]))
-    parts = []
-    for part in range(rows // group):
+    made = []
+    for part in parts:
         sums = None
         for block, table in zip(blocks, tables):
             piece = block[:, part * group : (part + 1) * group, :].reshape(points * group, width)
@@ -133,8 +133,8 @@
                 term = jnp.dot(half, piece, preferred_element_type=F32)
                 sums = term if sums is None else sums + term
         coded = encode_columns(sums.reshape(group, kept, width), kept)
-        parts.append(coded.reshape(group * kept, width).astype(BF16))
-    coded = jnp.concatenate(parts, axis=0)
+        made.append(coded.reshape(group * kept, width).astype(BF16))
+    coded = jnp.concatenate(made, axis=0)
     for place, out_ref in enumerate(out_refs):
 
         @pl.when(step == place)
@@ -142,36 +142,61 @@
             out_ref[...] = coded
 
 
-def gather_body(_, upper_ref, lower_ref, *refs, kept, sent, rows):
-    *in_refs, __, own_ref, send_ref = refs
+def gather_body(_, upper_ref, lower_ref, *refs, kept, rows):
+    *in_refs, __, own_ref, send_ref, scale_ref = refs
+    step = pl.program_id(0)
     width = send_ref.shape[1]
     table = (upper_ref[0], lower_ref[0])
     own = own_ref.shape[1]
+    made = []
     for row in range(rows):
-        coded = [ref[row * kept : (row + 1) * kept, :].astype(F32) for ref in in_refs]
-        values = decode_columns(jnp.stack(coded), kept).reshape(len(in_refs) * kept, width)
-        sums = dot3(table, split(values))
+        here = slice(row * kept, (row + 1) * kept)
+        coded = jnp.stack([ref[here, :].astype(F32) for ref in in_refs])
+        sums = dot3(table, split(decode_columns(coded, kept).reshape(-1, width)))
         own_ref[row] = sums[:own]
-        send_ref[row * sent : (row + 1) * sent, :] = encode_columns(sums[None, own:], sent)[0].astype(BF16)
-
-
-def join_body(
-    _, upper_ref, lower_ref, axial_ref, own_ref, in_ref, __, out_ref, held_ref, *, sent, rows
-):
+        scale = code_scale(jnp.max(jnp.abs(sums[own:]), axis=0, keepdims=True))
+        scale_ref[pl.ds(step * rows + row, 1), :] = scale
+        made.append(linear_encode(sums[own:], scale))
+    made = jnp.concatenate(made, axis=0).astype(BF16)
+    count = made.shape[0]
+    send_ref[pl.ds(pl.multiple_of(step * count, count), count), :] = made
+
+    @pl.when(step == pl.num_programs(0) - 1)
+    def _():
+        send_ref[send_ref.shape[0] - scale_ref.shape[0] :, :] = scale_ref[...].astype(BF16)
+
+
+def join_body(_, upper_ref, lower_ref, axial_ref, *refs, sent, rows, turns):
+    *pieces, __, out_ref, held_ref = refs
     step = pl.program_id(0)
-    width = in_ref.shape[1]
-    owners, coded_rows = out_ref.shape[:2]
+    owners, coded_rows, width = out_ref.shape
     block = coded_rows - 16
     table = (upper_ref[0], lower_ref[0])
     axial = split(axial_ref[...])
-    for row in range(rows):
-        coded = in_ref[row * sent : (row + 1) * sent, :].astype(F32)
-        values = decode_columns(coded[None], sent)[0]
-        spectrum = own_ref[row] + dot3(table, split(values))
-        axial_coef = dot3(split(spectrum), axial, ROWS_BY_ROWS).reshape(owners, -1, width)
-        each = axial_coef.shape[1]
-        place = pl.multiple_of((step * rows + row) * each, each)
-        held_ref[:, pl.ds(place, each), :] = axial_coef
+
+    def add(own_ref, in_ref, start):
+        total = in_ref.shape[0] // (sent + 1)
+        count = rows * sent
+        local = step - start
+        coded = in_ref[pl.ds(pl.multiple_of(local * count, count), count), :].astype(F32)
+        scales = in_ref[total * sent :, :].astype(F32)
+        place = lax.broadcasted_iota(jnp.int32, scales.shape, 0)
+        for row in range(rows):
+            here = place == local * rows + row
+            scale = jnp.sum(jnp.where(here, scales, 0.0), axis=0, keepdims=True)
+            values = linear_decode(coded[row * sent : (row + 1) * sent], scale)
+            spectrum = own_ref[row] + dot3(table, split(values))
+            axial_coef = dot3(split(spectrum), axial, ROWS_BY_ROWS).reshape(owners, -1, width)
+            each = axial_coef.shape[1]
+            target = pl.multiple_of((step * rows + row) * each, each)
+            held_ref[:, pl.ds(target, each), :] = axial_coef
+
+    if len(turns) == 1:
+        add(*pieces, 0)
+    else:
+        for number, (start, count) in enumerate(turns):
+            here = pieces[2 * number : 2 * number + 2]
+            pl.when((step >= start) & (step < start + count))(functools.partial(add, *here, start))
 
     @pl.when(step == pl.num_programs(0) - 1)
     def _():
@@ -190,17 +215,19 @@
     axial_ref,
     forward_ref,
     backward_ref,
-    in_ref,
     *rest,
     field,
     radial_devices,
     modes,
+    first_mode,
+    pieces,
 ):
+    in_refs = rest[:pieces]
     out_ref, send_ref, held_ref = rest[-3:]
     step = pl.program_id(0)
     each = forward_ref.shape[0]
-    devices, coded_rows, width = in_ref.shape
-    rows = coded_rows - 16
+    devices, _, width = in_refs[0].shape
+    rows = sum(ref.shape[1] - 16 for ref in in_refs)
     chips = devices // radial_devices // 2
     stride = 2 * modes
 
@@ -209,23 +236,25 @@
         for source in range(devices):
             chip, core, block = source // radial_devices // 2, source // radial_devices % 2, source % radial_devices
             target = (block * 2 + core) * chips + chip
-            coded = in_ref[source].astype(F32)
-            values = linear_decode(coded[:rows], coded[rows : rows + 1])
-            for lane in range(width // 128):
-                held_ref[lane, target * rows : (target + 1) * rows, :] = values[
-                    :, lane * 128 : (lane + 1) * 128
-                ]
+            start = target * rows
+            for in_ref in in_refs:
+                count = in_ref.shape[1] - 16
+                coded = in_ref[source].astype(F32)
+                values = linear_decode(coded[:count], coded[count : count + 1])
+                for lane in range(width // 128):
+                    held_ref[lane, start : start + count, :] = values[:, lane * 128 : (lane + 1) * 128]
+                start += count
 
     radial = devices * rows // stride
     axial = split(axial_ref[...])
     first = place_ref[0] == 0
     for mode in range(each):
-        pieces = []
+        columns = []
         for part in range(2):
             for lane in range(width // 128):
-                start = (step * each + mode) * 2 + part
-                pieces.append(held_ref[lane, pl.ds(start, radial, stride=stride), :])
-        values = jnp.concatenate(pieces, axis=1)
+                start = (first_mode + step * each + mode) * 2 + part
+                columns.append(held_ref[lane, pl.ds(start, radial, stride=stride), :])
+        values = jnp.concatenate(columns, axis=1)
         values = dot3(split(forward_ref[mode]), split(values))
         eigen = jnp.broadcast_to(radial_eigen_ref[mode], (128, radial)).T[:, :1]
         denominator = 1.0 + diffusion_ref[field] * (eigen + axial_eigen_ref[...])
@@ -289,7 +318,7 @@
     near = processors // 2
     owners = near * radial_devices
     rows = radial_block // near
-    group, kept, sent = 8, slab * 3 // 4, 96
+    group, kept, sent = 8, slab * 3 // 4, 88
     per_owner = 2 * own_modes
     chips = near // 2
     position = lax.axis_index("modes")
@@ -313,10 +342,10 @@
     def chosen(table, index):
         return pl.BlockSpec((1,) + table.shape[1:], lambda i, p: (index(p), 0, 0))
 
-    def encode(field, other, after):
-        message = (rows * kept, width)
+    def encode(field, parts, other, after):
+        message = (len(parts) * group * kept, width)
         return pl.pallas_call(
-            functools.partial(encode_body, group=group, kept=kept),
+            functools.partial(encode_body, group=group, kept=kept, parts=parts),
             grid_spec=pltpu.PrefetchScalarGridSpec(
                 num_scalar_prefetch=1,
                 grid=(chips,),
@@ -328,7 +357,7 @@
                     pl.BlockSpec(
                         (1, slab, rows, width), lambda i, p: (field, 0, p[2] * chips + (p[3] ^ i), 0)
                     ),
-                    pl.BlockSpec((slab, rows, width), lambda i, p: (0, p[3] ^ i, 0)),
+                    pl.BlockSpec((slab, rows, width), lambda i, p: (0, (p[3] ^ i), 0)),
                     ANY,
                 ],
                 out_specs=[whole(message)] * chips,
@@ -350,8 +379,10 @@
 
     def gather(received, after):
         step = 4
+        rows = received[0].shape[0] // kept
+        message = (rows * (sent + 1), width)
         return pl.pallas_call(
-            functools.partial(gather_body, kept=kept, sent=sent, rows=step),
+            functools.partial(gather_body, kept=kept, rows=step),
             grid_spec=pltpu.PrefetchScalarGridSpec(
                 num_scalar_prefetch=1,
                 grid=(rows // step,),
@@ -360,34 +391,45 @@
                 + [ANY],
                 out_specs=[
                     pl.BlockSpec((step, retained, width), lambda i, _: (i, 0, 0)),
-                    pl.BlockSpec((step * sent, width), lambda i, _: (i, 0)),
+                    whole(message),
                 ],
+                scratch_shapes=[pltpu.VMEM((rows, width), F32)],
             ),
             out_shape=[
                 jax.ShapeDtypeStruct((rows, retained, width), F32),
-                jax.ShapeDtypeStruct((rows * sent, width), BF16),
+                jax.ShapeDtypeStruct(message, BF16),
             ],
             compiler_params=params(),
             cost_estimate=cost(5),
             name="half_sums",
         )(place, jnp.asarray(local_upper), jnp.asarray(local_lower), *received, after)
 
-    def join(own, received, after):
+    def join(pieces, after):
         step = 4
-        block = rows * per_owner
+        turns, specs, start = [], [], 0
+        for own, message in pieces:
+            count = own.shape[0] // step
+
+            def turn(i, start=start, count=count):
+                return jnp.clip(i - start, 0, count - 1)
+
+            specs.append(pl.BlockSpec((step, retained, width), lambda i, _, turn=turn: (turn(i), 0, 0)))
+            specs.append(whole(message.shape))
+            turns.append((start, count))
+            start += count
+        block = start * step * per_owner
         return pl.pallas_call(
-            functools.partial(join_body, sent=sent, rows=step),
+            functools.partial(join_body, sent=sent, rows=step, turns=turns),
             grid_spec=pltpu.PrefetchScalarGridSpec(
                 num_scalar_prefetch=1,
-                grid=(rows // step,),
+                grid=(start,),
                 in_specs=[
                     chosen(join_upper, lambda p: p[1]),
                     chosen(join_lower, lambda p: p[1]),
                     whole(axial_forward.shape),
-                    pl.BlockSpec((step, retained, width), lambda i, _: (i, 0, 0)),
-                    pl.BlockSpec((step * sent, width), lambda i, _: (i, 0)),
-                    ANY,
-                ],
+                ]
+                + specs
+                + [ANY],
                 out_specs=whole((owners, block + 16, width)),
                 scratch_shapes=[pltpu.VMEM((owners, block, width), F32)],
             ),
@@ -395,7 +437,14 @@
             compiler_params=params(),
             cost_estimate=cost(6),
             name="modal_axial_coefficients",
-        )(place, jnp.asarray(join_upper), jnp.asarray(join_lower), axial_forward, own, received, after)
+        )(
+            place,
+            jnp.asarray(join_upper),
+            jnp.asarray(join_lower),
+            axial_forward,
+            *[value for piece in pieces for value in piece],
+            after,
+        )
 
     out_shape = jax.ShapeDtypeStruct((fields, own_modes * radial_devices, 2, radial_block, width), F32)
     each = 2
@@ -403,36 +452,40 @@
     out_block = (1, each, 2, radial_block, width)
     send_rows = radial + 16
 
-    def solve(field, received, out, after):
+    def solve(field, modes, received, out, after):
         carried = [] if out is None else [out]
-        first = 9
+        begin = modes[0] // each
+        count = len(modes) // each
         return pl.pallas_call(
             functools.partial(
-                solve_body, field=field, radial_devices=radial_devices, modes=own_modes
+                solve_body,
+                field=field,
+                radial_devices=radial_devices,
+                modes=own_modes,
+                first_mode=modes[0],
+                pieces=len(received),
             ),
             grid_spec=pltpu.PrefetchScalarGridSpec(
                 num_scalar_prefetch=1,
-                grid=(turns,),
+                grid=(count,),
                 in_specs=[
                     SMEM,
                     whole(axial_eigen.shape),
-                    pl.BlockSpec((each, 1, radial), lambda i, _: (i, 0, 0)),
+                    pl.BlockSpec((each, 1, radial), lambda i, _: (begin + i, 0, 0)),
                     whole(axial_inverse_map.shape),
-                    pl.BlockSpec((each, radial, radial), lambda i, _: (i, 0, 0)),
-                    pl.BlockSpec((each, radial, radial), lambda i, _: (i, 0, 0)),
-                    whole(received.shape),
+                    pl.BlockSpec((each, radial, radial), lambda i, _: (begin + i, 0, 0)),
+                    pl.BlockSpec((each, radial, radial), lambda i, _: (begin + i, 0, 0)),
                 ]
+                + [whole(piece.shape) for piece in received]
                 + [ANY] * (1 + len(carried)),
                 out_specs=[
-                    pl.BlockSpec(out_block, lambda i, y: (field, y[0] * turns + i, 0, 0, 0)),
+                    pl.BlockSpec(out_block, lambda i, y: (field, y[0] * turns + begin + i, 0, 0, 0)),
                     pl.BlockSpec((each, send_rows, width), lambda i, _: (i, 0, 0)),
                 ],
-                scratch_shapes=[
-                    pltpu.VMEM((width // 128, radial * per_owner, 128), F32)
-                ],
+                scratch_shapes=[pltpu.VMEM((width // 128, radial * per_owner, 128), F32)],
             ),
-            out_shape=[out_shape, jax.ShapeDtypeStruct((own_modes, send_rows, width), BF16)],
-            input_output_aliases={first: 0} if carried else {},
+            out_shape=[out_shape, jax.ShapeDtypeStruct((len(modes), send_rows, width), BF16)],
+            input_output_aliases={8 + len(received): 0} if carried else {},
             compiler_params=params(),
             cost_estimate=cost(7),
             name="radial_solve",
@@ -444,24 +497,25 @@
             axial_inverse_map,
             radial_forward,
             radial_backward,
-            received,
+            *received,
             after,
             *carried,
         )
 
-    def finish(field, received, out, after):
+    def finish(field, modes, received, out, after):
+        begin = modes[0] // each
         return pl.pallas_call(
             finish_body,
             grid_spec=pltpu.PrefetchScalarGridSpec(
                 num_scalar_prefetch=1,
-                grid=(turns,),
+                grid=(len(modes) // each,),
                 in_specs=[
                     pl.BlockSpec((each, send_rows, width), lambda i, _: (i, 0, 0)),
                     ANY,
                     ANY,
                 ],
                 out_specs=pl.BlockSpec(
-                    out_block, lambda i, y: (field, (1 - y[0]) * turns + i, 0, 0, 0)
+                    out_block, lambda i, y: (field, (1 - y[0]) * turns + begin + i, 0, 0, 0)
                 ),
             ),
             out_shape=out_shape,
@@ -505,34 +559,54 @@
     def partner(values):
         return lax.ppermute(values, "rad", [(0, 1), (1, 0)])
 
-    windows, own, away, spectra, partners = {}, {}, {}, {}, {}
-    swapped = {}
+    both = (0, 1)
+    every = tuple(range(own_modes))
+    head, tail = every[: own_modes // 2], every[own_modes // 2 :]
+    steps = [
+        ("rows", 0, both),
+        ("rows", 1, both),
+        ("encode", 0, both),
+        ("rows", 2, both),
+        ("encode", 1, both),
+        ("gather", 0, both),
+        ("encode", 2, both),
+        ("gather", 1, both),
+        ("join", 0, (both,)),
+        ("gather", 2, both),
+        ("join", 1, (both,)),
+        ("solve", 0, every),
+        ("join", 2, (both,)),
+        ("solve", 1, every),
+        ("finish", 0, every),
+        ("solve", 2, head),
+        ("solve", 2, tail),
+        ("finish", 1, every),
+        ("finish", 2, head),
+        ("finish", 2, tail),
+    ]
+    swapped, windows, own, away, partners = {}, {}, {}, {}, {}
+    spectra = {field: [] for field in range(fields)}
     last, out = diffusion, None
-    steps = (
-        ["c0", "c1", "e0", "c2", "e1", "h0", "e2", "h1"]
-        + ["j0", "h2", "j1", "s0", "j2"]
-        + ["s1", "f0", "s2", "f1", "f2"]
-    )
-    for step in steps:
-        field = int(step[1])
-        if step[0] == "c":
+    for name, field, which in steps:
+        key = (field, which)
+        if name == "rows":
             last = other_rows(field, last)
             swapped[field] = flip(last, 1)
-        elif step[0] == "e":
-            made = encode(field, swapped[field], last)
+        elif name == "encode":
+            made = encode(field, which, swapped[field], last)
             last = made[0]
-            windows[field] = [last] + [flip(made[j], 2 * j) for j in range(1, chips)]
-        elif step[0] == "h":
-            own[field], last = gather(windows[field], last)
-            away[field] = flip(last, near)
-        elif step[0] == "j":
-            last = join(own[field], away[field], last)
-            spectra[field] = exchange(last, ("modes", "rad"), side_owners)
-        elif step[0] == "s":
-            out, last = solve(field, spectra[field], out, last)
-            partners[field] = partner(last)
+            windows[key] = [last] + [flip(made[j], 2 * j) for j in range(1, chips)]
+        elif name == "gather":
+            own[key], last = gather(windows[key], last)
+            away[key] = flip(last, near)
+        elif name == "join":
+            last = join([(own[field, part], away[field, part]) for part in which], last)
+            spectra[field].append(exchange(last, ("modes", "rad"), side_owners))
+        elif name == "solve":
+            out, last = solve(field, which, spectra[field], out, last)
+            partners[key] = partner(last)
         else:
-            out = finish(field, partners[field], out, last)
+            out = finish(field, which, partners[key], out, last)
     return out
 
 

time: 215 us -> 203 us (0.944)
  waiting for transfers between devices: 54.2 us -> 45.1 us
  Pallas kernels: 111 us -> 107 us
    ppermute x15, waiting for transfers between devices: 24.8 us -> 14.5 us  [flip(): lax.ppermute(values, 'modes', [(i, i ^ bits) for i in range(processors)])]
    all_to_all x3, waiting for transfers between devices: 16.8 us -> 23.8 us  [exchange(): lax.all_to_all(values, names, split_axis=0, concat_axis=0, tiled=True, ax...]
    ppermute x3 -> x4, waiting for transfers between devices: 12.5 us -> 6.76 us  [partner(): return lax.ppermute(values, 'rad', [(0, 1), (1, 0)])]
    pallas_call x9, Pallas kernels: 64.6 us -> 59.8 us  [the longest x3 22.6 us: encode(): pl.pallas_call(functools.partial(encode_body, group=group, kept=kept, par...]
    pallas_call x3 -> x4, Pallas kernels: 25.1 us -> 26.2 us  [solve(): pl.pallas_call(functools.partial(solve_body, field=field, radial_devices=...]
    pallas_call x3 -> x4, Pallas kernels: 8.12 us -> 9.01 us  [finish(): pl.pallas_call(finish_body, grid_spec=pltpu.PrefetchScalarGridSpec(num_sc...]
  transfers between devices with their start and end apart: 21 -> 22, of which waited for: 10 -> 9; matrix products, arithmetic and copies ran while one was open for 0% -> 0% of each run, Pallas kernels for 49% -> 51%
where the time goes in v5:
time: 203 us; the launch traced here: 202 us
  Pallas kernels  107 us (53%)
  starting transfers between devices  46.2 us (23%)
  waiting for transfers between devices  45.1 us (22%)
  local copies, waits for them, and re-layouts  3.54 us (2%)
    all_to_all x3, starting transfers between devices, exchange(): lax.all_to_all(values, names, split_axis=0, concat_axis=0, tiled=True, ax...  27.7 us
    pallas_call x4, Pallas kernels, solve(): pl.pallas_call(functools.partial(solve_body, field=field, radial_devices=...  26.2 us
    all_to_all x3, waiting for transfers between devices, exchange(): lax.all_to_all(values, names, split_axis=0, concat_axis=0, tiled=True, ax...  23.8 us
    pallas_call x3, Pallas kernels, encode(): pl.pallas_call(functools.partial(encode_body, group=group, kept=kept, par...  22.6 us
    pallas_call x3, Pallas kernels, join(): pl.pallas_call(functools.partial(join_body, sent=sent, rows=step, turns=t...  20.6 us
    pallas_call x3, Pallas kernels, gather(): pl.pallas_call(functools.partial(gather_body, kept=kept, rows=step), grid...  16.6 us
    ppermute x15, waiting for transfers between devices, flip(): lax.ppermute(values, 'modes', [(i, i ^ bits) for i in range(processors)])  14.5 us
    ppermute x15, starting transfers between devices, flip(): lax.ppermute(values, 'modes', [(i, i ^ bits) for i in range(processors)])  14.3 us
  transfers between devices with their start and end apart: 22, of which 9 were waited for; matrix products, arithmetic and copies ran while one was open for 0% of the time, Pallas kernels for 51%

profile of v5, /device:TPU:17, one launch (start us, length us, event | category | flops | bytes accessed | tf_op | source)
XLA Modules:
  0.0 201.8 jit_solution(14261319149393791918)
XLA Ops:
  0.1 0.7 copy-done.7
  0.7 2.9 %other_core_rows.3.__ = bf16[64,64,256]{2,1,0:T(8,128)(2,1)S(1)} custom-call(s32[5]{0:T(128)S(1)} %stack.23._.place_ref, bf16[3,64,128,256]{3,2,1,0:T(8,128)(2,1)} %own_ref.5, f32[3]{0:T(128)S(1)} %copy-done.7), custom_call_target="tpu_custom_call" | custom-call | flops 60000002048 | bytes 600000000 | tf_op jit(solution)/shard_map/other_core_rows/pallas_call | solution.py:540
  3.7 0.7 collective-permute-start
  4.5 4.3 %other_core_rows.4.__ = bf16[64,64,256]{2,1,0:T(8,128)(2,1)} custom-call(s32[5]{0:T(128)S(1)} %stack.23._.place_ref, bf16[3,64,128,256]{3,2,1,0:T(8,128)(2,1)} %own_ref.5, bf16[64,64,256]{2,1,0:T(8,128)(2,1)S(1)} %other_core_rows.3.__), custom_call_target="tpu_custom_call" | custom-call | flops 60000002048 | bytes 600000000 | tf_op jit(solution)/shard_map/other_core_rows/pallas_call | solution.py:540
  8.9 7.4 %window_coefficients.3 = (bf16[768,256]{1,0:T(8,128)(2,1)S(1)}, bf16[768,256]{1,0:T(8,128)(2,1)}, bf16[768,256]{1,0:T(8,128)(2,1)}, bf16[768,256]{1,0:T(8,128)(2,1)}) custom-call(s32[5]{0:T(128)S(1)} %stack.23._.place_ref, bf16[2,384,512]{2,1,0:T(8,128)(2,1)S(1)} %copy-done.14, bf16[2,384,512]{2,1,0:T(8,128)(2,1)S(1)} %copy-done.13, ...), custom_call_target="tpu_custom_call" | custom-call | flops 210000003072 | bytes 2100000000 | tf_op jit(solution)/shard_map/window_coefficients/pallas_call | solution.py:347
  16.3 1.2 collective-permute-start.2
  17.5 1.3 collective-permute-start.3
  18.9 4.4 %other_core_rows.5.__ = bf16[64,64,256]{2,1,0:T(8,128)(2,1)} custom-call(s32[5]{0:T(128)S(1)} %stack.23._.place_ref, bf16[3,64,128,256]{3,2,1,0:T(8,128)(2,1)} %own_ref.5, bf16[768,256]{1,0:T(8,128)(2,1)S(1)} %get-tuple-element.31.__.refs_0_), custom_call_target="tpu_custom_call" | custom-call | flops 60000002048 | bytes 600000000 | tf_op jit(solution)/shard_map/other_core_rows/pallas_call | solution.py:540
  23.3 1.3 collective-permute-start.1
  24.7 7.6 %window_coefficients.4 = (bf16[768,256]{1,0:T(8,128)(2,1)S(1)}, bf16[768,256]{1,0:T(8,128)(2,1)}, bf16[768,256]{1,0:T(8,128)(2,1)}, bf16[768,256]{1,0:T(8,128)(2,1)}) custom-call(s32[5]{0:T(128)S(1)} %stack.23._.place_ref, bf16[2,384,512]{2,1,0:T(8,128)(2,1)S(1)} %copy-done.14, bf16[2,384,512]{2,1,0:T(8,128)(2,1)S(1)} %copy-done.13, ...), custom_call_target="tpu_custom_call" | custom-call | flops 210000003072 | bytes 2100000000 | tf_op jit(solution)/shard_map/window_coefficients/pallas_call | solution.py:347
  32.2 1.2 collective-permute-start.10
  33.5 1.3 collective-permute-start.11
  34.9 1.2 collective-permute-done.4.refs_3_
  36.1 5.5 %half_sums.3 = (f32[16,128,256]{2,1,0:T(8,128)S(1)}, bf16[1424,256]{1,0:T(8,128)(2,1)}) custom-call(s32[5]{0:T(128)S(1)} %stack.23._.place_ref, bf16[8,216,192]{2,1,0:T(8,128)(2,1)S(1)} %copy-done.11, bf16[8,216,192]{2,1,0:T(8,128)(2,1)S(1)} %copy-done.9, bf16[768,256]{1,0:T(8,128)(2,1)S(1)} %copy-done.22, bf16[768,256]{1,0:T(8,128)(2,1)} %collective-permute-done.2.refs_1_, ...), custom_call_target="tpu_custom_call" | custom-call | flops 149999992832 | bytes 1500000000 | tf_op jit(solution)/shard_map/half_sums/pallas_call | solution.py:384
  41.8 7.5 %window_coefficients.5 = (bf16[768,256]{1,0:T(8,128)(2,1)S(1)}, bf16[768,256]{1,0:T(8,128)(2,1)}, bf16[768,256]{1,0:T(8,128)(2,1)}, bf16[768,256]{1,0:T(8,128)(2,1)}) custom-call(s32[5]{0:T(128)S(1)} %stack.23._.place_ref, bf16[2,384,512]{2,1,0:T(8,128)(2,1)S(1)} %copy-done.14, bf16[2,384,512]{2,1,0:T(8,128)(2,1)S(1)} %copy-done.13, ...), custom_call_target="tpu_custom_call" | custom-call | flops 210000003072 | bytes 2100000000 | tf_op jit(solution)/shard_map/window_coefficients/pallas_call | solution.py:347
  49.3 1.1 collective-permute-start.6
  50.4 1.3 collective-permute-start.7
  52.0 9.2 %collective-permute-done.12.refs_3_ = bf16[768,256]{1,0:T(8,128)(2,1)} collective-permute-done((bf16[768,256]{1,0:T(8,128)(2,1)}, bf16[768,256]{1,0:T(8,128)(2,1)}, u32[]{:S(2)}, u32[]{:S(2)}) %collective-permute-start.12) | collective-permute-done | bytes 393248 | tf_op jit(solution)/shard_map/ppermute | solution.py:536
  61.1 5.4 %half_sums.4 = (f32[16,128,256]{2,1,0:T(8,128)S(1)}, bf16[1424,256]{1,0:T(8,128)(2,1)}) custom-call(s32[5]{0:T(128)S(1)} %stack.23._.place_ref, bf16[8,216,192]{2,1,0:T(8,128)(2,1)S(1)} %copy-done.11, bf16[8,216,192]{2,1,0:T(8,128)(2,1)S(1)} %copy-done.9, bf16[768,256]{1,0:T(8,128)(2,1)S(1)} %copy-done.30, bf16[768,256]{1,0:T(8,128)(2,1)} %collective-permute-done.10.refs_1_, ...), custom_call_target="tpu_custom_call" | custom-call | flops 149999992832 | bytes 1500000000 | tf_op jit(solution)/shard_map/half_sums/pallas_call | solution.py:384
  66.6 1.3 copy-done.25
  67.9 2.0 collective-permute-start.14
  69.9 1.3 collective-permute-done.9.refs_1_
  71.3 6.9 %modal_axial_coefficients.3.refs_4_ = bf16[16,144,256]{2,1,0:T(8,128)(2,1)} custom-call(s32[5]{0:T(128)S(1)} %stack.23._.place_ref, bf16[2,128,88]{2,1,0:T(8,128)(2,1)S(1)} %copy-done.18, bf16[2,128,88]{2,1,0:T(8,128)(2,1)S(1)} %copy-done.15, f32[256,256]{1,0:T(8,128)S(1)} %copy-done.2, f32[16,128,256]{2,1,0:T(8,128)S(1)} %get-tuple-element.41.refs_0_, ...), custom_call_target="tpu_custom_call" | custom-call | flops 179999997952 | bytes 1800000000 | tf_op jit(solution)/shard_map/modal_axial_coefficients/pallas_call | solution.py:421
  78.2 13.9 %all-to-all-start = ((bf16[16,144,256]{2,1,0:T(8,128)(2,1)}), bf16[16,144,256]{2,1,0:T(8,128)(2,1)}, u32[]{:S(2)}, u32[]{:S(2)}) async-start(bf16[16,144,256]{2,1,0:T(8,128)(2,1)} %modal_axial_coefficients.3.refs_4_), calls=%async_computation | async-start | bytes 2359296 | tf_op jit(solution)/shard_map/all_to_all | solution.py:531
  92.0 2.8 %collective-permute-done.8.refs_3_ = bf16[768,256]{1,0:T(8,128)(2,1)} collective-permute-done((bf16[768,256]{1,0:T(8,128)(2,1)}, bf16[768,256]{1,0:T(8,128)(2,1)}, u32[]{:S(2)}, u32[]{:S(2)}) %collective-permute-start.8) | collective-permute-done | bytes 393248 | tf_op jit(solution)/shard_map/ppermute | solution.py:536
  94.9 5.7 %half_sums.5 = (f32[16,128,256]{2,1,0:T(8,128)S(1)}, bf16[1424,256]{1,0:T(8,128)(2,1)}) custom-call(s32[5]{0:T(128)S(1)} %stack.23._.place_ref, bf16[8,216,192]{2,1,0:T(8,128)(2,1)S(1)} %copy-done.12, bf16[8,216,192]{2,1,0:T(8,128)(2,1)S(1)} %copy-done.10, bf16[768,256]{1,0:T(8,128)(2,1)S(1)} %copy-done.28, bf16[768,256]{1,0:T(8,128)(2,1)} %collective-permute-done.6.refs_1_, ...), custom_call_target="tpu_custom_call" | custom-call | flops 149999992832 | bytes 1500000000 | tf_op jit(solution)/shard_map/half_sums/pallas_call | solution.py:384
  100.6 1.3 copy-done.23
  101.9 2.0 %collective-permute-start.13 = (bf16[1424,256]{1,0:T(8,128)(2,1)}, bf16[1424,256]{1,0:T(8,128)(2,1)}, u32[]{:S(2)}, u32[]{:S(2)}) collective-permute-start(bf16[1424,256]{1,0:T(8,128)(2,1)} %get-tuple-element.47.refs_2_), channel_id=1, source_target_pairs={{0,16},{2,18},{4,20},{6,22},{8,24},{10,26},{12,28},{14,30},{16,0},... | collective-permute-start | bytes 2187272 | tf_op jit(solution)/shard_map/ppermute | solution.py:536
  104.0 6.9 %modal_axial_coefficients.4.rest_1_ = bf16[16,144,256]{2,1,0:T(8,128)(2,1)} custom-call(s32[5]{0:T(128)S(1)} %stack.23._.place_ref, bf16[2,128,88]{2,1,0:T(8,128)(2,1)S(1)} %copy-done.19, bf16[2,128,88]{2,1,0:T(8,128)(2,1)S(1)} %copy-done.16, f32[256,256]{1,0:T(8,128)S(1)} %copy-done.3, f32[16,128,256]{2,1,0:T(8,128)S(1)} %copy-done.26, ...), custom_call_target="tpu_custom_call" | custom-call | flops 179999997952 | bytes 1800000000 | tf_op jit(solution)/shard_map/modal_axial_coefficients/pallas_call | solution.py:421
  110.9 9.7 %all-to-all-done.rest_0_ = bf16[16,144,256]{2,1,0:T(8,128)(2,1)} async-done(((bf16[16,144,256]{2,1,0:T(8,128)(2,1)}), bf16[16,144,256]{2,1,0:T(8,128)(2,1)}, u32[]{:S(2)}, u32[]{:S(2)}) %all-to-all-start) | async-done | bytes 1179680 | tf_op jit(solution)/shard_map/all_to_all | solution.py:531
  120.6 6.6 %all-to-all-start.2 = ((bf16[16,144,256]{2,1,0:T(8,128)(2,1)}), bf16[16,144,256]{2,1,0:T(8,128)(2,1)}, u32[]{:S(2)}, u32[]{:S(2)}) async-start(bf16[16,144,256]{2,1,0:T(8,128)(2,1)} %modal_axial_coefficients.4.rest_1_), calls=%async_computation.2 | async-start | bytes 2359296 | tf_op jit(solution)/shard_map/all_to_all | solution.py:531
  127.3 7.8 %radial_solve.4 = (f32[3,8,2,128,256]{4,3,2,1,0:T(8,128)}, bf16[4,272,256]{2,1,0:T(8,128)(2,1)}) custom-call(s32[5]{0:T(128)S(1)} %stack.23._.place_ref, f32[3]{0:T(128)S(1)} %copy-done.8, f32[1,256]{1,0:T(1,128)S(1)} %bitcast.6, f32[4,1,256]{2,1,0:T(1,128)S(1)} %reshape.7.radial_eigen_ref, f32[256,256]{1,0:T(8,128)S(1)} %copy-done.5, ...), custom_call_target="tpu_custom_call" | custom-call | flops 210000003072 | bytes 2100000000 | tf_op jit(solution)/shard_map/radial_solve/pallas_call | solution.py:459
  135.1 1.4 collective-permute-start.15
  136.5 6.8 %modal_axial_coefficients.5.rest_1_ = bf16[16,144,256]{2,1,0:T(8,128)(2,1)} custom-call(s32[5]{0:T(128)S(1)} %stack.23._.place_ref, bf16[2,128,88]{2,1,0:T(8,128)(2,1)S(1)} %copy-done.20, bf16[2,128,88]{2,1,0:T(8,128)(2,1)S(1)} %copy-done.17, f32[256,256]{1,0:T(8,128)S(1)} %copy-done.4, f32[16,128,256]{2,1,0:T(8,128)S(1)} %copy-done.24, ...), custom_call_target="tpu_custom_call" | custom-call | flops 179999997952 | bytes 1800000000 | tf_op jit(solution)/shard_map/modal_axial_coefficients/pallas_call | solution.py:421
  143.3 7.4 %all-to-all-done.2.rest_0_ = bf16[16,144,256]{2,1,0:T(8,128)(2,1)} async-done(((bf16[16,144,256]{2,1,0:T(8,128)(2,1)}), bf16[16,144,256]{2,1,0:T(8,128)(2,1)}, u32[]{:S(2)}, u32[]{:S(2)}) %all-to-all-start.2) | async-done | bytes 1179680 | tf_op jit(solution)/shard_map/all_to_all | solution.py:531
  150.7 7.3 %all-to-all-start.1 = ((bf16[16,144,256]{2,1,0:T(8,128)(2,1)}), bf16[16,144,256]{2,1,0:T(8,128)(2,1)}, u32[]{:S(2)}, u32[]{:S(2)}) async-start(bf16[16,144,256]{2,1,0:T(8,128)(2,1)} %modal_axial_coefficients.5.rest_1_), calls=%async_computation.1 | async-start | bytes 2359296 | tf_op jit(solution)/shard_map/all_to_all | solution.py:531
  158.0 7.7 %radial_solve.5 = (f32[3,8,2,128,256]{4,3,2,1,0:T(8,128)}, bf16[4,272,256]{2,1,0:T(8,128)(2,1)}) custom-call(s32[5]{0:T(128)S(1)} %stack.23._.place_ref, f32[3]{0:T(128)S(1)} %copy-done.8, f32[1,256]{1,0:T(1,128)S(1)} %bitcast.7, f32[4,1,256]{2,1,0:T(1,128)S(1)} %reshape.7.radial_eigen_ref, ...), custom_call_target="tpu_custom_call", output_to_operand_aliasing={{0}: (9, {})} | custom-call | flops 210000003072 | bytes 2100000000 | tf_op jit(solution)/shard_map/radial_solve/pallas_call | solution.py:459
  165.7 1.4 collective-permute-start.18
  167.1 2.6 %partner_rows.4.rest_2_ = f32[3,8,2,128,256]{4,3,2,1,0:T(8,128)} custom-call(s32[5]{0:T(128)S(1)} %stack.23._.place_ref, bf16[4,272,256]{2,1,0:T(8,128)(2,1)} %collective-permute-done.15.in_ref, f32[3,8,2,128,256]{4,3,2,1,0:T(8,128)} %get-tuple-element.52._, bf16[4,272,256]{2,1,0:T(8,128)(2,1)} %get-tuple-element.51.__.rest_1_), custom_call_target="tpu_custom_call", output_to_operand_aliasing={{}: (2, {})} | custom-call | flops 60000002048 | bytes 600000000 | tf_op jit(solution)/shard_map/partner_rows/pallas_call | solution.py:507
  169.6 6.8 %all-to-all-done.1.rest_0_ = bf16[16,144,256]{2,1,0:T(8,128)(2,1)} async-done(((bf16[16,144,256]{2,1,0:T(8,128)(2,1)}), bf16[16,144,256]{2,1,0:T(8,128)(2,1)}, u32[]{:S(2)}, u32[]{:S(2)}) %all-to-all-start.1) | async-done | bytes 1179680 | tf_op jit(solution)/shard_map/all_to_all | solution.py:531
  176.4 5.4 %radial_solve.6 = (f32[3,8,2,128,256]{4,3,2,1,0:T(8,128)}, bf16[2,272,256]{2,1,0:T(8,128)(2,1)}) custom-call(s32[5]{0:T(128)S(1)} %stack.23._.place_ref, f32[3]{0:T(128)S(1)} %copy-done.8, f32[1,256]{1,0:T(1,128)S(1)} %bitcast.8, f32[4,1,256]{2,1,0:T(1,128)S(1)} %reshape.7.radial_eigen_ref, ...), custom_call_target="tpu_custom_call", output_to_operand_aliasing={{0}: (9, {})} | custom-call | flops 210000003072 | bytes 2100000000 | tf_op jit(solution)/shard_map/radial_solve/pallas_call | solution.py:459
  182.1 5.3 %radial_solve.7 = (f32[3,8,2,128,256]{4,3,2,1,0:T(8,128)}, bf16[2,272,256]{2,1,0:T(8,128)(2,1)S(1)}) custom-call(s32[5]{0:T(128)S(1)} %stack.23._.place_ref, f32[3]{0:T(128)S(1)} %copy-done.8, f32[1,256]{1,0:T(1,128)S(1)} %bitcast.9, f32[4,1,256]{2,1,0:T(1,128)S(1)} %reshape.7.radial_eigen_ref, ...), custom_call_target="tpu_custom_call", output_to_operand_aliasing={{0}: (9, {})} | custom-call | flops 210000003072 | bytes 2100000000 | tf_op jit(solution)/shard_map/radial_solve/pallas_call | solution.py:459
  187.4 1.2 collective-permute-start.16
  188.6 2.6 %partner_rows.5._ = f32[3,8,2,128,256]{4,3,2,1,0:T(8,128)} custom-call(s32[5]{0:T(128)S(1)} %stack.23._.place_ref, bf16[4,272,256]{2,1,0:T(8,128)(2,1)} %collective-permute-done.18.in_ref, f32[3,8,2,128,256]{4,3,2,1,0:T(8,128)} %get-tuple-element.56._, bf16[2,272,256]{2,1,0:T(8,128)(2,1)S(1)} %get-tuple-element.55.__), custom_call_target="tpu_custom_call", output_to_operand_aliasing={{}: (2, {})} | custom-call | flops 60000002048 | bytes 600000000 | tf_op jit(solution)/shard_map/partner_rows/pallas_call | solution.py:507
  191.2 3.3 %collective-permute-done.17.in_ref = bf16[2,272,256]{2,1,0:T(8,128)(2,1)} collective-permute-done((bf16[2,272,256]{2,1,0:T(8,128)(2,1)}, bf16[2,272,256]{2,1,0:T(8,128)(2,1)}, u32[]{:S(2)}, u32[]{:S(2)}) %collective-permute-start.17) | collective-permute-done | bytes 278560 | tf_op jit(solution)/shard_map/ppermute | solution.py:560
  194.5 2.4 %partner_rows.6._ = f32[3,8,2,128,256]{4,3,2,1,0:T(8,128)} custom-call(s32[5]{0:T(128)S(1)} %stack.23._.place_ref, bf16[2,272,256]{2,1,0:T(8,128)(2,1)} %collective-permute-done.17.in_ref, f32[3,8,2,128,256]{4,3,2,1,0:T(8,128)} %partner_rows.5._, bf16[2,272,256]{2,1,0:T(8,128)(2,1)S(1)} %get-tuple-element.55.__), custom_call_target="tpu_custom_call", output_to_operand_aliasing={{}: (2, {})} | custom-call | flops 60000002048 | bytes 600000000 | tf_op jit(solution)/shard_map/partner_rows/pallas_call | solution.py:507
  196.9 3.5 %collective-permute-done.16.in_ref = bf16[2,272,256]{2,1,0:T(8,128)(2,1)S(1)} collective-permute-done((bf16[2,272,256]{2,1,0:T(8,128)(2,1)S(1)}, bf16[2,272,256]{2,1,0:T(8,128)(2,1)S(1)}, u32[]{:S(2)}, u32[]{:S(2)}) %collective-permute-start.16) | collective-permute-done | bytes 278560 | tf_op jit(solution)/shard_map/ppermute | solution.py:560
  200.3 1.4 partner_rows.7
  (82 shorter events, 1.3 us)
Async XLA Ops:
  3.7 5.1 %collective-permute-start = (bf16[64,64,256]{2,1,0:T(8,128)(2,1)S(1)}, bf16[64,64,256]{2,1,0:T(8,128)(2,1)S(1)}, u32[]{:S(2)}, u32[]{:S(2)}) collective-permute-start(bf16[64,64,256]{2,1,0:T(8,128)(2,1)S(1)} %other_core_rows.3.__), channel_id=1, source_target_pairs={{0,2},{2,0},{4,6},{6,4},{8,10},{10,8},{12,14},{14,12},{16,18},{18,... | collective-permute-start | bytes 6291464 | tf_op jit(solution)/shard_map/ppermute | solution.py:536
  8.8 15.8 %collective-permute-start.5 = (bf16[64,64,256]{2,1,0:T(8,128)(2,1)}, bf16[64,64,256]{2,1,0:T(8,128)(2,1)}, u32[]{:S(2)}, u32[]{:S(2)}) collective-permute-start(bf16[64,64,256]{2,1,0:T(8,128)(2,1)} %other_core_rows.4.__), channel_id=1, source_target_pairs={{0,2},{2,0},{4,6},{6,4},{8,10},{10,8},{12,14},{14,12},{16,18},{18,... | collective-permute-start | bytes 6291464 | tf_op jit(solution)/shard_map/ppermute | solution.py:536
  16.3 7.0 %copy-start.21 = (bf16[768,256]{1,0:T(8,128)(2,1)}, bf16[768,256]{1,0:T(8,128)(2,1)S(1)}, u32[]{:S(2)}) copy-start(bf16[768,256]{1,0:T(8,128)(2,1)S(1)} %get-tuple-element.31.__.refs_0_) | copy-start | bytes 1179652
  16.3 17.2 %collective-permute-start.2 = (bf16[768,256]{1,0:T(8,128)(2,1)}, bf16[768,256]{1,0:T(8,128)(2,1)}, u32[]{:S(2)}, u32[]{:S(2)}) collective-permute-start(bf16[768,256]{1,0:T(8,128)(2,1)} %get-tuple-element.32), channel_id=1, source_target_pairs={{0,4},{2,6},{4,0},{6,2},{8,12},{10,14},{12,8},{14,10},{16,20},{18,... | collective-permute-start | bytes 1179656 | tf_op jit(solution)/shard_map/ppermute | solution.py:536
  17.5 17.3 %collective-permute-start.3 = (bf16[768,256]{1,0:T(8,128)(2,1)}, bf16[768,256]{1,0:T(8,128)(2,1)}, u32[]{:S(2)}, u32[]{:S(2)}) collective-permute-start(bf16[768,256]{1,0:T(8,128)(2,1)} %get-tuple-element.33), channel_id=1, source_target_pairs={{0,8},{2,10},{4,12},{6,14},{8,0},{10,2},{12,4},{14,6},{16,24},{18,... | collective-permute-start | bytes 1179656 | tf_op jit(solution)/shard_map/ppermute | solution.py:536
  18.8 17.3 %collective-permute-start.4 = (bf16[768,256]{1,0:T(8,128)(2,1)}, bf16[768,256]{1,0:T(8,128)(2,1)}, u32[]{:S(2)}, u32[]{:S(2)}) collective-permute-start(bf16[768,256]{1,0:T(8,128)(2,1)} %get-tuple-element.34), channel_id=1, source_target_pairs={{0,12},{2,14},{4,8},{6,10},{8,4},{10,6},{12,0},{14,2},{16,28},{18,... | collective-permute-start | bytes 1179656 | tf_op jit(solution)/shard_map/ppermute | solution.py:536
  23.3 18.5 %collective-permute-start.1 = (bf16[64,64,256]{2,1,0:T(8,128)(2,1)}, bf16[64,64,256]{2,1,0:T(8,128)(2,1)}, u32[]{:S(2)}, u32[]{:S(2)}) collective-permute-start(bf16[64,64,256]{2,1,0:T(8,128)(2,1)} %other_core_rows.5.__), channel_id=1, source_target_pairs={{0,2},{2,0},{4,6},{6,4},{8,10},{10,8},{12,14},{14,12},{16,18},{18,... | collective-permute-start | bytes 6291464 | tf_op jit(solution)/shard_map/ppermute | solution.py:536
  24.6 11.4 %copy-start.9 = (bf16[8,216,192]{2,1,0:T(8,128)(2,1)S(1)}, bf16[8,216,192]{2,1,0:T(8,128)(2,1)}, u32[]{:S(2)}) copy-start(bf16[8,216,192]{2,1,0:T(8,128)(2,1)} %constant.67.clone.lower_ref) | copy-start | bytes 1990660
  24.6 11.4 %copy-start.11 = (bf16[8,216,192]{2,1,0:T(8,128)(2,1)S(1)}, bf16[8,216,192]{2,1,0:T(8,128)(2,1)}, u32[]{:S(2)}) copy-start(bf16[8,216,192]{2,1,0:T(8,128)(2,1)} %constant.66.clone.upper_ref) | copy-start | bytes 1990660
  24.6 11.4 %copy-start.22 = (bf16[768,256]{1,0:T(8,128)(2,1)S(1)}, bf16[768,256]{1,0:T(8,128)(2,1)}, u32[]{:S(2)}) copy-start(bf16[768,256]{1,0:T(8,128)(2,1)} %copy-done.21) | copy-start | bytes 1179652
  32.2 9.3 %copy-start.29 = (bf16[768,256]{1,0:T(8,128)(2,1)}, bf16[768,256]{1,0:T(8,128)(2,1)S(1)}, u32[]{:S(2)}) copy-start(bf16[768,256]{1,0:T(8,128)(2,1)S(1)} %get-tuple-element.35.refs_4_.refs_0_) | copy-start | bytes 1179652
  32.2 18.1 %collective-permute-start.10 = (bf16[768,256]{1,0:T(8,128)(2,1)}, bf16[768,256]{1,0:T(8,128)(2,1)}, u32[]{:S(2)}, u32[]{:S(2)}) collective-permute-start(bf16[768,256]{1,0:T(8,128)(2,1)} %get-tuple-element.42), channel_id=1, source_target_pairs={{0,4},{2,6},{4,0},{6,2},{8,12},{10,14},{12,8},{14,10},{16,20},{18,... | collective-permute-start | bytes 1179656 | tf_op jit(solution)/shard_map/ppermute | solution.py:536
  33.5 18.2 %collective-permute-start.11 = (bf16[768,256]{1,0:T(8,128)(2,1)}, bf16[768,256]{1,0:T(8,128)(2,1)}, u32[]{:S(2)}, u32[]{:S(2)}) collective-permute-start(bf16[768,256]{1,0:T(8,128)(2,1)} %get-tuple-element.43), channel_id=1, source_target_pairs={{0,8},{2,10},{4,12},{6,14},{8,0},{10,2},{12,4},{14,6},{16,24},{18,... | collective-permute-start | bytes 1179656 | tf_op jit(solution)/shard_map/ppermute | solution.py:536
  34.8 26.4 %collective-permute-start.12 = (bf16[768,256]{1,0:T(8,128)(2,1)}, bf16[768,256]{1,0:T(8,128)(2,1)}, u32[]{:S(2)}, u32[]{:S(2)}) collective-permute-start(bf16[768,256]{1,0:T(8,128)(2,1)} %get-tuple-element.44), channel_id=1, source_target_pairs={{0,12},{2,14},{4,8},{6,10},{8,4},{10,6},{12,0},{14,2},{16,28},{18,... | collective-permute-start | bytes 1179656 | tf_op jit(solution)/shard_map/ppermute | solution.py:536
  41.6 29.7 %collective-permute-start.9 = (bf16[1424,256]{1,0:T(8,128)(2,1)}, bf16[1424,256]{1,0:T(8,128)(2,1)}, u32[]{:S(2)}, u32[]{:S(2)}) collective-permute-start(bf16[1424,256]{1,0:T(8,128)(2,1)} %get-tuple-element.36.__), channel_id=1, source_target_pairs={{0,16},{2,18},{4,20},{6,22},{8,24},{10,26},{12,28},{14,30},{16,0},... | collective-permute-start | bytes 2187272 | tf_op jit(solution)/shard_map/ppermute | solution.py:536
  41.8 19.4 %copy-start.30 = (bf16[768,256]{1,0:T(8,128)(2,1)S(1)}, bf16[768,256]{1,0:T(8,128)(2,1)}, u32[]{:S(2)}) copy-start(bf16[768,256]{1,0:T(8,128)(2,1)} %copy-done.29) | copy-start | bytes 1179652
  49.3 17.3 %copy-start.27 = (bf16[768,256]{1,0:T(8,128)(2,1)}, bf16[768,256]{1,0:T(8,128)(2,1)S(1)}, u32[]{:S(2)}) copy-start(bf16[768,256]{1,0:T(8,128)(2,1)S(1)} %get-tuple-element.37.refs_4_.refs_0_) | copy-start | bytes 1179652
  49.3 42.7 %collective-permute-start.6 = (bf16[768,256]{1,0:T(8,128)(2,1)}, bf16[768,256]{1,0:T(8,128)(2,1)}, u32[]{:S(2)}, u32[]{:S(2)}) collective-permute-start(bf16[768,256]{1,0:T(8,128)(2,1)} %get-tuple-element.38), channel_id=1, source_target_pairs={{0,4},{2,6},{4,0},{6,2},{8,12},{10,14},{12,8},{14,10},{16,20},{18,... | collective-permute-start | bytes 1179656 | tf_op jit(solution)/shard_map/ppermute | solution.py:536
  50.4 41.7 %collective-permute-start.7 = (bf16[768,256]{1,0:T(8,128)(2,1)}, bf16[768,256]{1,0:T(8,128)(2,1)}, u32[]{:S(2)}, u32[]{:S(2)}) collective-permute-start(bf16[768,256]{1,0:T(8,128)(2,1)} %get-tuple-element.39), channel_id=1, source_target_pairs={{0,8},{2,10},{4,12},{6,14},{8,0},{10,2},{12,4},{14,6},{16,24},{18,... | collective-permute-start | bytes 1179656 | tf_op jit(solution)/shard_map/ppermute | solution.py:536
  51.7 43.2 %collective-permute-start.8 = (bf16[768,256]{1,0:T(8,128)(2,1)}, bf16[768,256]{1,0:T(8,128)(2,1)}, u32[]{:S(2)}, u32[]{:S(2)}) collective-permute-start(bf16[768,256]{1,0:T(8,128)(2,1)} %get-tuple-element.40), channel_id=1, source_target_pairs={{0,12},{2,14},{4,8},{6,10},{8,4},{10,6},{12,0},{14,2},{16,28},{18,... | collective-permute-start | bytes 1179656 | tf_op jit(solution)/shard_map/ppermute | solution.py:536
  61.1 10.1 %copy-start.2 = (f32[256,256]{1,0:T(8,128)S(1)}, f32[256,256]{1,0:T(8,128)}, u32[]{:S(2)}) copy-start(f32[256,256]{1,0:T(8,128)} %axial_ref.10) | copy-start | bytes 786436
  61.1 10.1 %copy-start.15 = (bf16[2,128,88]{2,1,0:T(8,128)(2,1)S(1)}, bf16[2,128,88]{2,1,0:T(8,128)(2,1)}, u32[]{:S(2)}) copy-start(bf16[2,128,88]{2,1,0:T(8,128)(2,1)} %constant.69.clone.lower_ref) | copy-start | bytes 135172
  61.1 10.1 %copy-start.18 = (bf16[2,128,88]{2,1,0:T(8,128)(2,1)S(1)}, bf16[2,128,88]{2,1,0:T(8,128)(2,1)}, u32[]{:S(2)}) copy-start(bf16[2,128,88]{2,1,0:T(8,128)(2,1)} %constant.68.clone.upper_ref) | copy-start | bytes 135172
  67.9 36.1 %collective-permute-start.14 = (bf16[1424,256]{1,0:T(8,128)(2,1)}, bf16[1424,256]{1,0:T(8,128)(2,1)}, u32[]{:S(2)}, u32[]{:S(2)}) collective-permute-start(bf16[1424,256]{1,0:T(8,128)(2,1)} %get-tuple-element.45.refs_2_), channel_id=1, source_target_pairs={{0,16},{2,18},{4,20},{6,22},{8,24},{10,26},{12,28},{14,30},{16,0},... | collective-permute-start | bytes 2187272 | tf_op jit(solution)/shard_map/ppermute | solution.py:536
  78.2 16.7 %copy-start.10 = (bf16[8,216,192]{2,1,0:T(8,128)(2,1)S(1)}, bf16[8,216,192]{2,1,0:T(8,128)(2,1)}, u32[]{:S(2)}) copy-start(bf16[8,216,192]{2,1,0:T(8,128)(2,1)} %constant.67.clone.lower_ref) | copy-start | bytes 1990660
  78.2 16.7 %copy-start.12 = (bf16[8,216,192]{2,1,0:T(8,128)(2,1)S(1)}, bf16[8,216,192]{2,1,0:T(8,128)(2,1)}, u32[]{:S(2)}) copy-start(bf16[8,216,192]{2,1,0:T(8,128)(2,1)} %constant.66.clone.upper_ref) | copy-start | bytes 1990660
  78.2 16.7 %copy-start.28 = (bf16[768,256]{1,0:T(8,128)(2,1)S(1)}, bf16[768,256]{1,0:T(8,128)(2,1)}, u32[]{:S(2)}) copy-start(bf16[768,256]{1,0:T(8,128)(2,1)} %copy-done.27) | copy-start | bytes 1179652
  78.2 42.5 %all-to-all-start = ((bf16[16,144,256]{2,1,0:T(8,128)(2,1)}), bf16[16,144,256]{2,1,0:T(8,128)(2,1)}, u32[]{:S(2)}, u32[]{:S(2)}) async-start(bf16[16,144,256]{2,1,0:T(8,128)(2,1)} %modal_axial_coefficients.3.refs_4_), calls=%async_computation | async-start | bytes 2359296 | tf_op jit(solution)/shard_map/all_to_all | solution.py:531
  94.9 9.1 %copy-start.3 = (f32[256,256]{1,0:T(8,128)S(1)}, f32[256,256]{1,0:T(8,128)}, u32[]{:S(2)}) copy-start(f32[256,256]{1,0:T(8,128)} %axial_ref.10) | copy-start | bytes 786436
  94.9 9.1 %copy-start.16 = (bf16[2,128,88]{2,1,0:T(8,128)(2,1)S(1)}, bf16[2,128,88]{2,1,0:T(8,128)(2,1)}, u32[]{:S(2)}) copy-start(bf16[2,128,88]{2,1,0:T(8,128)(2,1)} %constant.69.clone.lower_ref) | copy-start | bytes 135172
  94.9 9.1 %copy-start.19 = (bf16[2,128,88]{2,1,0:T(8,128)(2,1)S(1)}, bf16[2,128,88]{2,1,0:T(8,128)(2,1)}, u32[]{:S(2)}) copy-start(bf16[2,128,88]{2,1,0:T(8,128)(2,1)} %constant.68.clone.upper_ref) | copy-start | bytes 135172
  94.9 9.1 %copy-start.26 = (f32[16,128,256]{2,1,0:T(8,128)S(1)}, f32[16,128,256]{2,1,0:T(8,128)}, u32[]{:S(2)}) copy-start(f32[16,128,256]{2,1,0:T(8,128)} %copy-done.25) | copy-start | bytes 6291460
  101.9 34.5 %collective-permute-start.13 = (bf16[1424,256]{1,0:T(8,128)(2,1)}, bf16[1424,256]{1,0:T(8,128)(2,1)}, u32[]{:S(2)}, u32[]{:S(2)}) collective-permute-start(bf16[1424,256]{1,0:T(8,128)(2,1)} %get-tuple-element.47.refs_2_), channel_id=1, source_target_pairs={{0,16},{2,18},{4,20},{6,22},{8,24},{10,26},{12,28},{14,30},{16,0},... | collective-permute-start | bytes 2187272 | tf_op jit(solution)/shard_map/ppermute | solution.py:536
  110.9 16.3 %copy-start = (f32[4,256,256]{2,1,0:T(8,128)S(1)}, f32[4,256,256]{2,1,0:T(8,128)}, u32[]{:S(2)}) copy-start(f32[4,256,256]{2,1,0:T(8,128)} %forward_ref.7) | copy-start | bytes 3145732
  110.9 16.3 %copy-start.1 = (f32[4,256,256]{2,1,0:T(8,128)S(1)}, f32[4,256,256]{2,1,0:T(8,128)}, u32[]{:S(2)}) copy-start(f32[4,256,256]{2,1,0:T(8,128)} %backward_ref.7) | copy-start | bytes 3145732
  110.9 16.3 %copy-start.5 = (f32[256,256]{1,0:T(8,128)S(1)}, f32[256,256]{1,0:T(8,128)}, u32[]{:S(2)}) copy-start(f32[256,256]{1,0:T(8,128)} %axial_ref.13) | copy-start | bytes 786436
  110.9 16.3 %copy-start.6 = (f32[256]{0:T(256)S(1)}, f32[256]{0:T(256)}, u32[]{:S(2)}) copy-start(f32[256]{0:T(256)} %param.18) | copy-start | bytes 3076
  110.9 16.3 %copy-start.8 = (f32[3]{0:T(128)S(1)}, f32[3]{0:T(128)}, u32[]{:S(2)}) copy-start(f32[3]{0:T(128)} %diffusion_ref.7) | copy-start | bytes 40
  120.6 30.1 %all-to-all-start.2 = ((bf16[16,144,256]{2,1,0:T(8,128)(2,1)}), bf16[16,144,256]{2,1,0:T(8,128)(2,1)}, u32[]{:S(2)}, u32[]{:S(2)}) async-start(bf16[16,144,256]{2,1,0:T(8,128)(2,1)} %modal_axial_coefficients.4.rest_1_), calls=%async_computation.2 | async-start | bytes 2359296 | tf_op jit(solution)/shard_map/all_to_all | solution.py:531
  127.2 9.2 %copy-start.4 = (f32[256,256]{1,0:T(8,128)S(1)}, f32[256,256]{1,0:T(8,128)}, u32[]{:S(2)}) copy-start(f32[256,256]{1,0:T(8,128)} %axial_ref.10) | copy-start | bytes 786436
  127.2 9.2 %copy-start.17 = (bf16[2,128,88]{2,1,0:T(8,128)(2,1)S(1)}, bf16[2,128,88]{2,1,0:T(8,128)(2,1)}, u32[]{:S(2)}) copy-start(bf16[2,128,88]{2,1,0:T(8,128)(2,1)} %constant.69.clone.lower_ref) | copy-start | bytes 135172
  127.2 9.2 %copy-start.20 = (bf16[2,128,88]{2,1,0:T(8,128)(2,1)S(1)}, bf16[2,128,88]{2,1,0:T(8,128)(2,1)}, u32[]{:S(2)}) copy-start(bf16[2,128,88]{2,1,0:T(8,128)(2,1)} %constant.68.clone.upper_ref) | copy-start | bytes 135172
  127.3 9.2 %copy-start.24 = (f32[16,128,256]{2,1,0:T(8,128)S(1)}, f32[16,128,256]{2,1,0:T(8,128)}, u32[]{:S(2)}) copy-start(f32[16,128,256]{2,1,0:T(8,128)} %copy-done.23) | copy-start | bytes 6291460
  135.1 32.0 %collective-permute-start.15 = (bf16[4,272,256]{2,1,0:T(8,128)(2,1)}, bf16[4,272,256]{2,1,0:T(8,128)(2,1)}, u32[]{:S(2)}, u32[]{:S(2)}) collective-permute-start(bf16[4,272,256]{2,1,0:T(8,128)(2,1)} %get-tuple-element.49.refs_2_), channel_id=1, source_target_pairs={{0,1},{1,0},{2,3},{3,2},{4,5},{5,4},{6,7},{7,6},{8,9},{9,8},{10,11... | collective-permute-start | bytes 1671176 | tf_op jit(solution)/shard_map/ppermute | solution.py:560
  150.7 25.7 %all-to-all-start.1 = ((bf16[16,144,256]{2,1,0:T(8,128)(2,1)}), bf16[16,144,256]{2,1,0:T(8,128)(2,1)}, u32[]{:S(2)}, u32[]{:S(2)}) async-start(bf16[16,144,256]{2,1,0:T(8,128)(2,1)} %modal_axial_coefficients.5.rest_1_), calls=%async_computation.1 | async-start | bytes 2359296 | tf_op jit(solution)/shard_map/all_to_all | solution.py:531
  165.7 22.9 %collective-permute-start.18 = (bf16[4,272,256]{2,1,0:T(8,128)(2,1)}, bf16[4,272,256]{2,1,0:T(8,128)(2,1)}, u32[]{:S(2)}, u32[]{:S(2)}) collective-permute-start(bf16[4,272,256]{2,1,0:T(8,128)(2,1)} %get-tuple-element.51.__.rest_1_), channel_id=1, source_target_pairs={{0,1},{1,0},{2,3},{3,2},{4,5},{5,4},{6,7},{7,6},{8,9},{9,8},{10,11... | collective-permute-start | bytes 1671176 | tf_op jit(solution)/shard_map/ppermute | solution.py:560
  181.8 12.6 %collective-permute-start.17 = (bf16[2,272,256]{2,1,0:T(8,128)(2,1)}, bf16[2,272,256]{2,1,0:T(8,128)(2,1)}, u32[]{:S(2)}, u32[]{:S(2)}) collective-permute-start(bf16[2,272,256]{2,1,0:T(8,128)(2,1)} %get-tuple-element.53.rest_1_), channel_id=1, source_target_pairs={{0,1},{1,0},{2,3},{3,2},{4,5},{5,4},{6,7},{7,6},{8,9},{9,8},{10,11... | collective-permute-start | bytes 835592 | tf_op jit(solution)/shard_map/ppermute | solution.py:560
  187.4 12.9 %collective-permute-start.16 = (bf16[2,272,256]{2,1,0:T(8,128)(2,1)S(1)}, bf16[2,272,256]{2,1,0:T(8,128)(2,1)S(1)}, u32[]{:S(2)}, u32[]{:S(2)}) collective-permute-start(bf16[2,272,256]{2,1,0:T(8,128)(2,1)S(1)} %get-tuple-element.55.__), channel_id=1, source_target_pairs={{0,1},{1,0},{2,3},{3,2},{4,5},{5,4},{6,7},{7,6},{8,9},{9,8},{10,11... | collective-permute-start | bytes 835592 | tf_op jit(solution)/shard_map/ppermute | solution.py:560
  (6 other events, 18.7 us)

commit v6 on v5

--- a/solution.py
+++ b/solution.py
@@ -117,14 +117,14 @@
 
 
 def encode_body(
-    _, own_upper, own_lower, other_upper, other_lower, own_ref, other_ref, __, *out_refs, group, kept, parts
+    _, own_upper, own_lower, other_upper, other_lower, own_ref, other_ref, __, *out_refs, group, kept
 ):
     step = pl.program_id(0)
-    points, _, width = other_ref.shape
+    points, rows, width = other_ref.shape
     blocks = (own_ref[0].astype(F32), other_ref[...].astype(F32))
     tables = ((own_upper[0], own_lower[0]), (other_upper[0], other_lower[0]))
     made = []
-    for part in parts:
+    for part in range(rows // group):
         sums = None
         for block, table in zip(blocks, tables):
             piece = block[:, part * group : (part + 1) * group, :].reshape(points * group, width)
@@ -166,37 +166,28 @@
         send_ref[send_ref.shape[0] - scale_ref.shape[0] :, :] = scale_ref[...].astype(BF16)
 
 
-def join_body(_, upper_ref, lower_ref, axial_ref, *refs, sent, rows, turns):
-    *pieces, __, out_ref, held_ref = refs
+def join_body(
+    _, upper_ref, lower_ref, axial_ref, own_ref, in_ref, __, out_ref, held_ref, *, sent, rows
+):
     step = pl.program_id(0)
     owners, coded_rows, width = out_ref.shape
     block = coded_rows - 16
     table = (upper_ref[0], lower_ref[0])
     axial = split(axial_ref[...])
-
-    def add(own_ref, in_ref, start):
-        total = in_ref.shape[0] // (sent + 1)
-        count = rows * sent
-        local = step - start
-        coded = in_ref[pl.ds(pl.multiple_of(local * count, count), count), :].astype(F32)
-        scales = in_ref[total * sent :, :].astype(F32)
-        place = lax.broadcasted_iota(jnp.int32, scales.shape, 0)
-        for row in range(rows):
-            here = place == local * rows + row
-            scale = jnp.sum(jnp.where(here, scales, 0.0), axis=0, keepdims=True)
-            values = linear_decode(coded[row * sent : (row + 1) * sent], scale)
-            spectrum = own_ref[row] + dot3(table, split(values))
-            axial_coef = dot3(split(spectrum), axial, ROWS_BY_ROWS).reshape(owners, -1, width)
-            each = axial_coef.shape[1]
-            target = pl.multiple_of((step * rows + row) * each, each)
-            held_ref[:, pl.ds(target, each), :] = axial_coef
-
-    if len(turns) == 1:
-        add(*pieces, 0)
-    else:
-        for number, (start, count) in enumerate(turns):
-            here = pieces[2 * number : 2 * number + 2]
-            pl.when((step >= start) & (step < start + count))(functools.partial(add, *here, start))
+    total = in_ref.shape[0] // (sent + 1)
+    count = rows * sent
+    coded = in_ref[pl.ds(pl.multiple_of(step * count, count), count), :].astype(F32)
+    scales = in_ref[total * sent :, :].astype(F32)
+    place = lax.broadcasted_iota(jnp.int32, scales.shape, 0)
+    for row in range(rows):
+        here = place == step * rows + row
+        scale = jnp.sum(jnp.where(here, scales, 0.0), axis=0, keepdims=True)
+        values = linear_decode(coded[row * sent : (row + 1) * sent], scale)
+        spectrum = own_ref[row] + dot3(table, split(values))
+        axial_coef = dot3(split(spectrum), axial, ROWS_BY_ROWS).reshape(owners, -1, width)
+        each = axial_coef.shape[1]
+        target = pl.multiple_of((step * rows + row) * each, each)
+        held_ref[:, pl.ds(target, each), :] = axial_coef
 
     @pl.when(step == pl.num_programs(0) - 1)
     def _():
@@ -215,19 +206,18 @@
     axial_ref,
     forward_ref,
     backward_ref,
+    in_ref,
     *rest,
     field,
     radial_devices,
     modes,
     first_mode,
-    pieces,
 ):
-    in_refs = rest[:pieces]
     out_ref, send_ref, held_ref = rest[-3:]
     step = pl.program_id(0)
     each = forward_ref.shape[0]
-    devices, _, width = in_refs[0].shape
-    rows = sum(ref.shape[1] - 16 for ref in in_refs)
+    devices, coded_rows, width = in_ref.shape
+    rows = coded_rows - 16
     chips = devices // radial_devices // 2
     stride = 2 * modes
 
@@ -236,14 +226,12 @@
         for source in range(devices):
             chip, core, block = source // radial_devices // 2, source // radial_devices % 2, source % radial_devices
             target = (block * 2 + core) * chips + chip
-            start = target * rows
-            for in_ref in in_refs:
-                count = in_ref.shape[1] - 16
-                coded = in_ref[source].astype(F32)
-                values = linear_decode(coded[:count], coded[count : count + 1])
-                for lane in range(width // 128):
-                    held_ref[lane, start : start + count, :] = values[:, lane * 128 : (lane + 1) * 128]
-                start += count
+            coded = in_ref[source].astype(F32)
+            values = linear_decode(coded[:rows], coded[rows : rows + 1])
+            for lane in range(width // 128):
+                held_ref[lane, target * rows : (target + 1) * rows, :] = values[
+                    :, lane * 128 : (lane + 1) * 128
+                ]
 
     radial = devices * rows // stride
     axial = split(axial_ref[...])
@@ -342,27 +330,28 @@
     def chosen(table, index):
         return pl.BlockSpec((1,) + table.shape[1:], lambda i, p: (index(p), 0, 0))
 
-    def encode(field, parts, other, after):
-        message = (len(parts) * group * kept, width)
+    def encode(field, targets, other, after):
+        message = (rows * kept, width)
+        first = targets[0]
         return pl.pallas_call(
-            functools.partial(encode_body, group=group, kept=kept, parts=parts),
+            functools.partial(encode_body, group=group, kept=kept),
             grid_spec=pltpu.PrefetchScalarGridSpec(
                 num_scalar_prefetch=1,
-                grid=(chips,),
+                grid=(len(targets),),
                 in_specs=[
                     chosen(spread_upper, lambda p: p[2]),
                     chosen(spread_lower, lambda p: p[2]),
                     chosen(spread_upper, lambda p: 1 - p[2]),
                     chosen(spread_lower, lambda p: 1 - p[2]),
                     pl.BlockSpec(
-                        (1, slab, rows, width), lambda i, p: (field, 0, p[2] * chips + (p[3] ^ i), 0)
+                        (1, slab, rows, width), lambda i, p: (field, 0, p[2] * chips + (p[3] ^ (first + i)), 0)
                     ),
-                    pl.BlockSpec((slab, rows, width), lambda i, p: (0, (p[3] ^ i), 0)),
+                    pl.BlockSpec((slab, rows, width), lambda i, p: (0, (p[3] ^ (first + i)), 0)),
                     ANY,
                 ],
-                out_specs=[whole(message)] * chips,
+                out_specs=[whole(message)] * len(targets),
             ),
-            out_shape=[jax.ShapeDtypeStruct(message, BF16)] * chips,
+            out_shape=[jax.ShapeDtypeStruct(message, BF16)] * len(targets),
             compiler_params=params(),
             cost_estimate=cost(7),
             name="window_coefficients",
@@ -378,8 +367,7 @@
         )
 
     def gather(received, after):
-        step = 4
-        rows = received[0].shape[0] // kept
+        step = 8
         message = (rows * (sent + 1), width)
         return pl.pallas_call(
             functools.partial(gather_body, kept=kept, rows=step),
@@ -404,32 +392,22 @@
             name="half_sums",
         )(place, jnp.asarray(local_upper), jnp.asarray(local_lower), *received, after)
 
-    def join(pieces, after):
-        step = 4
-        turns, specs, start = [], [], 0
-        for own, message in pieces:
-            count = own.shape[0] // step
-
-            def turn(i, start=start, count=count):
-                return jnp.clip(i - start, 0, count - 1)
-
-            specs.append(pl.BlockSpec((step, retained, width), lambda i, _, turn=turn: (turn(i), 0, 0)))
-            specs.append(whole(message.shape))
-            turns.append((start, count))
-            start += count
-        block = start * step * per_owner
+    def join(own, received, after):
+        step = 8
+        block = rows * per_owner
         return pl.pallas_call(
-            functools.partial(join_body, sent=sent, rows=step, turns=turns),
+            functools.partial(join_body, sent=sent, rows=step),
             grid_spec=pltpu.PrefetchScalarGridSpec(
                 num_scalar_prefetch=1,
-                grid=(start,),
+                grid=(rows // step,),
                 in_specs=[
                     chosen(join_upper, lambda p: p[1]),
                     chosen(join_lower, lambda p: p[1]),
                     whole(axial_forward.shape),
-                ]
-                + specs
-                + [ANY],
+                    pl.BlockSpec((step, retained, width), lambda i, _: (i, 0, 0)),
+                    whole(received.shape),
+                    ANY,
+                ],
                 out_specs=whole((owners, block + 16, width)),
                 scratch_shapes=[pltpu.VMEM((owners, block, width), F32)],
             ),
@@ -442,7 +420,8 @@
             jnp.asarray(join_upper),
             jnp.asarray(join_lower),
             axial_forward,
-            *[value for piece in pieces for value in piece],
+            own,
+            received,
             after,
         )
 
@@ -463,7 +442,6 @@
                 radial_devices=radial_devices,
                 modes=own_modes,
                 first_mode=modes[0],
-                pieces=len(received),
             ),
             grid_spec=pltpu.PrefetchScalarGridSpec(
                 num_scalar_prefetch=1,
@@ -475,8 +453,8 @@
                     whole(axial_inverse_map.shape),
                     pl.BlockSpec((each, radial, radial), lambda i, _: (begin + i, 0, 0)),
                     pl.BlockSpec((each, radial, radial), lambda i, _: (begin + i, 0, 0)),
+                    whole(received.shape),
                 ]
-                + [whole(piece.shape) for piece in received]
                 + [ANY] * (1 + len(carried)),
                 out_specs=[
                     pl.BlockSpec(out_block, lambda i, y: (field, y[0] * turns + begin + i, 0, 0, 0)),
@@ -485,7 +463,7 @@
                 scratch_shapes=[pltpu.VMEM((width // 128, radial * per_owner, 128), F32)],
             ),
             out_shape=[out_shape, jax.ShapeDtypeStruct((len(modes), send_rows, width), BF16)],
-            input_output_aliases={8 + len(received): 0} if carried else {},
+            input_output_aliases={9: 0} if carried else {},
             compiler_params=params(),
             cost_estimate=cost(7),
             name="radial_solve",
@@ -497,7 +475,7 @@
             axial_inverse_map,
             radial_forward,
             radial_backward,
-            *received,
+            received,
             after,
             *carried,
         )
@@ -541,14 +519,14 @@
             rows_body,
             grid_spec=pltpu.PrefetchScalarGridSpec(
                 num_scalar_prefetch=1,
-                grid=(4,),
+                grid=(2,),
                 in_specs=[
                     pl.BlockSpec(
-                        (1, slab // 4) + shape[1:], lambda i, p: (field, i, 1 - p[2], 0)
+                        (1, slab // 2) + shape[1:], lambda i, p: (field, i, 1 - p[2], 0)
                     ),
                     ANY,
                 ],
-                out_specs=pl.BlockSpec((slab // 4,) + shape[1:], lambda i, _: (i, 0, 0)),
+                out_specs=pl.BlockSpec((slab // 2,) + shape[1:], lambda i, _: (i, 0, 0)),
             ),
             out_shape=jax.ShapeDtypeStruct(shape, BF16),
             compiler_params=params(),
@@ -559,23 +537,23 @@
     def partner(values):
         return lax.ppermute(values, "rad", [(0, 1), (1, 0)])
 
-    both = (0, 1)
+    places = tuple(range(chips))
     every = tuple(range(own_modes))
     head, tail = every[: own_modes // 2], every[own_modes // 2 :]
     steps = [
-        ("rows", 0, both),
-        ("rows", 1, both),
-        ("encode", 0, both),
-        ("rows", 2, both),
-        ("encode", 1, both),
-        ("gather", 0, both),
-        ("encode", 2, both),
-        ("gather", 1, both),
-        ("join", 0, (both,)),
-        ("gather", 2, both),
-        ("join", 1, (both,)),
+        ("rows", 0, None),
+        ("rows", 1, None),
+        ("encode", 0, places),
+        ("rows", 2, None),
+        ("encode", 1, places),
+        ("gather", 0, None),
+        ("encode", 2, places),
+        ("gather", 1, None),
+        ("join", 0, None),
+        ("gather", 2, None),
+        ("join", 1, None),
         ("solve", 0, every),
-        ("join", 2, (both,)),
+        ("join", 2, None),
         ("solve", 1, every),
         ("finish", 0, every),
         ("solve", 2, head),
@@ -584,8 +562,8 @@
         ("finish", 2, head),
         ("finish", 2, tail),
     ]
-    swapped, windows, own, away, partners = {}, {}, {}, {}, {}
-    spectra = {field: [] for field in range(fields)}
+    swapped, own, away, spectra, partners = {}, {}, {}, {}, {}
+    windows = {field: {} for field in range(fields)}
     last, out = diffusion, None
     for name, field, which in steps:
         key = (field, which)
@@ -595,13 +573,14 @@
         elif name == "encode":
             made = encode(field, which, swapped[field], last)
             last = made[0]
-            windows[key] = [last] + [flip(made[j], 2 * j) for j in range(1, chips)]
+            for target, message in zip(which, made):
+                windows[field][target] = flip(message, 2 * target) if target else message
         elif name == "gather":
-            own[key], last = gather(windows[key], last)
-            away[key] = flip(last, near)
+            own[field], last = gather([windows[field][j] for j in range(chips)], last)
+            away[field] = flip(last, near)
         elif name == "join":
-            last = join([(own[field, part], away[field, part]) for part in which], last)
-            spectra[field].append(exchange(last, ("modes", "rad"), side_owners))
+            last = join(own[field], away[field], last)
+            spectra[field] = exchange(last, ("modes", "rad"), side_owners)
         elif name == "solve":
             out, last = solve(field, which, spectra[field], out, last)
             partners[key] = partner(last)

time: 203 us -> 202 us (level)
  Pallas kernels: 107 us -> 100 us
  waiting for transfers between devices: 45.1 us -> 49.2 us
    pallas_call x3, Pallas kernels: 11.6 us -> 8.57 us  [other_rows(): pl.pallas_call(rows_body, grid_spec=pltpu.PrefetchScalarGridSpec(num_scal...]
    ppermute x15, waiting for transfers between devices: 14.5 us -> 17.6 us  [flip(): lax.ppermute(values, 'modes', [(i, i ^ bits) for i in range(processors)])]
  transfers between devices with their start and end apart: 22 -> 22, of which waited for: 9 -> 10; matrix products, arithmetic and copies ran while one was open for 0% -> 0% of each run, Pallas kernels for 51% -> 48%
where the time goes in v6:
time: 202 us; the launch traced here: 201 us
  Pallas kernels  100 us (50%)
  waiting for transfers between devices  49.2 us (24%)
  starting transfers between devices  47.3 us (23%)
  local copies, waits for them, and re-layouts  3.54 us (2%)
    all_to_all x3, starting transfers between devices, exchange(): lax.all_to_all(values, names, split_axis=0, concat_axis=0, tiled=True, ax...  28.2 us
    pallas_call x4, Pallas kernels, solve(): pl.pallas_call(functools.partial(solve_body, field=field, radial_devices=...  26.2 us
    all_to_all x3, waiting for transfers between devices, exchange(): lax.all_to_all(values, names, split_axis=0, concat_axis=0, tiled=True, ax...  24.8 us
    pallas_call x3, Pallas kernels, encode(): pl.pallas_call(functools.partial(encode_body, group=group, kept=kept), gr...  22.6 us
    pallas_call x3, Pallas kernels, join(): pl.pallas_call(functools.partial(join_body, sent=sent, rows=step), grid_s...  19.3 us
    ppermute x15, waiting for transfers between devices, flip(): lax.ppermute(values, 'modes', [(i, i ^ bits) for i in range(processors)])  17.6 us
    ppermute x15, starting transfers between devices, flip(): lax.ppermute(values, 'modes', [(i, i ^ bits) for i in range(processors)])  14.9 us
    pallas_call x3, Pallas kernels, gather(): pl.pallas_call(functools.partial(gather_body, kept=kept, rows=step), grid...  14.7 us
  transfers between devices with their start and end apart: 22, of which 10 were waited for; matrix products, arithmetic and copies ran while one was open for 0% of the time, Pallas kernels for 48%

profile of v6, /device:TPU:17, one launch (start us, length us, event | category | flops | bytes accessed | tf_op | source)
XLA Modules:
  0.0 200.6 jit_solution(7575675998221660002)
XLA Ops:
  0.1 0.7 copy-done.7
  0.7 2.2 %other_core_rows.3.__ = bf16[64,64,256]{2,1,0:T(8,128)(2,1)S(1)} custom-call(s32[5]{0:T(128)S(1)} %stack.23._.place_ref, bf16[3,64,128,256]{3,2,1,0:T(8,128)(2,1)} %own_ref.5, f32[3]{0:T(128)S(1)} %copy-done.7), custom_call_target="tpu_custom_call" | custom-call | flops 60000002048 | bytes 600000000 | tf_op jit(solution)/shard_map/other_core_rows/pallas_call | solution.py:518
  3.0 0.7 collective-permute-start
  3.7 3.2 %other_core_rows.4.__ = bf16[64,64,256]{2,1,0:T(8,128)(2,1)} custom-call(s32[5]{0:T(128)S(1)} %stack.23._.place_ref, bf16[3,64,128,256]{3,2,1,0:T(8,128)(2,1)} %own_ref.5, bf16[64,64,256]{2,1,0:T(8,128)(2,1)S(1)} %other_core_rows.3.__), custom_call_target="tpu_custom_call" | custom-call | flops 60000002048 | bytes 600000000 | tf_op jit(solution)/shard_map/other_core_rows/pallas_call | solution.py:518
  7.5 7.4 %window_coefficients.3 = (bf16[768,256]{1,0:T(8,128)(2,1)S(1)}, bf16[768,256]{1,0:T(8,128)(2,1)}, bf16[768,256]{1,0:T(8,128)(2,1)}, bf16[768,256]{1,0:T(8,128)(2,1)}) custom-call(s32[5]{0:T(128)S(1)} %stack.23._.place_ref, bf16[2,384,512]{2,1,0:T(8,128)(2,1)S(1)} %copy-done.14, bf16[2,384,512]{2,1,0:T(8,128)(2,1)S(1)} %copy-done.13, ...), custom_call_target="tpu_custom_call" | custom-call | flops 210000003072 | bytes 2100000000 | tf_op jit(solution)/shard_map/window_coefficients/pallas_call | solution.py:336
  14.9 1.2 collective-permute-start.2
  16.2 1.3 collective-permute-start.3
  17.6 3.2 %other_core_rows.5.__ = bf16[64,64,256]{2,1,0:T(8,128)(2,1)} custom-call(s32[5]{0:T(128)S(1)} %stack.23._.place_ref, bf16[3,64,128,256]{3,2,1,0:T(8,128)(2,1)} %own_ref.5, bf16[768,256]{1,0:T(8,128)(2,1)S(1)} %get-tuple-element.31.__.refs_0_), custom_call_target="tpu_custom_call" | custom-call | flops 60000002048 | bytes 600000000 | tf_op jit(solution)/shard_map/other_core_rows/pallas_call | solution.py:518
  20.8 1.2 collective-permute-start.1
  22.0 7.6 %window_coefficients.4 = (bf16[768,256]{1,0:T(8,128)(2,1)S(1)}, bf16[768,256]{1,0:T(8,128)(2,1)}, bf16[768,256]{1,0:T(8,128)(2,1)}, bf16[768,256]{1,0:T(8,128)(2,1)}) custom-call(s32[5]{0:T(128)S(1)} %stack.23._.place_ref, bf16[2,384,512]{2,1,0:T(8,128)(2,1)S(1)} %copy-done.14, bf16[2,384,512]{2,1,0:T(8,128)(2,1)S(1)} %copy-done.13, ...), custom_call_target="tpu_custom_call" | custom-call | flops 210000003072 | bytes 2100000000 | tf_op jit(solution)/shard_map/window_coefficients/pallas_call | solution.py:336
  29.6 1.2 collective-permute-start.10
  30.8 1.3 collective-permute-start.11
  32.3 2.6 %collective-permute-done.4.refs_3_ = bf16[768,256]{1,0:T(8,128)(2,1)} collective-permute-done((bf16[768,256]{1,0:T(8,128)(2,1)}, bf16[768,256]{1,0:T(8,128)(2,1)}, u32[]{:S(2)}, u32[]{:S(2)}) %collective-permute-start.4) | collective-permute-done | bytes 393248 | tf_op jit(solution)/shard_map/ppermute | solution.py:514
  34.9 4.8 %half_sums.3 = (f32[16,128,256]{2,1,0:T(8,128)S(1)}, bf16[1424,256]{1,0:T(8,128)(2,1)}) custom-call(s32[5]{0:T(128)S(1)} %stack.23._.place_ref, bf16[8,216,192]{2,1,0:T(8,128)(2,1)S(1)} %copy-done.11, bf16[8,216,192]{2,1,0:T(8,128)(2,1)S(1)} %copy-done.9, bf16[768,256]{1,0:T(8,128)(2,1)S(1)} %copy-done.22, bf16[768,256]{1,0:T(8,128)(2,1)} %collective-permute-done.2.refs_1_, ...), custom_call_target="tpu_custom_call" | custom-call | flops 149999992832 | bytes 1500000000 | tf_op jit(solution)/shard_map/half_sums/pallas_call | solution.py:372
  40.0 7.5 %window_coefficients.5 = (bf16[768,256]{1,0:T(8,128)(2,1)S(1)}, bf16[768,256]{1,0:T(8,128)(2,1)}, bf16[768,256]{1,0:T(8,128)(2,1)}, bf16[768,256]{1,0:T(8,128)(2,1)}) custom-call(s32[5]{0:T(128)S(1)} %stack.23._.place_ref, bf16[2,384,512]{2,1,0:T(8,128)(2,1)S(1)} %copy-done.14, bf16[2,384,512]{2,1,0:T(8,128)(2,1)S(1)} %copy-done.13, ...), custom_call_target="tpu_custom_call" | custom-call | flops 210000003072 | bytes 2100000000 | tf_op jit(solution)/shard_map/window_coefficients/pallas_call | solution.py:336
  47.5 1.0 collective-permute-start.6
  48.5 1.4 collective-permute-start.7
  50.2 9.8 %collective-permute-done.12.refs_3_ = bf16[768,256]{1,0:T(8,128)(2,1)} collective-permute-done((bf16[768,256]{1,0:T(8,128)(2,1)}, bf16[768,256]{1,0:T(8,128)(2,1)}, u32[]{:S(2)}, u32[]{:S(2)}) %collective-permute-start.12) | collective-permute-done | bytes 393248 | tf_op jit(solution)/shard_map/ppermute | solution.py:514
  60.0 4.8 %half_sums.4 = (f32[16,128,256]{2,1,0:T(8,128)S(1)}, bf16[1424,256]{1,0:T(8,128)(2,1)}) custom-call(s32[5]{0:T(128)S(1)} %stack.23._.place_ref, bf16[8,216,192]{2,1,0:T(8,128)(2,1)S(1)} %copy-done.11, bf16[8,216,192]{2,1,0:T(8,128)(2,1)S(1)} %copy-done.9, bf16[768,256]{1,0:T(8,128)(2,1)S(1)} %copy-done.30, bf16[768,256]{1,0:T(8,128)(2,1)} %collective-permute-done.10.refs_1_, ...), custom_call_target="tpu_custom_call" | custom-call | flops 149999992832 | bytes 1500000000 | tf_op jit(solution)/shard_map/half_sums/pallas_call | solution.py:372
  64.8 1.3 copy-done.25
  66.1 2.4 %collective-permute-start.14 = (bf16[1424,256]{1,0:T(8,128)(2,1)}, bf16[1424,256]{1,0:T(8,128)(2,1)}, u32[]{:S(2)}, u32[]{:S(2)}) collective-permute-start(bf16[1424,256]{1,0:T(8,128)(2,1)} %get-tuple-element.45.__), channel_id=1, source_target_pairs={{0,16},{2,18},{4,20},{6,22},{8,24},{10,26},{12,28},{14,30},{16,0},... | collective-permute-start | bytes 2187272 | tf_op jit(solution)/shard_map/ppermute | solution.py:514
  68.5 0.8 collective-permute-done.9.in_ref
  69.3 6.4 %modal_axial_coefficients.3.refs_4_ = bf16[16,144,256]{2,1,0:T(8,128)(2,1)} custom-call(s32[5]{0:T(128)S(1)} %stack.23._.place_ref, bf16[2,128,88]{2,1,0:T(8,128)(2,1)S(1)} %copy-done.18, bf16[2,128,88]{2,1,0:T(8,128)(2,1)S(1)} %copy-done.15, f32[256,256]{1,0:T(8,128)S(1)} %copy-done.2, f32[16,128,256]{2,1,0:T(8,128)S(1)} %get-tuple-element.41.own_ref, ...), custom_call_target="tpu_custom_call" | custom-call | flops 179999997952 | bytes 1800000000 | tf_op jit(solution)/shard_map/modal_axial_coefficients/pallas_call | solution.py:398
  75.7 14.2 %all-to-all-start = ((bf16[16,144,256]{2,1,0:T(8,128)(2,1)}), bf16[16,144,256]{2,1,0:T(8,128)(2,1)}, u32[]{:S(2)}, u32[]{:S(2)}) async-start(bf16[16,144,256]{2,1,0:T(8,128)(2,1)} %modal_axial_coefficients.3.refs_4_), calls=%async_computation | async-start | bytes 2359296 | tf_op jit(solution)/shard_map/all_to_all | solution.py:509
  90.0 3.8 %collective-permute-done.8.refs_3_ = bf16[768,256]{1,0:T(8,128)(2,1)} collective-permute-done((bf16[768,256]{1,0:T(8,128)(2,1)}, bf16[768,256]{1,0:T(8,128)(2,1)}, u32[]{:S(2)}, u32[]{:S(2)}) %collective-permute-start.8) | collective-permute-done | bytes 393248 | tf_op jit(solution)/shard_map/ppermute | solution.py:514
  93.8 5.1 %half_sums.5 = (f32[16,128,256]{2,1,0:T(8,128)S(1)}, bf16[1424,256]{1,0:T(8,128)(2,1)}) custom-call(s32[5]{0:T(128)S(1)} %stack.23._.place_ref, bf16[8,216,192]{2,1,0:T(8,128)(2,1)S(1)} %copy-done.12, bf16[8,216,192]{2,1,0:T(8,128)(2,1)S(1)} %copy-done.10, bf16[768,256]{1,0:T(8,128)(2,1)S(1)} %copy-done.28, bf16[768,256]{1,0:T(8,128)(2,1)} %collective-permute-done.6.refs_1_, ...), custom_call_target="tpu_custom_call" | custom-call | flops 149999992832 | bytes 1500000000 | tf_op jit(solution)/shard_map/half_sums/pallas_call | solution.py:372
  98.8 1.3 copy-done.23
  100.2 2.4 %collective-permute-start.13 = (bf16[1424,256]{1,0:T(8,128)(2,1)}, bf16[1424,256]{1,0:T(8,128)(2,1)}, u32[]{:S(2)}, u32[]{:S(2)}) collective-permute-start(bf16[1424,256]{1,0:T(8,128)(2,1)} %get-tuple-element.47.__), channel_id=1, source_target_pairs={{0,16},{2,18},{4,20},{6,22},{8,24},{10,26},{12,28},{14,30},{16,0},... | collective-permute-start | bytes 2187272 | tf_op jit(solution)/shard_map/ppermute | solution.py:514
  102.6 6.5 %modal_axial_coefficients.4.rest_0_ = bf16[16,144,256]{2,1,0:T(8,128)(2,1)} custom-call(s32[5]{0:T(128)S(1)} %stack.23._.place_ref, bf16[2,128,88]{2,1,0:T(8,128)(2,1)S(1)} %copy-done.19, bf16[2,128,88]{2,1,0:T(8,128)(2,1)S(1)} %copy-done.16, f32[256,256]{1,0:T(8,128)S(1)} %copy-done.3, f32[16,128,256]{2,1,0:T(8,128)S(1)} %copy-done.26, ...), custom_call_target="tpu_custom_call" | custom-call | flops 179999997952 | bytes 1800000000 | tf_op jit(solution)/shard_map/modal_axial_coefficients/pallas_call | solution.py:398
  109.1 9.9 %all-to-all-done.in_ref = bf16[16,144,256]{2,1,0:T(8,128)(2,1)} async-done(((bf16[16,144,256]{2,1,0:T(8,128)(2,1)}), bf16[16,144,256]{2,1,0:T(8,128)(2,1)}, u32[]{:S(2)}, u32[]{:S(2)}) %all-to-all-start) | async-done | bytes 1179680 | tf_op jit(solution)/shard_map/all_to_all | solution.py:509
  119.0 7.2 %all-to-all-start.2 = ((bf16[16,144,256]{2,1,0:T(8,128)(2,1)}), bf16[16,144,256]{2,1,0:T(8,128)(2,1)}, u32[]{:S(2)}, u32[]{:S(2)}) async-start(bf16[16,144,256]{2,1,0:T(8,128)(2,1)} %modal_axial_coefficients.4.rest_0_), calls=%async_computation.2 | async-start | bytes 2359296 | tf_op jit(solution)/shard_map/all_to_all | solution.py:509
  126.3 7.8 %radial_solve.4 = (f32[3,8,2,128,256]{4,3,2,1,0:T(8,128)}, bf16[4,272,256]{2,1,0:T(8,128)(2,1)}) custom-call(s32[5]{0:T(128)S(1)} %stack.23._.place_ref, f32[3]{0:T(128)S(1)} %copy-done.8, f32[1,256]{1,0:T(1,128)S(1)} %bitcast.6, f32[4,1,256]{2,1,0:T(1,128)S(1)} %reshape.7.radial_eigen_ref, f32[256,256]{1,0:T(8,128)S(1)} %copy-done.5, ...), custom_call_target="tpu_custom_call" | custom-call | flops 210000003072 | bytes 2100000000 | tf_op jit(solution)/shard_map/radial_solve/pallas_call | solution.py:438
  134.1 1.4 collective-permute-start.15
  135.5 6.4 %modal_axial_coefficients.5.rest_0_ = bf16[16,144,256]{2,1,0:T(8,128)(2,1)} custom-call(s32[5]{0:T(128)S(1)} %stack.23._.place_ref, bf16[2,128,88]{2,1,0:T(8,128)(2,1)S(1)} %copy-done.20, bf16[2,128,88]{2,1,0:T(8,128)(2,1)S(1)} %copy-done.17, f32[256,256]{1,0:T(8,128)S(1)} %copy-done.4, f32[16,128,256]{2,1,0:T(8,128)S(1)} %copy-done.24, ...), custom_call_target="tpu_custom_call" | custom-call | flops 179999997952 | bytes 1800000000 | tf_op jit(solution)/shard_map/modal_axial_coefficients/pallas_call | solution.py:398
  141.9 8.1 %all-to-all-done.2.in_ref = bf16[16,144,256]{2,1,0:T(8,128)(2,1)} async-done(((bf16[16,144,256]{2,1,0:T(8,128)(2,1)}), bf16[16,144,256]{2,1,0:T(8,128)(2,1)}, u32[]{:S(2)}, u32[]{:S(2)}) %all-to-all-start.2) | async-done | bytes 1179680 | tf_op jit(solution)/shard_map/all_to_all | solution.py:509
  150.1 6.8 %all-to-all-start.1 = ((bf16[16,144,256]{2,1,0:T(8,128)(2,1)}), bf16[16,144,256]{2,1,0:T(8,128)(2,1)}, u32[]{:S(2)}, u32[]{:S(2)}) async-start(bf16[16,144,256]{2,1,0:T(8,128)(2,1)} %modal_axial_coefficients.5.rest_0_), calls=%async_computation.1 | async-start | bytes 2359296 | tf_op jit(solution)/shard_map/all_to_all | solution.py:509
  156.8 7.7 %radial_solve.5 = (f32[3,8,2,128,256]{4,3,2,1,0:T(8,128)}, bf16[4,272,256]{2,1,0:T(8,128)(2,1)}) custom-call(s32[5]{0:T(128)S(1)} %stack.23._.place_ref, f32[3]{0:T(128)S(1)} %copy-done.8, f32[1,256]{1,0:T(1,128)S(1)} %bitcast.7, f32[4,1,256]{2,1,0:T(1,128)S(1)} %reshape.7.radial_eigen_ref, ...), custom_call_target="tpu_custom_call", output_to_operand_aliasing={{0}: (9, {})} | custom-call | flops 210000003072 | bytes 2100000000 | tf_op jit(solution)/shard_map/radial_solve/pallas_call | solution.py:438
  164.5 1.4 collective-permute-start.18
  165.9 2.6 %partner_rows.4.rest_1_ = f32[3,8,2,128,256]{4,3,2,1,0:T(8,128)} custom-call(s32[5]{0:T(128)S(1)} %stack.23._.place_ref, bf16[4,272,256]{2,1,0:T(8,128)(2,1)} %collective-permute-done.15.in_ref, f32[3,8,2,128,256]{4,3,2,1,0:T(8,128)} %get-tuple-element.52._, bf16[4,272,256]{2,1,0:T(8,128)(2,1)} %get-tuple-element.51.__.rest_0_), custom_call_target="tpu_custom_call", output_to_operand_aliasing={{}: (2, {})} | custom-call | flops 60000002048 | bytes 600000000 | tf_op jit(solution)/shard_map/partner_rows/pallas_call | solution.py:485
  168.5 6.8 %all-to-all-done.1.in_ref = bf16[16,144,256]{2,1,0:T(8,128)(2,1)} async-done(((bf16[16,144,256]{2,1,0:T(8,128)(2,1)}), bf16[16,144,256]{2,1,0:T(8,128)(2,1)}, u32[]{:S(2)}, u32[]{:S(2)}) %all-to-all-start.1) | async-done | bytes 1179680 | tf_op jit(solution)/shard_map/all_to_all | solution.py:509
  175.3 5.4 %radial_solve.6 = (f32[3,8,2,128,256]{4,3,2,1,0:T(8,128)}, bf16[2,272,256]{2,1,0:T(8,128)(2,1)}) custom-call(s32[5]{0:T(128)S(1)} %stack.23._.place_ref, f32[3]{0:T(128)S(1)} %copy-done.8, f32[1,256]{1,0:T(1,128)S(1)} %bitcast.8, f32[4,1,256]{2,1,0:T(1,128)S(1)} %reshape.7.radial_eigen_ref, ...), custom_call_target="tpu_custom_call", output_to_operand_aliasing={{0}: (9, {})} | custom-call | flops 210000003072 | bytes 2100000000 | tf_op jit(solution)/shard_map/radial_solve/pallas_call | solution.py:438
  180.9 5.3 %radial_solve.7 = (f32[3,8,2,128,256]{4,3,2,1,0:T(8,128)}, bf16[2,272,256]{2,1,0:T(8,128)(2,1)S(1)}) custom-call(s32[5]{0:T(128)S(1)} %stack.23._.place_ref, f32[3]{0:T(128)S(1)} %copy-done.8, f32[1,256]{1,0:T(1,128)S(1)} %bitcast.9, f32[4,1,256]{2,1,0:T(1,128)S(1)} %reshape.7.radial_eigen_ref, ...), custom_call_target="tpu_custom_call", output_to_operand_aliasing={{0}: (9, {})} | custom-call | flops 210000003072 | bytes 2100000000 | tf_op jit(solution)/shard_map/radial_solve/pallas_call | solution.py:438
  186.3 1.2 collective-permute-start.16
  187.4 2.6 %partner_rows.5._ = f32[3,8,2,128,256]{4,3,2,1,0:T(8,128)} custom-call(s32[5]{0:T(128)S(1)} %stack.23._.place_ref, bf16[4,272,256]{2,1,0:T(8,128)(2,1)} %collective-permute-done.18.in_ref, f32[3,8,2,128,256]{4,3,2,1,0:T(8,128)} %get-tuple-element.56._, bf16[2,272,256]{2,1,0:T(8,128)(2,1)S(1)} %get-tuple-element.55.__), custom_call_target="tpu_custom_call", output_to_operand_aliasing={{}: (2, {})} | custom-call | flops 60000002048 | bytes 600000000 | tf_op jit(solution)/shard_map/partner_rows/pallas_call | solution.py:485
  190.0 3.3 %collective-permute-done.17.in_ref = bf16[2,272,256]{2,1,0:T(8,128)(2,1)} collective-permute-done((bf16[2,272,256]{2,1,0:T(8,128)(2,1)}, bf16[2,272,256]{2,1,0:T(8,128)(2,1)}, u32[]{:S(2)}, u32[]{:S(2)}) %collective-permute-start.17) | collective-permute-done | bytes 278560 | tf_op jit(solution)/shard_map/ppermute | solution.py:538
  193.3 2.4 %partner_rows.6._ = f32[3,8,2,128,256]{4,3,2,1,0:T(8,128)} custom-call(s32[5]{0:T(128)S(1)} %stack.23._.place_ref, bf16[2,272,256]{2,1,0:T(8,128)(2,1)} %collective-permute-done.17.in_ref, f32[3,8,2,128,256]{4,3,2,1,0:T(8,128)} %partner_rows.5._, bf16[2,272,256]{2,1,0:T(8,128)(2,1)S(1)} %get-tuple-element.55.__), custom_call_target="tpu_custom_call", output_to_operand_aliasing={{}: (2, {})} | custom-call | flops 60000002048 | bytes 600000000 | tf_op jit(solution)/shard_map/partner_rows/pallas_call | solution.py:485
  195.7 3.5 %collective-permute-done.16.in_ref = bf16[2,272,256]{2,1,0:T(8,128)(2,1)S(1)} collective-permute-done((bf16[2,272,256]{2,1,0:T(8,128)(2,1)S(1)}, bf16[2,272,256]{2,1,0:T(8,128)(2,1)S(1)}, u32[]{:S(2)}, u32[]{:S(2)}) %collective-permute-start.16) | collective-permute-done | bytes 278560 | tf_op jit(solution)/shard_map/ppermute | solution.py:538
  199.2 1.4 partner_rows.7
  (82 shorter events, 1.9 us)
Async XLA Ops:
  3.0 4.5 %collective-permute-start = (bf16[64,64,256]{2,1,0:T(8,128)(2,1)S(1)}, bf16[64,64,256]{2,1,0:T(8,128)(2,1)S(1)}, u32[]{:S(2)}, u32[]{:S(2)}) collective-permute-start(bf16[64,64,256]{2,1,0:T(8,128)(2,1)S(1)} %other_core_rows.3.__), channel_id=1, source_target_pairs={{0,2},{2,0},{4,6},{6,4},{8,10},{10,8},{12,14},{14,12},{16,18},{18,... | collective-permute-start | bytes 6291464 | tf_op jit(solution)/shard_map/ppermute | solution.py:514
  6.9 15.1 %collective-permute-start.5 = (bf16[64,64,256]{2,1,0:T(8,128)(2,1)}, bf16[64,64,256]{2,1,0:T(8,128)(2,1)}, u32[]{:S(2)}, u32[]{:S(2)}) collective-permute-start(bf16[64,64,256]{2,1,0:T(8,128)(2,1)} %other_core_rows.4.__), channel_id=1, source_target_pairs={{0,2},{2,0},{4,6},{6,4},{8,10},{10,8},{12,14},{14,12},{16,18},{18,... | collective-permute-start | bytes 6291464 | tf_op jit(solution)/shard_map/ppermute | solution.py:514
  14.9 5.9 %copy-start.21 = (bf16[768,256]{1,0:T(8,128)(2,1)}, bf16[768,256]{1,0:T(8,128)(2,1)S(1)}, u32[]{:S(2)}) copy-start(bf16[768,256]{1,0:T(8,128)(2,1)S(1)} %get-tuple-element.31.__.refs_0_) | copy-start | bytes 1179652
  14.9 15.9 %collective-permute-start.2 = (bf16[768,256]{1,0:T(8,128)(2,1)}, bf16[768,256]{1,0:T(8,128)(2,1)}, u32[]{:S(2)}, u32[]{:S(2)}) collective-permute-start(bf16[768,256]{1,0:T(8,128)(2,1)} %get-tuple-element.32), channel_id=1, source_target_pairs={{0,4},{2,6},{4,0},{6,2},{8,12},{10,14},{12,8},{14,10},{16,20},{18,... | collective-permute-start | bytes 1179656 | tf_op jit(solution)/shard_map/ppermute | solution.py:514
  16.2 16.0 %collective-permute-start.3 = (bf16[768,256]{1,0:T(8,128)(2,1)}, bf16[768,256]{1,0:T(8,128)(2,1)}, u32[]{:S(2)}, u32[]{:S(2)}) collective-permute-start(bf16[768,256]{1,0:T(8,128)(2,1)} %get-tuple-element.33), channel_id=1, source_target_pairs={{0,8},{2,10},{4,12},{6,14},{8,0},{10,2},{12,4},{14,6},{16,24},{18,... | collective-permute-start | bytes 1179656 | tf_op jit(solution)/shard_map/ppermute | solution.py:514
  17.4 17.5 %collective-permute-start.4 = (bf16[768,256]{1,0:T(8,128)(2,1)}, bf16[768,256]{1,0:T(8,128)(2,1)}, u32[]{:S(2)}, u32[]{:S(2)}) collective-permute-start(bf16[768,256]{1,0:T(8,128)(2,1)} %get-tuple-element.34), channel_id=1, source_target_pairs={{0,12},{2,14},{4,8},{6,10},{8,4},{10,6},{12,0},{14,2},{16,28},{18,... | collective-permute-start | bytes 1179656 | tf_op jit(solution)/shard_map/ppermute | solution.py:514
  20.8 19.2 %collective-permute-start.1 = (bf16[64,64,256]{2,1,0:T(8,128)(2,1)}, bf16[64,64,256]{2,1,0:T(8,128)(2,1)}, u32[]{:S(2)}, u32[]{:S(2)}) collective-permute-start(bf16[64,64,256]{2,1,0:T(8,128)(2,1)} %other_core_rows.5.__), channel_id=1, source_target_pairs={{0,2},{2,0},{4,6},{6,4},{8,10},{10,8},{12,14},{14,12},{16,18},{18,... | collective-permute-start | bytes 6291464 | tf_op jit(solution)/shard_map/ppermute | solution.py:514
  22.0 12.9 %copy-start.9 = (bf16[8,216,192]{2,1,0:T(8,128)(2,1)S(1)}, bf16[8,216,192]{2,1,0:T(8,128)(2,1)}, u32[]{:S(2)}) copy-start(bf16[8,216,192]{2,1,0:T(8,128)(2,1)} %constant.67.clone.lower_ref) | copy-start | bytes 1990660
  22.0 12.9 %copy-start.11 = (bf16[8,216,192]{2,1,0:T(8,128)(2,1)S(1)}, bf16[8,216,192]{2,1,0:T(8,128)(2,1)}, u32[]{:S(2)}) copy-start(bf16[8,216,192]{2,1,0:T(8,128)(2,1)} %constant.66.clone.upper_ref) | copy-start | bytes 1990660
  22.0 12.9 %copy-start.22 = (bf16[768,256]{1,0:T(8,128)(2,1)S(1)}, bf16[768,256]{1,0:T(8,128)(2,1)}, u32[]{:S(2)}) copy-start(bf16[768,256]{1,0:T(8,128)(2,1)} %copy-done.21) | copy-start | bytes 1179652
  29.6 10.1 %copy-start.29 = (bf16[768,256]{1,0:T(8,128)(2,1)}, bf16[768,256]{1,0:T(8,128)(2,1)S(1)}, u32[]{:S(2)}) copy-start(bf16[768,256]{1,0:T(8,128)(2,1)S(1)} %get-tuple-element.35.refs_4_.refs_0_) | copy-start | bytes 1179652
  29.6 18.9 %collective-permute-start.10 = (bf16[768,256]{1,0:T(8,128)(2,1)}, bf16[768,256]{1,0:T(8,128)(2,1)}, u32[]{:S(2)}, u32[]{:S(2)}) collective-permute-start(bf16[768,256]{1,0:T(8,128)(2,1)} %get-tuple-element.42), channel_id=1, source_target_pairs={{0,4},{2,6},{4,0},{6,2},{8,12},{10,14},{12,8},{14,10},{16,20},{18,... | collective-permute-start | bytes 1179656 | tf_op jit(solution)/shard_map/ppermute | solution.py:514
  30.8 19.1 %collective-permute-start.11 = (bf16[768,256]{1,0:T(8,128)(2,1)}, bf16[768,256]{1,0:T(8,128)(2,1)}, u32[]{:S(2)}, u32[]{:S(2)}) collective-permute-start(bf16[768,256]{1,0:T(8,128)(2,1)} %get-tuple-element.43), channel_id=1, source_target_pairs={{0,8},{2,10},{4,12},{6,14},{8,0},{10,2},{12,4},{14,6},{16,24},{18,... | collective-permute-start | bytes 1179656 | tf_op jit(solution)/shard_map/ppermute | solution.py:514
  32.1 27.8 %collective-permute-start.12 = (bf16[768,256]{1,0:T(8,128)(2,1)}, bf16[768,256]{1,0:T(8,128)(2,1)}, u32[]{:S(2)}, u32[]{:S(2)}) collective-permute-start(bf16[768,256]{1,0:T(8,128)(2,1)} %get-tuple-element.44), channel_id=1, source_target_pairs={{0,12},{2,14},{4,8},{6,10},{8,4},{10,6},{12,0},{14,2},{16,28},{18,... | collective-permute-start | bytes 1179656 | tf_op jit(solution)/shard_map/ppermute | solution.py:514
  39.8 29.5 %collective-permute-start.9 = (bf16[1424,256]{1,0:T(8,128)(2,1)}, bf16[1424,256]{1,0:T(8,128)(2,1)}, u32[]{:S(2)}, u32[]{:S(2)}) collective-permute-start(bf16[1424,256]{1,0:T(8,128)(2,1)} %get-tuple-element.36.__), channel_id=1, source_target_pairs={{0,16},{2,18},{4,20},{6,22},{8,24},{10,26},{12,28},{14,30},{16,0},... | collective-permute-start | bytes 2187272 | tf_op jit(solution)/shard_map/ppermute | solution.py:514
  40.0 20.0 %copy-start.30 = (bf16[768,256]{1,0:T(8,128)(2,1)S(1)}, bf16[768,256]{1,0:T(8,128)(2,1)}, u32[]{:S(2)}) copy-start(bf16[768,256]{1,0:T(8,128)(2,1)} %copy-done.29) | copy-start | bytes 1179652
  47.5 17.3 %copy-start.27 = (bf16[768,256]{1,0:T(8,128)(2,1)}, bf16[768,256]{1,0:T(8,128)(2,1)S(1)}, u32[]{:S(2)}) copy-start(bf16[768,256]{1,0:T(8,128)(2,1)S(1)} %get-tuple-element.37.refs_4_.refs_0_) | copy-start | bytes 1179652
  47.5 42.4 %collective-permute-start.6 = (bf16[768,256]{1,0:T(8,128)(2,1)}, bf16[768,256]{1,0:T(8,128)(2,1)}, u32[]{:S(2)}, u32[]{:S(2)}) collective-permute-start(bf16[768,256]{1,0:T(8,128)(2,1)} %get-tuple-element.38), channel_id=1, source_target_pairs={{0,4},{2,6},{4,0},{6,2},{8,12},{10,14},{12,8},{14,10},{16,20},{18,... | collective-permute-start | bytes 1179656 | tf_op jit(solution)/shard_map/ppermute | solution.py:514
  48.5 41.4 %collective-permute-start.7 = (bf16[768,256]{1,0:T(8,128)(2,1)}, bf16[768,256]{1,0:T(8,128)(2,1)}, u32[]{:S(2)}, u32[]{:S(2)}) collective-permute-start(bf16[768,256]{1,0:T(8,128)(2,1)} %get-tuple-element.39), channel_id=1, source_target_pairs={{0,8},{2,10},{4,12},{6,14},{8,0},{10,2},{12,4},{14,6},{16,24},{18,... | collective-permute-start | bytes 1179656 | tf_op jit(solution)/shard_map/ppermute | solution.py:514
  49.9 43.8 %collective-permute-start.8 = (bf16[768,256]{1,0:T(8,128)(2,1)}, bf16[768,256]{1,0:T(8,128)(2,1)}, u32[]{:S(2)}, u32[]{:S(2)}) collective-permute-start(bf16[768,256]{1,0:T(8,128)(2,1)} %get-tuple-element.40), channel_id=1, source_target_pairs={{0,12},{2,14},{4,8},{6,10},{8,4},{10,6},{12,0},{14,2},{16,28},{18,... | collective-permute-start | bytes 1179656 | tf_op jit(solution)/shard_map/ppermute | solution.py:514
  60.0 9.3 %copy-start.2 = (f32[256,256]{1,0:T(8,128)S(1)}, f32[256,256]{1,0:T(8,128)}, u32[]{:S(2)}) copy-start(f32[256,256]{1,0:T(8,128)} %axial_ref.10) | copy-start | bytes 786436
  60.0 9.3 %copy-start.15 = (bf16[2,128,88]{2,1,0:T(8,128)(2,1)S(1)}, bf16[2,128,88]{2,1,0:T(8,128)(2,1)}, u32[]{:S(2)}) copy-start(bf16[2,128,88]{2,1,0:T(8,128)(2,1)} %constant.69.clone.lower_ref) | copy-start | bytes 135172
  60.0 9.3 %copy-start.18 = (bf16[2,128,88]{2,1,0:T(8,128)(2,1)S(1)}, bf16[2,128,88]{2,1,0:T(8,128)(2,1)}, u32[]{:S(2)}) copy-start(bf16[2,128,88]{2,1,0:T(8,128)(2,1)} %constant.68.clone.upper_ref) | copy-start | bytes 135172
  66.1 36.4 %collective-permute-start.14 = (bf16[1424,256]{1,0:T(8,128)(2,1)}, bf16[1424,256]{1,0:T(8,128)(2,1)}, u32[]{:S(2)}, u32[]{:S(2)}) collective-permute-start(bf16[1424,256]{1,0:T(8,128)(2,1)} %get-tuple-element.45.__), channel_id=1, source_target_pairs={{0,16},{2,18},{4,20},{6,22},{8,24},{10,26},{12,28},{14,30},{16,0},... | collective-permute-start | bytes 2187272 | tf_op jit(solution)/shard_map/ppermute | solution.py:514
  75.7 18.0 %copy-start.10 = (bf16[8,216,192]{2,1,0:T(8,128)(2,1)S(1)}, bf16[8,216,192]{2,1,0:T(8,128)(2,1)}, u32[]{:S(2)}) copy-start(bf16[8,216,192]{2,1,0:T(8,128)(2,1)} %constant.67.clone.lower_ref) | copy-start | bytes 1990660
  75.7 18.0 %copy-start.12 = (bf16[8,216,192]{2,1,0:T(8,128)(2,1)S(1)}, bf16[8,216,192]{2,1,0:T(8,128)(2,1)}, u32[]{:S(2)}) copy-start(bf16[8,216,192]{2,1,0:T(8,128)(2,1)} %constant.66.clone.upper_ref) | copy-start | bytes 1990660
  75.7 18.0 %copy-start.28 = (bf16[768,256]{1,0:T(8,128)(2,1)S(1)}, bf16[768,256]{1,0:T(8,128)(2,1)}, u32[]{:S(2)}) copy-start(bf16[768,256]{1,0:T(8,128)(2,1)} %copy-done.27) | copy-start | bytes 1179652
  75.7 43.3 %all-to-all-start = ((bf16[16,144,256]{2,1,0:T(8,128)(2,1)}), bf16[16,144,256]{2,1,0:T(8,128)(2,1)}, u32[]{:S(2)}, u32[]{:S(2)}) async-start(bf16[16,144,256]{2,1,0:T(8,128)(2,1)} %modal_axial_coefficients.3.refs_4_), calls=%async_computation | async-start | bytes 2359296 | tf_op jit(solution)/shard_map/all_to_all | solution.py:509
  93.7 8.8 %copy-start.3 = (f32[256,256]{1,0:T(8,128)S(1)}, f32[256,256]{1,0:T(8,128)}, u32[]{:S(2)}) copy-start(f32[256,256]{1,0:T(8,128)} %axial_ref.10) | copy-start | bytes 786436
  93.7 8.8 %copy-start.16 = (bf16[2,128,88]{2,1,0:T(8,128)(2,1)S(1)}, bf16[2,128,88]{2,1,0:T(8,128)(2,1)}, u32[]{:S(2)}) copy-start(bf16[2,128,88]{2,1,0:T(8,128)(2,1)} %constant.69.clone.lower_ref) | copy-start | bytes 135172
  93.8 8.8 %copy-start.19 = (bf16[2,128,88]{2,1,0:T(8,128)(2,1)S(1)}, bf16[2,128,88]{2,1,0:T(8,128)(2,1)}, u32[]{:S(2)}) copy-start(bf16[2,128,88]{2,1,0:T(8,128)(2,1)} %constant.68.clone.upper_ref) | copy-start | bytes 135172
  93.8 8.8 %copy-start.26 = (f32[16,128,256]{2,1,0:T(8,128)S(1)}, f32[16,128,256]{2,1,0:T(8,128)}, u32[]{:S(2)}) copy-start(f32[16,128,256]{2,1,0:T(8,128)} %copy-done.25) | copy-start | bytes 6291460
  100.2 35.3 %collective-permute-start.13 = (bf16[1424,256]{1,0:T(8,128)(2,1)}, bf16[1424,256]{1,0:T(8,128)(2,1)}, u32[]{:S(2)}, u32[]{:S(2)}) collective-permute-start(bf16[1424,256]{1,0:T(8,128)(2,1)} %get-tuple-element.47.__), channel_id=1, source_target_pairs={{0,16},{2,18},{4,20},{6,22},{8,24},{10,26},{12,28},{14,30},{16,0},... | collective-permute-start | bytes 2187272 | tf_op jit(solution)/shard_map/ppermute | solution.py:514
  109.1 17.2 %copy-start = (f32[4,256,256]{2,1,0:T(8,128)S(1)}, f32[4,256,256]{2,1,0:T(8,128)}, u32[]{:S(2)}) copy-start(f32[4,256,256]{2,1,0:T(8,128)} %forward_ref.7) | copy-start | bytes 3145732
  109.1 17.2 %copy-start.1 = (f32[4,256,256]{2,1,0:T(8,128)S(1)}, f32[4,256,256]{2,1,0:T(8,128)}, u32[]{:S(2)}) copy-start(f32[4,256,256]{2,1,0:T(8,128)} %backward_ref.7) | copy-start | bytes 3145732
  109.1 17.2 %copy-start.5 = (f32[256,256]{1,0:T(8,128)S(1)}, f32[256,256]{1,0:T(8,128)}, u32[]{:S(2)}) copy-start(f32[256,256]{1,0:T(8,128)} %axial_ref.13) | copy-start | bytes 786436
  109.1 17.2 %copy-start.6 = (f32[256]{0:T(256)S(1)}, f32[256]{0:T(256)}, u32[]{:S(2)}) copy-start(f32[256]{0:T(256)} %param.18) | copy-start | bytes 3076
  109.1 17.2 %copy-start.8 = (f32[3]{0:T(128)S(1)}, f32[3]{0:T(128)}, u32[]{:S(2)}) copy-start(f32[3]{0:T(128)} %diffusion_ref.7) | copy-start | bytes 40
  119.0 31.1 %all-to-all-start.2 = ((bf16[16,144,256]{2,1,0:T(8,128)(2,1)}), bf16[16,144,256]{2,1,0:T(8,128)(2,1)}, u32[]{:S(2)}, u32[]{:S(2)}) async-start(bf16[16,144,256]{2,1,0:T(8,128)(2,1)} %modal_axial_coefficients.4.rest_0_), calls=%async_computation.2 | async-start | bytes 2359296 | tf_op jit(solution)/shard_map/all_to_all | solution.py:509
  126.3 9.3 %copy-start.4 = (f32[256,256]{1,0:T(8,128)S(1)}, f32[256,256]{1,0:T(8,128)}, u32[]{:S(2)}) copy-start(f32[256,256]{1,0:T(8,128)} %axial_ref.10) | copy-start | bytes 786436
  126.3 9.2 %copy-start.17 = (bf16[2,128,88]{2,1,0:T(8,128)(2,1)S(1)}, bf16[2,128,88]{2,1,0:T(8,128)(2,1)}, u32[]{:S(2)}) copy-start(bf16[2,128,88]{2,1,0:T(8,128)(2,1)} %constant.69.clone.lower_ref) | copy-start | bytes 135172
  126.3 9.2 %copy-start.20 = (bf16[2,128,88]{2,1,0:T(8,128)(2,1)S(1)}, bf16[2,128,88]{2,1,0:T(8,128)(2,1)}, u32[]{:S(2)}) copy-start(bf16[2,128,88]{2,1,0:T(8,128)(2,1)} %constant.68.clone.upper_ref) | copy-start | bytes 135172
  126.3 9.2 %copy-start.24 = (f32[16,128,256]{2,1,0:T(8,128)S(1)}, f32[16,128,256]{2,1,0:T(8,128)}, u32[]{:S(2)}) copy-start(f32[16,128,256]{2,1,0:T(8,128)} %copy-done.23) | copy-start | bytes 6291460
  134.1 31.8 %collective-permute-start.15 = (bf16[4,272,256]{2,1,0:T(8,128)(2,1)}, bf16[4,272,256]{2,1,0:T(8,128)(2,1)}, u32[]{:S(2)}, u32[]{:S(2)}) collective-permute-start(bf16[4,272,256]{2,1,0:T(8,128)(2,1)} %get-tuple-element.49.__), channel_id=1, source_target_pairs={{0,1},{1,0},{2,3},{3,2},{4,5},{5,4},{6,7},{7,6},{8,9},{9,8},{10,11... | collective-permute-start | bytes 1671176 | tf_op jit(solution)/shard_map/ppermute | solution.py:538
  150.1 25.2 %all-to-all-start.1 = ((bf16[16,144,256]{2,1,0:T(8,128)(2,1)}), bf16[16,144,256]{2,1,0:T(8,128)(2,1)}, u32[]{:S(2)}, u32[]{:S(2)}) async-start(bf16[16,144,256]{2,1,0:T(8,128)(2,1)} %modal_axial_coefficients.5.rest_0_), calls=%async_computation.1 | async-start | bytes 2359296 | tf_op jit(solution)/shard_map/all_to_all | solution.py:509
  164.5 22.9 %collective-permute-start.18 = (bf16[4,272,256]{2,1,0:T(8,128)(2,1)}, bf16[4,272,256]{2,1,0:T(8,128)(2,1)}, u32[]{:S(2)}, u32[]{:S(2)}) collective-permute-start(bf16[4,272,256]{2,1,0:T(8,128)(2,1)} %get-tuple-element.51.__.rest_0_), channel_id=1, source_target_pairs={{0,1},{1,0},{2,3},{3,2},{4,5},{5,4},{6,7},{7,6},{8,9},{9,8},{10,11... | collective-permute-start | bytes 1671176 | tf_op jit(solution)/shard_map/ppermute | solution.py:538
  180.7 12.6 %collective-permute-start.17 = (bf16[2,272,256]{2,1,0:T(8,128)(2,1)}, bf16[2,272,256]{2,1,0:T(8,128)(2,1)}, u32[]{:S(2)}, u32[]{:S(2)}) collective-permute-start(bf16[2,272,256]{2,1,0:T(8,128)(2,1)} %get-tuple-element.53.rest_0_), channel_id=1, source_target_pairs={{0,1},{1,0},{2,3},{3,2},{4,5},{5,4},{6,7},{7,6},{8,9},{9,8},{10,11... | collective-permute-start | bytes 835592 | tf_op jit(solution)/shard_map/ppermute | solution.py:538
  186.3 12.9 %collective-permute-start.16 = (bf16[2,272,256]{2,1,0:T(8,128)(2,1)S(1)}, bf16[2,272,256]{2,1,0:T(8,128)(2,1)S(1)}, u32[]{:S(2)}, u32[]{:S(2)}) collective-permute-start(bf16[2,272,256]{2,1,0:T(8,128)(2,1)S(1)} %get-tuple-element.55.__), channel_id=1, source_target_pairs={{0,1},{1,0},{2,3},{3,2},{4,5},{5,4},{6,7},{7,6},{8,9},{9,8},{10,11... | collective-permute-start | bytes 835592 | tf_op jit(solution)/shard_map/ppermute | solution.py:538
  (6 other events, 16.4 us)

commit v7 on v6

--- a/solution.py
+++ b/solution.py
@@ -460,7 +460,7 @@
                     pl.BlockSpec(out_block, lambda i, y: (field, y[0] * turns + begin + i, 0, 0, 0)),
                     pl.BlockSpec((each, send_rows, width), lambda i, _: (i, 0, 0)),
                 ],
-                scratch_shapes=[pltpu.VMEM((width // 128, radial * per_owner, 128), F32)],
+                scratch_shapes=[pltpu.VMEM((width // 128, (radial + 1) * per_owner, 128), F32)],
             ),
             out_shape=[out_shape, jax.ShapeDtypeStruct((len(modes), send_rows, width), BF16)],
             input_output_aliases={9: 0} if carried else {},

time: 202 us -> 202 us (level)
  no operation moved by 1% of the time
where the time goes in v7:
time: 202 us; the launch traced here: 201 us
  Pallas kernels  100 us (50%)
  waiting for transfers between devices  49.2 us (24%)
  starting transfers between devices  47.4 us (23%)
  local copies, waits for them, and re-layouts  3.54 us (2%)
    all_to_all x3, starting transfers between devices, exchange(): lax.all_to_all(values, names, split_axis=0, concat_axis=0, tiled=True, ax...  28.2 us
    pallas_call x4, Pallas kernels, solve(): pl.pallas_call(functools.partial(solve_body, field=field, radial_devices=...  26.2 us
    all_to_all x3, waiting for transfers between devices, exchange(): lax.all_to_all(values, names, split_axis=0, concat_axis=0, tiled=True, ax...  24.8 us
    pallas_call x3, Pallas kernels, encode(): pl.pallas_call(functools.partial(encode_body, group=group, kept=kept), gr...  22.6 us
    pallas_call x3, Pallas kernels, join(): pl.pallas_call(functools.partial(join_body, sent=sent, rows=step), grid_s...  19.3 us
    ppermute x15, waiting for transfers between devices, flip(): lax.ppermute(values, 'modes', [(i, i ^ bits) for i in range(processors)])  17.6 us
    ppermute x15, starting transfers between devices, flip(): lax.ppermute(values, 'modes', [(i, i ^ bits) for i in range(processors)])  14.9 us
    pallas_call x3, Pallas kernels, gather(): pl.pallas_call(functools.partial(gather_body, kept=kept, rows=step), grid...  14.7 us
  transfers between devices with their start and end apart: 22, of which 10 were waited for; matrix products, arithmetic and copies ran while one was open for 0% of the time, Pallas kernels for 48%

profile of v7, /device:TPU:17, one launch (start us, length us, event | category | flops | bytes accessed | tf_op | source)
XLA Modules:
  0.0 200.6 jit_solution(9939991666286160009)
XLA Ops:
  0.1 0.7 copy-done.7
  0.7 2.2 %other_core_rows.3.__ = bf16[64,64,256]{2,1,0:T(8,128)(2,1)S(1)} custom-call(s32[5]{0:T(128)S(1)} %stack.23._.place_ref, bf16[3,64,128,256]{3,2,1,0:T(8,128)(2,1)} %own_ref.5, f32[3]{0:T(128)S(1)} %copy-done.7), custom_call_target="tpu_custom_call" | custom-call | flops 60000002048 | bytes 600000000 | tf_op jit(solution)/shard_map/other_core_rows/pallas_call | solution.py:518
  3.0 0.7 collective-permute-start
  3.7 3.2 %other_core_rows.4.__ = bf16[64,64,256]{2,1,0:T(8,128)(2,1)} custom-call(s32[5]{0:T(128)S(1)} %stack.23._.place_ref, bf16[3,64,128,256]{3,2,1,0:T(8,128)(2,1)} %own_ref.5, bf16[64,64,256]{2,1,0:T(8,128)(2,1)S(1)} %other_core_rows.3.__), custom_call_target="tpu_custom_call" | custom-call | flops 60000002048 | bytes 600000000 | tf_op jit(solution)/shard_map/other_core_rows/pallas_call | solution.py:518
  7.5 7.4 %window_coefficients.3 = (bf16[768,256]{1,0:T(8,128)(2,1)S(1)}, bf16[768,256]{1,0:T(8,128)(2,1)}, bf16[768,256]{1,0:T(8,128)(2,1)}, bf16[768,256]{1,0:T(8,128)(2,1)}) custom-call(s32[5]{0:T(128)S(1)} %stack.23._.place_ref, bf16[2,384,512]{2,1,0:T(8,128)(2,1)S(1)} %copy-done.14, bf16[2,384,512]{2,1,0:T(8,128)(2,1)S(1)} %copy-done.13, ...), custom_call_target="tpu_custom_call" | custom-call | flops 210000003072 | bytes 2100000000 | tf_op jit(solution)/shard_map/window_coefficients/pallas_call | solution.py:336
  14.9 1.2 collective-permute-start.2
  16.2 1.3 collective-permute-start.3
  17.6 3.2 %other_core_rows.5.__ = bf16[64,64,256]{2,1,0:T(8,128)(2,1)} custom-call(s32[5]{0:T(128)S(1)} %stack.23._.place_ref, bf16[3,64,128,256]{3,2,1,0:T(8,128)(2,1)} %own_ref.5, bf16[768,256]{1,0:T(8,128)(2,1)S(1)} %get-tuple-element.31.__.refs_0_), custom_call_target="tpu_custom_call" | custom-call | flops 60000002048 | bytes 600000000 | tf_op jit(solution)/shard_map/other_core_rows/pallas_call | solution.py:518
  20.8 1.2 collective-permute-start.1
  22.0 7.6 %window_coefficients.4 = (bf16[768,256]{1,0:T(8,128)(2,1)S(1)}, bf16[768,256]{1,0:T(8,128)(2,1)}, bf16[768,256]{1,0:T(8,128)(2,1)}, bf16[768,256]{1,0:T(8,128)(2,1)}) custom-call(s32[5]{0:T(128)S(1)} %stack.23._.place_ref, bf16[2,384,512]{2,1,0:T(8,128)(2,1)S(1)} %copy-done.14, bf16[2,384,512]{2,1,0:T(8,128)(2,1)S(1)} %copy-done.13, ...), custom_call_target="tpu_custom_call" | custom-call | flops 210000003072 | bytes 2100000000 | tf_op jit(solution)/shard_map/window_coefficients/pallas_call | solution.py:336
  29.6 1.2 collective-permute-start.10
  30.8 1.3 collective-permute-start.11
  32.3 2.6 %collective-permute-done.4.refs_3_ = bf16[768,256]{1,0:T(8,128)(2,1)} collective-permute-done((bf16[768,256]{1,0:T(8,128)(2,1)}, bf16[768,256]{1,0:T(8,128)(2,1)}, u32[]{:S(2)}, u32[]{:S(2)}) %collective-permute-start.4) | collective-permute-done | bytes 393248 | tf_op jit(solution)/shard_map/ppermute | solution.py:514
  34.9 4.8 %half_sums.3 = (f32[16,128,256]{2,1,0:T(8,128)S(1)}, bf16[1424,256]{1,0:T(8,128)(2,1)}) custom-call(s32[5]{0:T(128)S(1)} %stack.23._.place_ref, bf16[8,216,192]{2,1,0:T(8,128)(2,1)S(1)} %copy-done.11, bf16[8,216,192]{2,1,0:T(8,128)(2,1)S(1)} %copy-done.9, bf16[768,256]{1,0:T(8,128)(2,1)S(1)} %copy-done.22, bf16[768,256]{1,0:T(8,128)(2,1)} %collective-permute-done.2.refs_1_, ...), custom_call_target="tpu_custom_call" | custom-call | flops 149999992832 | bytes 1500000000 | tf_op jit(solution)/shard_map/half_sums/pallas_call | solution.py:372
  40.0 7.5 %window_coefficients.5 = (bf16[768,256]{1,0:T(8,128)(2,1)S(1)}, bf16[768,256]{1,0:T(8,128)(2,1)}, bf16[768,256]{1,0:T(8,128)(2,1)}, bf16[768,256]{1,0:T(8,128)(2,1)}) custom-call(s32[5]{0:T(128)S(1)} %stack.23._.place_ref, bf16[2,384,512]{2,1,0:T(8,128)(2,1)S(1)} %copy-done.14, bf16[2,384,512]{2,1,0:T(8,128)(2,1)S(1)} %copy-done.13, ...), custom_call_target="tpu_custom_call" | custom-call | flops 210000003072 | bytes 2100000000 | tf_op jit(solution)/shard_map/window_coefficients/pallas_call | solution.py:336
  47.5 1.0 collective-permute-start.6
  48.5 1.4 collective-permute-start.7
  50.2 9.8 %collective-permute-done.12.refs_3_ = bf16[768,256]{1,0:T(8,128)(2,1)} collective-permute-done((bf16[768,256]{1,0:T(8,128)(2,1)}, bf16[768,256]{1,0:T(8,128)(2,1)}, u32[]{:S(2)}, u32[]{:S(2)}) %collective-permute-start.12) | collective-permute-done | bytes 393248 | tf_op jit(solution)/shard_map/ppermute | solution.py:514
  60.0 4.8 %half_sums.4 = (f32[16,128,256]{2,1,0:T(8,128)S(1)}, bf16[1424,256]{1,0:T(8,128)(2,1)}) custom-call(s32[5]{0:T(128)S(1)} %stack.23._.place_ref, bf16[8,216,192]{2,1,0:T(8,128)(2,1)S(1)} %copy-done.11, bf16[8,216,192]{2,1,0:T(8,128)(2,1)S(1)} %copy-done.9, bf16[768,256]{1,0:T(8,128)(2,1)S(1)} %copy-done.30, bf16[768,256]{1,0:T(8,128)(2,1)} %collective-permute-done.10.refs_1_, ...), custom_call_target="tpu_custom_call" | custom-call | flops 149999992832 | bytes 1500000000 | tf_op jit(solution)/shard_map/half_sums/pallas_call | solution.py:372
  64.8 1.3 copy-done.25
  66.1 2.4 %collective-permute-start.14 = (bf16[1424,256]{1,0:T(8,128)(2,1)}, bf16[1424,256]{1,0:T(8,128)(2,1)}, u32[]{:S(2)}, u32[]{:S(2)}) collective-permute-start(bf16[1424,256]{1,0:T(8,128)(2,1)} %get-tuple-element.45.__), channel_id=1, source_target_pairs={{0,16},{2,18},{4,20},{6,22},{8,24},{10,26},{12,28},{14,30},{16,0},... | collective-permute-start | bytes 2187272 | tf_op jit(solution)/shard_map/ppermute | solution.py:514
  68.5 0.8 collective-permute-done.9.in_ref
  69.3 6.4 %modal_axial_coefficients.3.refs_4_ = bf16[16,144,256]{2,1,0:T(8,128)(2,1)} custom-call(s32[5]{0:T(128)S(1)} %stack.23._.place_ref, bf16[2,128,88]{2,1,0:T(8,128)(2,1)S(1)} %copy-done.18, bf16[2,128,88]{2,1,0:T(8,128)(2,1)S(1)} %copy-done.15, f32[256,256]{1,0:T(8,128)S(1)} %copy-done.2, f32[16,128,256]{2,1,0:T(8,128)S(1)} %get-tuple-element.41.own_ref, ...), custom_call_target="tpu_custom_call" | custom-call | flops 179999997952 | bytes 1800000000 | tf_op jit(solution)/shard_map/modal_axial_coefficients/pallas_call | solution.py:398
  75.7 14.2 %all-to-all-start = ((bf16[16,144,256]{2,1,0:T(8,128)(2,1)}), bf16[16,144,256]{2,1,0:T(8,128)(2,1)}, u32[]{:S(2)}, u32[]{:S(2)}) async-start(bf16[16,144,256]{2,1,0:T(8,128)(2,1)} %modal_axial_coefficients.3.refs_4_), calls=%async_computation | async-start | bytes 2359296 | tf_op jit(solution)/shard_map/all_to_all | solution.py:509
  90.0 3.8 %collective-permute-done.8.refs_3_ = bf16[768,256]{1,0:T(8,128)(2,1)} collective-permute-done((bf16[768,256]{1,0:T(8,128)(2,1)}, bf16[768,256]{1,0:T(8,128)(2,1)}, u32[]{:S(2)}, u32[]{:S(2)}) %collective-permute-start.8) | collective-permute-done | bytes 393248 | tf_op jit(solution)/shard_map/ppermute | solution.py:514
  93.8 5.1 %half_sums.5 = (f32[16,128,256]{2,1,0:T(8,128)S(1)}, bf16[1424,256]{1,0:T(8,128)(2,1)}) custom-call(s32[5]{0:T(128)S(1)} %stack.23._.place_ref, bf16[8,216,192]{2,1,0:T(8,128)(2,1)S(1)} %copy-done.12, bf16[8,216,192]{2,1,0:T(8,128)(2,1)S(1)} %copy-done.10, bf16[768,256]{1,0:T(8,128)(2,1)S(1)} %copy-done.28, bf16[768,256]{1,0:T(8,128)(2,1)} %collective-permute-done.6.refs_1_, ...), custom_call_target="tpu_custom_call" | custom-call | flops 149999992832 | bytes 1500000000 | tf_op jit(solution)/shard_map/half_sums/pallas_call | solution.py:372
  98.8 1.3 copy-done.23
  100.2 2.4 %collective-permute-start.13 = (bf16[1424,256]{1,0:T(8,128)(2,1)}, bf16[1424,256]{1,0:T(8,128)(2,1)}, u32[]{:S(2)}, u32[]{:S(2)}) collective-permute-start(bf16[1424,256]{1,0:T(8,128)(2,1)} %get-tuple-element.47.__), channel_id=1, source_target_pairs={{0,16},{2,18},{4,20},{6,22},{8,24},{10,26},{12,28},{14,30},{16,0},... | collective-permute-start | bytes 2187272 | tf_op jit(solution)/shard_map/ppermute | solution.py:514
  102.6 6.5 %modal_axial_coefficients.4.rest_0_ = bf16[16,144,256]{2,1,0:T(8,128)(2,1)} custom-call(s32[5]{0:T(128)S(1)} %stack.23._.place_ref, bf16[2,128,88]{2,1,0:T(8,128)(2,1)S(1)} %copy-done.19, bf16[2,128,88]{2,1,0:T(8,128)(2,1)S(1)} %copy-done.16, f32[256,256]{1,0:T(8,128)S(1)} %copy-done.3, f32[16,128,256]{2,1,0:T(8,128)S(1)} %copy-done.26, ...), custom_call_target="tpu_custom_call" | custom-call | flops 179999997952 | bytes 1800000000 | tf_op jit(solution)/shard_map/modal_axial_coefficients/pallas_call | solution.py:398
  109.1 9.9 %all-to-all-done.in_ref = bf16[16,144,256]{2,1,0:T(8,128)(2,1)} async-done(((bf16[16,144,256]{2,1,0:T(8,128)(2,1)}), bf16[16,144,256]{2,1,0:T(8,128)(2,1)}, u32[]{:S(2)}, u32[]{:S(2)}) %all-to-all-start) | async-done | bytes 1179680 | tf_op jit(solution)/shard_map/all_to_all | solution.py:509
  119.0 7.2 %all-to-all-start.2 = ((bf16[16,144,256]{2,1,0:T(8,128)(2,1)}), bf16[16,144,256]{2,1,0:T(8,128)(2,1)}, u32[]{:S(2)}, u32[]{:S(2)}) async-start(bf16[16,144,256]{2,1,0:T(8,128)(2,1)} %modal_axial_coefficients.4.rest_0_), calls=%async_computation.2 | async-start | bytes 2359296 | tf_op jit(solution)/shard_map/all_to_all | solution.py:509
  126.3 7.8 %radial_solve.4 = (f32[3,8,2,128,256]{4,3,2,1,0:T(8,128)}, bf16[4,272,256]{2,1,0:T(8,128)(2,1)}) custom-call(s32[5]{0:T(128)S(1)} %stack.23._.place_ref, f32[3]{0:T(128)S(1)} %copy-done.8, f32[1,256]{1,0:T(1,128)S(1)} %bitcast.6, f32[4,1,256]{2,1,0:T(1,128)S(1)} %reshape.7.radial_eigen_ref, f32[256,256]{1,0:T(8,128)S(1)} %copy-done.5, ...), custom_call_target="tpu_custom_call" | custom-call | flops 210000003072 | bytes 2100000000 | tf_op jit(solution)/shard_map/radial_solve/pallas_call | solution.py:438
  134.1 1.4 collective-permute-start.15
  135.5 6.4 %modal_axial_coefficients.5.rest_0_ = bf16[16,144,256]{2,1,0:T(8,128)(2,1)} custom-call(s32[5]{0:T(128)S(1)} %stack.23._.place_ref, bf16[2,128,88]{2,1,0:T(8,128)(2,1)S(1)} %copy-done.20, bf16[2,128,88]{2,1,0:T(8,128)(2,1)S(1)} %copy-done.17, f32[256,256]{1,0:T(8,128)S(1)} %copy-done.4, f32[16,128,256]{2,1,0:T(8,128)S(1)} %copy-done.24, ...), custom_call_target="tpu_custom_call" | custom-call | flops 179999997952 | bytes 1800000000 | tf_op jit(solution)/shard_map/modal_axial_coefficients/pallas_call | solution.py:398
  141.9 8.1 %all-to-all-done.2.in_ref = bf16[16,144,256]{2,1,0:T(8,128)(2,1)} async-done(((bf16[16,144,256]{2,1,0:T(8,128)(2,1)}), bf16[16,144,256]{2,1,0:T(8,128)(2,1)}, u32[]{:S(2)}, u32[]{:S(2)}) %all-to-all-start.2) | async-done | bytes 1179680 | tf_op jit(solution)/shard_map/all_to_all | solution.py:509
  150.1 6.8 %all-to-all-start.1 = ((bf16[16,144,256]{2,1,0:T(8,128)(2,1)}), bf16[16,144,256]{2,1,0:T(8,128)(2,1)}, u32[]{:S(2)}, u32[]{:S(2)}) async-start(bf16[16,144,256]{2,1,0:T(8,128)(2,1)} %modal_axial_coefficients.5.rest_0_), calls=%async_computation.1 | async-start | bytes 2359296 | tf_op jit(solution)/shard_map/all_to_all | solution.py:509
  156.8 7.7 %radial_solve.5 = (f32[3,8,2,128,256]{4,3,2,1,0:T(8,128)}, bf16[4,272,256]{2,1,0:T(8,128)(2,1)}) custom-call(s32[5]{0:T(128)S(1)} %stack.23._.place_ref, f32[3]{0:T(128)S(1)} %copy-done.8, f32[1,256]{1,0:T(1,128)S(1)} %bitcast.7, f32[4,1,256]{2,1,0:T(1,128)S(1)} %reshape.7.radial_eigen_ref, ...), custom_call_target="tpu_custom_call", output_to_operand_aliasing={{0}: (9, {})} | custom-call | flops 210000003072 | bytes 2100000000 | tf_op jit(solution)/shard_map/radial_solve/pallas_call | solution.py:438
  164.5 1.4 collective-permute-start.18
  165.9 2.6 %partner_rows.4.rest_1_ = f32[3,8,2,128,256]{4,3,2,1,0:T(8,128)} custom-call(s32[5]{0:T(128)S(1)} %stack.23._.place_ref, bf16[4,272,256]{2,1,0:T(8,128)(2,1)} %collective-permute-done.15.in_ref, f32[3,8,2,128,256]{4,3,2,1,0:T(8,128)} %get-tuple-element.52._, bf16[4,272,256]{2,1,0:T(8,128)(2,1)} %get-tuple-element.51.__.rest_0_), custom_call_target="tpu_custom_call", output_to_operand_aliasing={{}: (2, {})} | custom-call | flops 60000002048 | bytes 600000000 | tf_op jit(solution)/shard_map/partner_rows/pallas_call | solution.py:485
  168.5 6.8 %all-to-all-done.1.in_ref = bf16[16,144,256]{2,1,0:T(8,128)(2,1)} async-done(((bf16[16,144,256]{2,1,0:T(8,128)(2,1)}), bf16[16,144,256]{2,1,0:T(8,128)(2,1)}, u32[]{:S(2)}, u32[]{:S(2)}) %all-to-all-start.1) | async-done | bytes 1179680 | tf_op jit(solution)/shard_map/all_to_all | solution.py:509
  175.3 5.4 %radial_solve.6 = (f32[3,8,2,128,256]{4,3,2,1,0:T(8,128)}, bf16[2,272,256]{2,1,0:T(8,128)(2,1)}) custom-call(s32[5]{0:T(128)S(1)} %stack.23._.place_ref, f32[3]{0:T(128)S(1)} %copy-done.8, f32[1,256]{1,0:T(1,128)S(1)} %bitcast.8, f32[4,1,256]{2,1,0:T(1,128)S(1)} %reshape.7.radial_eigen_ref, ...), custom_call_target="tpu_custom_call", output_to_operand_aliasing={{0}: (9, {})} | custom-call | flops 210000003072 | bytes 2100000000 | tf_op jit(solution)/shard_map/radial_solve/pallas_call | solution.py:438
  181.0 5.3 %radial_solve.7 = (f32[3,8,2,128,256]{4,3,2,1,0:T(8,128)}, bf16[2,272,256]{2,1,0:T(8,128)(2,1)S(1)}) custom-call(s32[5]{0:T(128)S(1)} %stack.23._.place_ref, f32[3]{0:T(128)S(1)} %copy-done.8, f32[1,256]{1,0:T(1,128)S(1)} %bitcast.9, f32[4,1,256]{2,1,0:T(1,128)S(1)} %reshape.7.radial_eigen_ref, ...), custom_call_target="tpu_custom_call", output_to_operand_aliasing={{0}: (9, {})} | custom-call | flops 210000003072 | bytes 2100000000 | tf_op jit(solution)/shard_map/radial_solve/pallas_call | solution.py:438
  186.3 1.2 collective-permute-start.16
  187.5 2.6 %partner_rows.5._ = f32[3,8,2,128,256]{4,3,2,1,0:T(8,128)} custom-call(s32[5]{0:T(128)S(1)} %stack.23._.place_ref, bf16[4,272,256]{2,1,0:T(8,128)(2,1)} %collective-permute-done.18.in_ref, f32[3,8,2,128,256]{4,3,2,1,0:T(8,128)} %get-tuple-element.56._, bf16[2,272,256]{2,1,0:T(8,128)(2,1)S(1)} %get-tuple-element.55.__), custom_call_target="tpu_custom_call", output_to_operand_aliasing={{}: (2, {})} | custom-call | flops 60000002048 | bytes 600000000 | tf_op jit(solution)/shard_map/partner_rows/pallas_call | solution.py:485
  190.0 3.3 %collective-permute-done.17.in_ref = bf16[2,272,256]{2,1,0:T(8,128)(2,1)} collective-permute-done((bf16[2,272,256]{2,1,0:T(8,128)(2,1)}, bf16[2,272,256]{2,1,0:T(8,128)(2,1)}, u32[]{:S(2)}, u32[]{:S(2)}) %collective-permute-start.17) | collective-permute-done | bytes 278560 | tf_op jit(solution)/shard_map/ppermute | solution.py:538
  193.3 2.4 %partner_rows.6._ = f32[3,8,2,128,256]{4,3,2,1,0:T(8,128)} custom-call(s32[5]{0:T(128)S(1)} %stack.23._.place_ref, bf16[2,272,256]{2,1,0:T(8,128)(2,1)} %collective-permute-done.17.in_ref, f32[3,8,2,128,256]{4,3,2,1,0:T(8,128)} %partner_rows.5._, bf16[2,272,256]{2,1,0:T(8,128)(2,1)S(1)} %get-tuple-element.55.__), custom_call_target="tpu_custom_call", output_to_operand_aliasing={{}: (2, {})} | custom-call | flops 60000002048 | bytes 600000000 | tf_op jit(solution)/shard_map/partner_rows/pallas_call | solution.py:485
  195.7 3.5 %collective-permute-done.16.in_ref = bf16[2,272,256]{2,1,0:T(8,128)(2,1)S(1)} collective-permute-done((bf16[2,272,256]{2,1,0:T(8,128)(2,1)S(1)}, bf16[2,272,256]{2,1,0:T(8,128)(2,1)S(1)}, u32[]{:S(2)}, u32[]{:S(2)}) %collective-permute-start.16) | collective-permute-done | bytes 278560 | tf_op jit(solution)/shard_map/ppermute | solution.py:538
  199.2 1.4 partner_rows.7
  (82 shorter events, 1.9 us)
Async XLA Ops:
  3.0 4.5 %collective-permute-start = (bf16[64,64,256]{2,1,0:T(8,128)(2,1)S(1)}, bf16[64,64,256]{2,1,0:T(8,128)(2,1)S(1)}, u32[]{:S(2)}, u32[]{:S(2)}) collective-permute-start(bf16[64,64,256]{2,1,0:T(8,128)(2,1)S(1)} %other_core_rows.3.__), channel_id=1, source_target_pairs={{0,2},{2,0},{4,6},{6,4},{8,10},{10,8},{12,14},{14,12},{16,18},{18,... | collective-permute-start | bytes 6291464 | tf_op jit(solution)/shard_map/ppermute | solution.py:514
  6.9 15.1 %collective-permute-start.5 = (bf16[64,64,256]{2,1,0:T(8,128)(2,1)}, bf16[64,64,256]{2,1,0:T(8,128)(2,1)}, u32[]{:S(2)}, u32[]{:S(2)}) collective-permute-start(bf16[64,64,256]{2,1,0:T(8,128)(2,1)} %other_core_rows.4.__), channel_id=1, source_target_pairs={{0,2},{2,0},{4,6},{6,4},{8,10},{10,8},{12,14},{14,12},{16,18},{18,... | collective-permute-start | bytes 6291464 | tf_op jit(solution)/shard_map/ppermute | solution.py:514
  14.9 5.9 %copy-start.21 = (bf16[768,256]{1,0:T(8,128)(2,1)}, bf16[768,256]{1,0:T(8,128)(2,1)S(1)}, u32[]{:S(2)}) copy-start(bf16[768,256]{1,0:T(8,128)(2,1)S(1)} %get-tuple-element.31.__.refs_0_) | copy-start | bytes 1179652
  14.9 15.9 %collective-permute-start.2 = (bf16[768,256]{1,0:T(8,128)(2,1)}, bf16[768,256]{1,0:T(8,128)(2,1)}, u32[]{:S(2)}, u32[]{:S(2)}) collective-permute-start(bf16[768,256]{1,0:T(8,128)(2,1)} %get-tuple-element.32), channel_id=1, source_target_pairs={{0,4},{2,6},{4,0},{6,2},{8,12},{10,14},{12,8},{14,10},{16,20},{18,... | collective-permute-start | bytes 1179656 | tf_op jit(solution)/shard_map/ppermute | solution.py:514
  16.2 16.0 %collective-permute-start.3 = (bf16[768,256]{1,0:T(8,128)(2,1)}, bf16[768,256]{1,0:T(8,128)(2,1)}, u32[]{:S(2)}, u32[]{:S(2)}) collective-permute-start(bf16[768,256]{1,0:T(8,128)(2,1)} %get-tuple-element.33), channel_id=1, source_target_pairs={{0,8},{2,10},{4,12},{6,14},{8,0},{10,2},{12,4},{14,6},{16,24},{18,... | collective-permute-start | bytes 1179656 | tf_op jit(solution)/shard_map/ppermute | solution.py:514
  17.4 17.5 %collective-permute-start.4 = (bf16[768,256]{1,0:T(8,128)(2,1)}, bf16[768,256]{1,0:T(8,128)(2,1)}, u32[]{:S(2)}, u32[]{:S(2)}) collective-permute-start(bf16[768,256]{1,0:T(8,128)(2,1)} %get-tuple-element.34), channel_id=1, source_target_pairs={{0,12},{2,14},{4,8},{6,10},{8,4},{10,6},{12,0},{14,2},{16,28},{18,... | collective-permute-start | bytes 1179656 | tf_op jit(solution)/shard_map/ppermute | solution.py:514
  20.8 19.2 %collective-permute-start.1 = (bf16[64,64,256]{2,1,0:T(8,128)(2,1)}, bf16[64,64,256]{2,1,0:T(8,128)(2,1)}, u32[]{:S(2)}, u32[]{:S(2)}) collective-permute-start(bf16[64,64,256]{2,1,0:T(8,128)(2,1)} %other_core_rows.5.__), channel_id=1, source_target_pairs={{0,2},{2,0},{4,6},{6,4},{8,10},{10,8},{12,14},{14,12},{16,18},{18,... | collective-permute-start | bytes 6291464 | tf_op jit(solution)/shard_map/ppermute | solution.py:514
  22.0 12.9 %copy-start.9 = (bf16[8,216,192]{2,1,0:T(8,128)(2,1)S(1)}, bf16[8,216,192]{2,1,0:T(8,128)(2,1)}, u32[]{:S(2)}) copy-start(bf16[8,216,192]{2,1,0:T(8,128)(2,1)} %constant.67.clone.lower_ref) | copy-start | bytes 1990660
  22.0 12.9 %copy-start.11 = (bf16[8,216,192]{2,1,0:T(8,128)(2,1)S(1)}, bf16[8,216,192]{2,1,0:T(8,128)(2,1)}, u32[]{:S(2)}) copy-start(bf16[8,216,192]{2,1,0:T(8,128)(2,1)} %constant.66.clone.upper_ref) | copy-start | bytes 1990660
  22.0 12.9 %copy-start.22 = (bf16[768,256]{1,0:T(8,128)(2,1)S(1)}, bf16[768,256]{1,0:T(8,128)(2,1)}, u32[]{:S(2)}) copy-start(bf16[768,256]{1,0:T(8,128)(2,1)} %copy-done.21) | copy-start | bytes 1179652
  29.6 10.1 %copy-start.29 = (bf16[768,256]{1,0:T(8,128)(2,1)}, bf16[768,256]{1,0:T(8,128)(2,1)S(1)}, u32[]{:S(2)}) copy-start(bf16[768,256]{1,0:T(8,128)(2,1)S(1)} %get-tuple-element.35.refs_4_.refs_0_) | copy-start | bytes 1179652
  29.6 18.9 %collective-permute-start.10 = (bf16[768,256]{1,0:T(8,128)(2,1)}, bf16[768,256]{1,0:T(8,128)(2,1)}, u32[]{:S(2)}, u32[]{:S(2)}) collective-permute-start(bf16[768,256]{1,0:T(8,128)(2,1)} %get-tuple-element.42), channel_id=1, source_target_pairs={{0,4},{2,6},{4,0},{6,2},{8,12},{10,14},{12,8},{14,10},{16,20},{18,... | collective-permute-start | bytes 1179656 | tf_op jit(solution)/shard_map/ppermute | solution.py:514
  30.8 19.1 %collective-permute-start.11 = (bf16[768,256]{1,0:T(8,128)(2,1)}, bf16[768,256]{1,0:T(8,128)(2,1)}, u32[]{:S(2)}, u32[]{:S(2)}) collective-permute-start(bf16[768,256]{1,0:T(8,128)(2,1)} %get-tuple-element.43), channel_id=1, source_target_pairs={{0,8},{2,10},{4,12},{6,14},{8,0},{10,2},{12,4},{14,6},{16,24},{18,... | collective-permute-start | bytes 1179656 | tf_op jit(solution)/shard_map/ppermute | solution.py:514
  32.1 27.8 %collective-permute-start.12 = (bf16[768,256]{1,0:T(8,128)(2,1)}, bf16[768,256]{1,0:T(8,128)(2,1)}, u32[]{:S(2)}, u32[]{:S(2)}) collective-permute-start(bf16[768,256]{1,0:T(8,128)(2,1)} %get-tuple-element.44), channel_id=1, source_target_pairs={{0,12},{2,14},{4,8},{6,10},{8,4},{10,6},{12,0},{14,2},{16,28},{18,... | collective-permute-start | bytes 1179656 | tf_op jit(solution)/shard_map/ppermute | solution.py:514
  39.8 29.5 %collective-permute-start.9 = (bf16[1424,256]{1,0:T(8,128)(2,1)}, bf16[1424,256]{1,0:T(8,128)(2,1)}, u32[]{:S(2)}, u32[]{:S(2)}) collective-permute-start(bf16[1424,256]{1,0:T(8,128)(2,1)} %get-tuple-element.36.__), channel_id=1, source_target_pairs={{0,16},{2,18},{4,20},{6,22},{8,24},{10,26},{12,28},{14,30},{16,0},... | collective-permute-start | bytes 2187272 | tf_op jit(solution)/shard_map/ppermute | solution.py:514
  40.0 20.0 %copy-start.30 = (bf16[768,256]{1,0:T(8,128)(2,1)S(1)}, bf16[768,256]{1,0:T(8,128)(2,1)}, u32[]{:S(2)}) copy-start(bf16[768,256]{1,0:T(8,128)(2,1)} %copy-done.29) | copy-start | bytes 1179652
  47.5 17.3 %copy-start.27 = (bf16[768,256]{1,0:T(8,128)(2,1)}, bf16[768,256]{1,0:T(8,128)(2,1)S(1)}, u32[]{:S(2)}) copy-start(bf16[768,256]{1,0:T(8,128)(2,1)S(1)} %get-tuple-element.37.refs_4_.refs_0_) | copy-start | bytes 1179652
  47.5 42.4 %collective-permute-start.6 = (bf16[768,256]{1,0:T(8,128)(2,1)}, bf16[768,256]{1,0:T(8,128)(2,1)}, u32[]{:S(2)}, u32[]{:S(2)}) collective-permute-start(bf16[768,256]{1,0:T(8,128)(2,1)} %get-tuple-element.38), channel_id=1, source_target_pairs={{0,4},{2,6},{4,0},{6,2},{8,12},{10,14},{12,8},{14,10},{16,20},{18,... | collective-permute-start | bytes 1179656 | tf_op jit(solution)/shard_map/ppermute | solution.py:514
  48.5 41.4 %collective-permute-start.7 = (bf16[768,256]{1,0:T(8,128)(2,1)}, bf16[768,256]{1,0:T(8,128)(2,1)}, u32[]{:S(2)}, u32[]{:S(2)}) collective-permute-start(bf16[768,256]{1,0:T(8,128)(2,1)} %get-tuple-element.39), channel_id=1, source_target_pairs={{0,8},{2,10},{4,12},{6,14},{8,0},{10,2},{12,4},{14,6},{16,24},{18,... | collective-permute-start | bytes 1179656 | tf_op jit(solution)/shard_map/ppermute | solution.py:514
  49.9 43.8 %collective-permute-start.8 = (bf16[768,256]{1,0:T(8,128)(2,1)}, bf16[768,256]{1,0:T(8,128)(2,1)}, u32[]{:S(2)}, u32[]{:S(2)}) collective-permute-start(bf16[768,256]{1,0:T(8,128)(2,1)} %get-tuple-element.40), channel_id=1, source_target_pairs={{0,12},{2,14},{4,8},{6,10},{8,4},{10,6},{12,0},{14,2},{16,28},{18,... | collective-permute-start | bytes 1179656 | tf_op jit(solution)/shard_map/ppermute | solution.py:514
  60.0 9.3 %copy-start.2 = (f32[256,256]{1,0:T(8,128)S(1)}, f32[256,256]{1,0:T(8,128)}, u32[]{:S(2)}) copy-start(f32[256,256]{1,0:T(8,128)} %axial_ref.10) | copy-start | bytes 786436
  60.0 9.3 %copy-start.15 = (bf16[2,128,88]{2,1,0:T(8,128)(2,1)S(1)}, bf16[2,128,88]{2,1,0:T(8,128)(2,1)}, u32[]{:S(2)}) copy-start(bf16[2,128,88]{2,1,0:T(8,128)(2,1)} %constant.69.clone.lower_ref) | copy-start | bytes 135172
  60.0 9.3 %copy-start.18 = (bf16[2,128,88]{2,1,0:T(8,128)(2,1)S(1)}, bf16[2,128,88]{2,1,0:T(8,128)(2,1)}, u32[]{:S(2)}) copy-start(bf16[2,128,88]{2,1,0:T(8,128)(2,1)} %constant.68.clone.upper_ref) | copy-start | bytes 135172
  66.1 36.4 %collective-permute-start.14 = (bf16[1424,256]{1,0:T(8,128)(2,1)}, bf16[1424,256]{1,0:T(8,128)(2,1)}, u32[]{:S(2)}, u32[]{:S(2)}) collective-permute-start(bf16[1424,256]{1,0:T(8,128)(2,1)} %get-tuple-element.45.__), channel_id=1, source_target_pairs={{0,16},{2,18},{4,20},{6,22},{8,24},{10,26},{12,28},{14,30},{16,0},... | collective-permute-start | bytes 2187272 | tf_op jit(solution)/shard_map/ppermute | solution.py:514
  75.7 18.0 %copy-start.10 = (bf16[8,216,192]{2,1,0:T(8,128)(2,1)S(1)}, bf16[8,216,192]{2,1,0:T(8,128)(2,1)}, u32[]{:S(2)}) copy-start(bf16[8,216,192]{2,1,0:T(8,128)(2,1)} %constant.67.clone.lower_ref) | copy-start | bytes 1990660
  75.7 18.0 %copy-start.12 = (bf16[8,216,192]{2,1,0:T(8,128)(2,1)S(1)}, bf16[8,216,192]{2,1,0:T(8,128)(2,1)}, u32[]{:S(2)}) copy-start(bf16[8,216,192]{2,1,0:T(8,128)(2,1)} %constant.66.clone.upper_ref) | copy-start | bytes 1990660
  75.7 18.0 %copy-start.28 = (bf16[768,256]{1,0:T(8,128)(2,1)S(1)}, bf16[768,256]{1,0:T(8,128)(2,1)}, u32[]{:S(2)}) copy-start(bf16[768,256]{1,0:T(8,128)(2,1)} %copy-done.27) | copy-start | bytes 1179652
  75.7 43.3 %all-to-all-start = ((bf16[16,144,256]{2,1,0:T(8,128)(2,1)}), bf16[16,144,256]{2,1,0:T(8,128)(2,1)}, u32[]{:S(2)}, u32[]{:S(2)}) async-start(bf16[16,144,256]{2,1,0:T(8,128)(2,1)} %modal_axial_coefficients.3.refs_4_), calls=%async_computation | async-start | bytes 2359296 | tf_op jit(solution)/shard_map/all_to_all | solution.py:509
  93.7 8.8 %copy-start.3 = (f32[256,256]{1,0:T(8,128)S(1)}, f32[256,256]{1,0:T(8,128)}, u32[]{:S(2)}) copy-start(f32[256,256]{1,0:T(8,128)} %axial_ref.10) | copy-start | bytes 786436
  93.7 8.8 %copy-start.16 = (bf16[2,128,88]{2,1,0:T(8,128)(2,1)S(1)}, bf16[2,128,88]{2,1,0:T(8,128)(2,1)}, u32[]{:S(2)}) copy-start(bf16[2,128,88]{2,1,0:T(8,128)(2,1)} %constant.69.clone.lower_ref) | copy-start | bytes 135172
  93.8 8.8 %copy-start.19 = (bf16[2,128,88]{2,1,0:T(8,128)(2,1)S(1)}, bf16[2,128,88]{2,1,0:T(8,128)(2,1)}, u32[]{:S(2)}) copy-start(bf16[2,128,88]{2,1,0:T(8,128)(2,1)} %constant.68.clone.upper_ref) | copy-start | bytes 135172
  93.8 8.8 %copy-start.26 = (f32[16,128,256]{2,1,0:T(8,128)S(1)}, f32[16,128,256]{2,1,0:T(8,128)}, u32[]{:S(2)}) copy-start(f32[16,128,256]{2,1,0:T(8,128)} %copy-done.25) | copy-start | bytes 6291460
  100.2 35.3 %collective-permute-start.13 = (bf16[1424,256]{1,0:T(8,128)(2,1)}, bf16[1424,256]{1,0:T(8,128)(2,1)}, u32[]{:S(2)}, u32[]{:S(2)}) collective-permute-start(bf16[1424,256]{1,0:T(8,128)(2,1)} %get-tuple-element.47.__), channel_id=1, source_target_pairs={{0,16},{2,18},{4,20},{6,22},{8,24},{10,26},{12,28},{14,30},{16,0},... | collective-permute-start | bytes 2187272 | tf_op jit(solution)/shard_map/ppermute | solution.py:514
  109.1 17.2 %copy-start = (f32[4,256,256]{2,1,0:T(8,128)S(1)}, f32[4,256,256]{2,1,0:T(8,128)}, u32[]{:S(2)}) copy-start(f32[4,256,256]{2,1,0:T(8,128)} %forward_ref.7) | copy-start | bytes 3145732
  109.1 17.2 %copy-start.1 = (f32[4,256,256]{2,1,0:T(8,128)S(1)}, f32[4,256,256]{2,1,0:T(8,128)}, u32[]{:S(2)}) copy-start(f32[4,256,256]{2,1,0:T(8,128)} %backward_ref.7) | copy-start | bytes 3145732
  109.1 17.2 %copy-start.5 = (f32[256,256]{1,0:T(8,128)S(1)}, f32[256,256]{1,0:T(8,128)}, u32[]{:S(2)}) copy-start(f32[256,256]{1,0:T(8,128)} %axial_ref.13) | copy-start | bytes 786436
  109.1 17.2 %copy-start.6 = (f32[256]{0:T(256)S(1)}, f32[256]{0:T(256)}, u32[]{:S(2)}) copy-start(f32[256]{0:T(256)} %param.18) | copy-start | bytes 3076
  109.1 17.2 %copy-start.8 = (f32[3]{0:T(128)S(1)}, f32[3]{0:T(128)}, u32[]{:S(2)}) copy-start(f32[3]{0:T(128)} %diffusion_ref.7) | copy-start | bytes 40
  119.0 31.1 %all-to-all-start.2 = ((bf16[16,144,256]{2,1,0:T(8,128)(2,1)}), bf16[16,144,256]{2,1,0:T(8,128)(2,1)}, u32[]{:S(2)}, u32[]{:S(2)}) async-start(bf16[16,144,256]{2,1,0:T(8,128)(2,1)} %modal_axial_coefficients.4.rest_0_), calls=%async_computation.2 | async-start | bytes 2359296 | tf_op jit(solution)/shard_map/all_to_all | solution.py:509
  126.3 9.3 %copy-start.4 = (f32[256,256]{1,0:T(8,128)S(1)}, f32[256,256]{1,0:T(8,128)}, u32[]{:S(2)}) copy-start(f32[256,256]{1,0:T(8,128)} %axial_ref.10) | copy-start | bytes 786436
  126.3 9.2 %copy-start.17 = (bf16[2,128,88]{2,1,0:T(8,128)(2,1)S(1)}, bf16[2,128,88]{2,1,0:T(8,128)(2,1)}, u32[]{:S(2)}) copy-start(bf16[2,128,88]{2,1,0:T(8,128)(2,1)} %constant.69.clone.lower_ref) | copy-start | bytes 135172
  126.3 9.2 %copy-start.20 = (bf16[2,128,88]{2,1,0:T(8,128)(2,1)S(1)}, bf16[2,128,88]{2,1,0:T(8,128)(2,1)}, u32[]{:S(2)}) copy-start(bf16[2,128,88]{2,1,0:T(8,128)(2,1)} %constant.68.clone.upper_ref) | copy-start | bytes 135172
  126.3 9.2 %copy-start.24 = (f32[16,128,256]{2,1,0:T(8,128)S(1)}, f32[16,128,256]{2,1,0:T(8,128)}, u32[]{:S(2)}) copy-start(f32[16,128,256]{2,1,0:T(8,128)} %copy-done.23) | copy-start | bytes 6291460
  134.1 31.8 %collective-permute-start.15 = (bf16[4,272,256]{2,1,0:T(8,128)(2,1)}, bf16[4,272,256]{2,1,0:T(8,128)(2,1)}, u32[]{:S(2)}, u32[]{:S(2)}) collective-permute-start(bf16[4,272,256]{2,1,0:T(8,128)(2,1)} %get-tuple-element.49.__), channel_id=1, source_target_pairs={{0,1},{1,0},{2,3},{3,2},{4,5},{5,4},{6,7},{7,6},{8,9},{9,8},{10,11... | collective-permute-start | bytes 1671176 | tf_op jit(solution)/shard_map/ppermute | solution.py:538
  150.1 25.2 %all-to-all-start.1 = ((bf16[16,144,256]{2,1,0:T(8,128)(2,1)}), bf16[16,144,256]{2,1,0:T(8,128)(2,1)}, u32[]{:S(2)}, u32[]{:S(2)}) async-start(bf16[16,144,256]{2,1,0:T(8,128)(2,1)} %modal_axial_coefficients.5.rest_0_), calls=%async_computation.1 | async-start | bytes 2359296 | tf_op jit(solution)/shard_map/all_to_all | solution.py:509
  164.5 22.9 %collective-permute-start.18 = (bf16[4,272,256]{2,1,0:T(8,128)(2,1)}, bf16[4,272,256]{2,1,0:T(8,128)(2,1)}, u32[]{:S(2)}, u32[]{:S(2)}) collective-permute-start(bf16[4,272,256]{2,1,0:T(8,128)(2,1)} %get-tuple-element.51.__.rest_0_), channel_id=1, source_target_pairs={{0,1},{1,0},{2,3},{3,2},{4,5},{5,4},{6,7},{7,6},{8,9},{9,8},{10,11... | collective-permute-start | bytes 1671176 | tf_op jit(solution)/shard_map/ppermute | solution.py:538
  180.7 12.6 %collective-permute-start.17 = (bf16[2,272,256]{2,1,0:T(8,128)(2,1)}, bf16[2,272,256]{2,1,0:T(8,128)(2,1)}, u32[]{:S(2)}, u32[]{:S(2)}) collective-permute-start(bf16[2,272,256]{2,1,0:T(8,128)(2,1)} %get-tuple-element.53.rest_0_), channel_id=1, source_target_pairs={{0,1},{1,0},{2,3},{3,2},{4,5},{5,4},{6,7},{7,6},{8,9},{9,8},{10,11... | collective-permute-start | bytes 835592 | tf_op jit(solution)/shard_map/ppermute | solution.py:538
  186.3 12.9 %collective-permute-start.16 = (bf16[2,272,256]{2,1,0:T(8,128)(2,1)S(1)}, bf16[2,272,256]{2,1,0:T(8,128)(2,1)S(1)}, u32[]{:S(2)}, u32[]{:S(2)}) collective-permute-start(bf16[2,272,256]{2,1,0:T(8,128)(2,1)S(1)} %get-tuple-element.55.__), channel_id=1, source_target_pairs={{0,1},{1,0},{2,3},{3,2},{4,5},{5,4},{6,7},{7,6},{8,9},{9,8},{10,11... | collective-permute-start | bytes 835592 | tf_op jit(solution)/shard_map/ppermute | solution.py:538
  (6 other events, 16.4 us)
